TPU v7x, 32 devices: a whole 2x2x4 slice. The times are simulated.
32 devices in a mesh: row: 8 (over z, y), col: 4 (over x, core).
Axes of the slice: x: 2, y: 2, z: 4, core: 2. Of those that a mesh axis runs over, the one named last changes fastest.
Arguments:
- frames: bfloat16 [2, 16, 128, 1280], P(None, 'row', 'col'), may hold values from -6 to 6
- targets: bfloat16 [2, 2, 16, 128, 1280], P(None, None, 'row', 'col'), may hold values from -6 to 6
- regions: int32 [2, 4], replicated, may hold values from 0 to 128, as said below
- master: float32 [12017664], P(('row', 'col')), as said below
- first_moment: float32 [12017664], P(('row', 'col')), may hold values from -9.1552734e-05 to 9.1552734e-05
- second_moment: float32 [12017664], P(('row', 'col')), may hold values from 8.737883e-11 to 1.4147049e-09
Outputs:
- master_out: float32 [12017664], P(('row', 'col'))
- first_out: float32 [12017664], P(('row', 'col'))
- second_out: float32 [12017664], P(('row', 'col'))
- weights_out: bfloat16 [12017664], P(('row', 'col'))
- loss_sum: float32 [], replicated
- loss_weight: float32 [], replicated
- grad_norm: float32 [], replicated
Inputs may be any that keep to these rules, and one draw needn't show every extreme that they name: `regions`: rows stay within the grid; a row count is 8 or more, a column count 128 // 2 or more; one micro-batch covers the whole grid. `master`: entries from 12016640 on are padding.
All inputs are finite; a program needn't handle non-finite values.
Results may differ from a plain program's by a relative error of at most 0.03.
Values may be sent and summed in bfloat16 or wider, within the bound.
A program may use at most 320 MiB of HBM per device.

v0:
```python
import math

import jax
import jax.numpy as jnp
from jax import lax
from jax.sharding import PartitionSpec as P

D = 768
FF = 3072
NBLK = 8
BS = 96
PIN = 1280
LAYERS = 2
STEPS = 2
ADAM_STEP = 5


highest = lax.Precision.HIGHEST
NORM_EPS = 1e-05
BETA_ONE = 0.9
BETA_TWO = 0.95
ADAM_EPS = 1e-08
RATE = 0.03
DECAY = 0.05
CLIP = 0.2
LANES = 128


def block_shapes():
    return [
        (D,),
        (D,),
        (2, NBLK, BS, BS),
        (2, NBLK, BS),
        (2, NBLK, BS, BS),
        (2, NBLK, BS),
        (D,),
        (D,),
        (D, FF),
        (FF,),
        (FF, D),
        (D,),
    ]


def all_shapes():
    return [(PIN, D), (D,)] + block_shapes() * LAYERS + [(D,), (D,), (D, PIN), (PIN,)]


def unpack(flat_vec):
    pieces = []
    offset = 0
    for layout in all_shapes():
        length = math.prod(layout)
        pieces.append(flat_vec[offset : offset + length].reshape(layout))
        offset += length
    return pieces


def rounded(value):
    return lax.optimization_barrier(value.astype(jnp.bfloat16)).astype(jnp.float32)


def mult(form, left, right):
    return jnp.einsum(
        form,
        left.astype(jnp.bfloat16),
        right.astype(jnp.bfloat16),
        preferred_element_type=jnp.float32,
    )


def mult_exact(form, grad_value, other):
    upper = grad_value.astype(jnp.bfloat16)
    lower = (grad_value - upper.astype(jnp.float32)).astype(jnp.bfloat16)
    return mult(form, upper, other) + mult(form, lower, other)


def layer_norm(values, gain_vec, shift_vec):
    center = values - jnp.mean(values, axis=-1, keepdims=True)
    spread = jnp.mean(center * center, axis=-1, keepdims=True)
    return center * lax.rsqrt(spread + NORM_EPS) * gain_vec + shift_vec


def dft_tables(length, direction):
    positions = jnp.arange(length, dtype=jnp.int32)
    phases = (positions[:, None] * positions[None, :] % length).astype(jnp.float32) * (
        2.0 * math.pi / length
    )
    factor = 1.0 / math.sqrt(length)
    return (jnp.cos(phases) * factor, direction * jnp.sin(phases) * factor)


def apply_pair(tables, real_part, imag_part, form):

    def contract(table, values):
        return jnp.einsum(form, table, values, precision=highest)

    return (
        contract(tables[0], real_part) - contract(tables[1], imag_part),
        contract(tables[1], real_part) + contract(tables[0], imag_part),
    )


def spectral(real_part, imag_part, weight, bias_vec):
    blocks = (weight.shape[1], weight.shape[2])
    block_re = real_part.reshape(real_part.shape[:-1] + blocks)
    block_im = imag_part.reshape(imag_part.shape[:-1] + blocks)
    form = "...kb,kbc->...kc"
    out_re = (
        jnp.einsum(form, block_re, weight[0], precision=highest)
        - jnp.einsum(form, block_im, weight[1], precision=highest)
        + bias_vec[0]
    )
    out_im = (
        jnp.einsum(form, block_im, weight[0], precision=highest)
        + jnp.einsum(form, block_re, weight[1], precision=highest)
        + bias_vec[1]
    )
    return (out_re.reshape(real_part.shape), out_im.reshape(imag_part.shape))


def first_spectral(real_part, imag_part, weight, bias_vec):
    out_re, out_im = spectral(real_part, imag_part, weight, bias_vec)
    return (jax.nn.gelu(out_re, approximate=False), jax.nn.gelu(out_im, approximate=False))


def region_masks(regions, row_ids, col_ids, width):
    row_start = regions[:, 0, None, None]
    row_span = regions[:, 1, None, None]
    col_start = regions[:, 2, None, None]
    col_span = regions[:, 3, None, None]
    row_inside = (row_ids[None, :, None] >= row_start) & (
        row_ids[None, :, None] < row_start + row_span
    )
    col_inside = (col_ids[None, None, :] - col_start) % width < col_span
    return (row_inside & col_inside).astype(jnp.float32)


def latitude(row_ids, height):
    return jnp.cos(-1.3 + 1.3 * (row_ids.astype(jnp.float32) + 0.5) / height)


def linear_forward(values, weight16, bias_vec):
    return mult("brci,io->brco", values, weight16) + bias_vec


def linear_backward(grad_value, values, weight16):
    grad_values = mult_exact("brco,io->brci", grad_value, weight16)
    grad_weight = mult_exact("brco,brci->io", grad_value, values)
    return (grad_values, grad_weight, jnp.sum(grad_value, axis=(0, 1, 2)))


def spectrum(field, forward_w, forward_h):
    values = lax.all_to_all(field, "col", split_axis=3, concat_axis=2, tiled=True).astype(
        jnp.float32
    )
    real_part = jnp.einsum("kw,bnwc->bnkc", forward_w[0], values, precision=highest)
    imag_part = jnp.einsum("kw,bnwc->bnkc", forward_w[1], values, precision=highest)
    real_part, imag_part = apply_pair(
        forward_h,
        lax.all_to_all(
            real_part.astype(jnp.bfloat16), "row", split_axis=2, concat_axis=1, tiled=True
        ).astype(jnp.float32),
        lax.all_to_all(
            imag_part.astype(jnp.bfloat16), "row", split_axis=2, concat_axis=1, tiled=True
        ).astype(jnp.float32),
        "kh,bhwc->bkwc",
    )
    return (real_part.astype(jnp.bfloat16), imag_part.astype(jnp.bfloat16))


def grid(real_part, imag_part, inverse_w, inverse_h):
    back_re, back_im = apply_pair(
        inverse_h, real_part.astype(jnp.float32), imag_part.astype(jnp.float32), "kh,bhwc->bkwc"
    )
    values_re = lax.all_to_all(
        back_re.astype(jnp.bfloat16), "row", split_axis=1, concat_axis=2, tiled=True
    ).astype(jnp.float32)
    values_im = lax.all_to_all(
        back_im.astype(jnp.bfloat16), "row", split_axis=1, concat_axis=2, tiled=True
    ).astype(jnp.float32)
    result = jnp.einsum("kw,bnwc->bnkc", inverse_w[0], values_re, precision=highest) - jnp.einsum(
        "kw,bnwc->bnkc", inverse_w[1], values_im, precision=highest
    )
    columns_back = result.astype(jnp.bfloat16)
    return lax.all_to_all(columns_back, "col", split_axis=2, concat_axis=3, tiled=True)


def local_blocks(params):
    block_count = D // lax.axis_size("col") // BS
    first_block = lax.axis_index("col") * block_count
    chosen = [
        lax.dynamic_slice_in_dim(params[index_pos], first_block, block_count, 1)
        for index_pos in (2, 3, 4, 5)
    ]
    return (chosen, first_block)


def layer_forward(stream, params, params16, tables):
    gain_one, shift_one, _, _, _, _, gain_two, shift_two, _, bias_in, _, bias_out = params
    (local_w1, local_b1, local_w2, local_b2), _ = local_blocks(params)
    normed = layer_norm(stream, gain_one, shift_one).astype(jnp.bfloat16)
    wave_re, wave_im = spectrum(normed, tables[0], tables[1])
    hid_re, hid_im = first_spectral(
        wave_re.astype(jnp.float32), wave_im.astype(jnp.float32), local_w1, local_b1
    )
    hid_re, hid_im = (rounded(hid_re), rounded(hid_im))
    spec_re, spec_im = spectral(hid_re, hid_im, local_w2, local_b2)
    filtered = grid(
        spec_re.astype(jnp.bfloat16), spec_im.astype(jnp.bfloat16), tables[2], tables[3]
    )
    mixed = stream + filtered.astype(jnp.float32)
    normed_two = rounded(layer_norm(mixed, gain_two, shift_two))
    hidden = rounded(
        jax.nn.gelu(linear_forward(normed_two, params16[8], bias_in), approximate=False)
    )
    output = mixed + linear_forward(hidden, params16[10], bias_out)
    return (output, (stream, wave_re, wave_im, hid_re, hid_im, mixed, normed_two, hidden))


def place_blocks(local_grad, full_like, first_block):
    return lax.dynamic_update_slice_in_dim(jnp.zeros_like(full_like), local_grad, first_block, 1)


def layer_backward(grad_out, saved, params, params16, tables):
    stream, wave_re, wave_im, hid_re, hid_im, mixed, normed_two, hidden = saved
    (
        gain_one,
        shift_one,
        spec_w1,
        spec_b1,
        spec_w2,
        spec_b2,
        gain_two,
        shift_two,
        weight_in,
        bias_in,
        weight_out,
        bias_out,
    ) = params
    (local_w1, local_b1, local_w2, local_b2), first_block = local_blocks(params)
    grad_hidden, grad_wout, grad_bout = linear_backward(grad_out, hidden, params16[10])
    grad_mixed = grad_out
    before = linear_forward(normed_two, params16[8], bias_in)
    _, pullback = jax.vjp(lambda value: jax.nn.gelu(value, approximate=False), before)
    (grad_before,) = pullback(rounded(grad_hidden))
    grad_normed, grad_win, grad_bin = linear_backward(grad_before, normed_two, params16[8])
    _, pullback = jax.vjp(layer_norm, mixed, gain_two, shift_two)
    grad_extra, grad_gain2, grad_shift2 = pullback(rounded(grad_normed))
    grad_mixed = grad_mixed + grad_extra
    back_re, back_im = spectrum(grad_mixed.astype(jnp.bfloat16), tables[0], tables[1])
    _, pullback = jax.vjp(spectral, hid_re, hid_im, local_w2, local_b2)
    grad_hre, grad_him, grad_lw2, grad_lb2 = pullback(
        (back_re.astype(jnp.float32), back_im.astype(jnp.float32))
    )
    _, pullback = jax.vjp(
        first_spectral, wave_re.astype(jnp.float32), wave_im.astype(jnp.float32), local_w1, local_b1
    )
    grad_wre, grad_wim, grad_lw1, grad_lb1 = pullback((rounded(grad_hre), rounded(grad_him)))
    grad_first = grid(
        grad_wre.astype(jnp.bfloat16), grad_wim.astype(jnp.bfloat16), tables[2], tables[3]
    )
    _, pullback = jax.vjp(layer_norm, stream, gain_one, shift_one)
    grad_stream, grad_gain1, grad_shift1 = pullback(grad_first.astype(jnp.float32))
    layer_grads = [
        grad_gain1,
        grad_shift1,
        place_blocks(grad_lw1, spec_w1, first_block),
        place_blocks(grad_lb1, spec_b1, first_block),
        place_blocks(grad_lw2, spec_w2, first_block),
        place_blocks(grad_lb2, spec_b2, first_block),
        grad_gain2,
        grad_shift2,
        grad_win,
        grad_bin,
        grad_wout,
        grad_bout,
    ]
    return (grad_stream + grad_mixed, layer_grads)


def add_into(gradients, start, values):
    middle = [left + right for left, right in zip(gradients[start : start + len(values)], values)]
    return gradients[:start] + middle + gradients[start + len(values) :]


def local(frames, targets, regions, master, first_moment, second_moment):
    row_devices = lax.axis_size("row")
    col_devices = lax.axis_size("col")
    local_rows = frames.shape[1]
    local_cols = frames.shape[2]
    height = local_rows * row_devices
    width = local_cols * col_devices
    weights = lax.all_gather(master.astype(jnp.bfloat16), ("row", "col"), axis=0, tiled=True)
    pieces16 = unpack(weights)
    pieces = unpack(weights.astype(jnp.float32))
    tail_params = pieces[2 + 12 * LAYERS :]
    tail16 = pieces16[2 + 12 * LAYERS :]
    tables = (
        dft_tables(width, -1.0),
        dft_tables(height, -1.0),
        dft_tables(width, 1.0),
        dft_tables(height, 1.0),
    )
    row_ids = lax.axis_index("row") * local_rows + jnp.arange(local_rows, dtype=jnp.int32)
    col_ids = lax.axis_index("col") * local_cols + jnp.arange(local_cols, dtype=jnp.int32)
    cell_masks = region_masks(regions, row_ids, col_ids, width)
    weighted = latitude(row_ids, height)[None, :, None] * cell_masks
    every_row = jnp.arange(height, dtype=jnp.int32)
    every_col = jnp.arange(width, dtype=jnp.int32)
    total_weight = (
        jnp.sum(
            latitude(every_row, height)[None, :, None]
            * region_masks(regions, every_row, every_col, width)
        )
        * STEPS
    )
    inputs = frames.astype(jnp.float32) * cell_masks[..., None]
    loss_sum = jnp.zeros((), jnp.float32)
    history = []
    for roll_step in range(STEPS):
        stream = linear_forward(inputs, pieces16[0], pieces[1])
        saved_layers = []
        for layer_idx in range(LAYERS):
            span = slice(2 + 12 * layer_idx, 14 + 12 * layer_idx)
            stream, saved = layer_forward(stream, pieces[span], pieces16[span], tables)
            saved_layers.append(saved)
        normed = rounded(layer_norm(stream, tail_params[0], tail_params[1]))
        predicted = linear_forward(normed, tail16[2], tail_params[3])
        errors = predicted - targets[:, roll_step].astype(jnp.float32)
        loss_sum = loss_sum + jnp.sum(weighted * jnp.sum(errors * errors, axis=-1))
        history.append((inputs, saved_layers, stream, normed, errors))
        inputs = rounded(predicted * cell_masks[..., None])
    loss_all = lax.psum(loss_sum, ("row", "col"))
    gradients = [jnp.zeros_like(piece) for piece in pieces]
    carried = jnp.zeros_like(inputs)
    for roll_step in reversed(range(STEPS)):
        inputs, saved_layers, stream, normed, errors = history[roll_step]
        grad_pred = 2.0 * weighted[..., None] * errors / total_weight + carried
        grad_normed, grad_head, grad_hbias = linear_backward(grad_pred, normed, tail16[2])
        _, pullback = jax.vjp(layer_norm, stream, tail_params[0], tail_params[1])
        grad_stream, grad_gain3, grad_shift3 = pullback(rounded(grad_normed))
        gradients = add_into(
            gradients, 2 + 12 * LAYERS, [grad_gain3, grad_shift3, grad_head, grad_hbias]
        )
        for layer_idx in reversed(range(LAYERS)):
            span = slice(2 + 12 * layer_idx, 14 + 12 * layer_idx)
            grad_stream, layer_grads = layer_backward(
                grad_stream, saved_layers[layer_idx], pieces[span], pieces16[span], tables
            )
            gradients = add_into(gradients, 2 + 12 * layer_idx, layer_grads)
        grad_inputs, grad_embed, grad_ebias = linear_backward(grad_stream, inputs, pieces16[0])
        gradients = add_into(gradients, 0, [grad_embed, grad_ebias])
        carried = cell_masks[..., None] * rounded(grad_inputs)
    flat_grad = jnp.concatenate([piece.ravel() for piece in gradients])
    padding = master.shape[0] * row_devices * col_devices - flat_grad.shape[0]
    flat_grad = jnp.concatenate([flat_grad, jnp.zeros((padding,), jnp.float32)])
    grad_table = flat_grad.reshape(-1, LANES)
    reduced = lax.psum_scatter(grad_table, ("row", "col"), scatter_dimension=0, tiled=True).reshape(
        -1
    )
    squares = jnp.sum(reduced * reduced)
    square_all = lax.psum(squares, ("row", "col"))
    grad_norm = jnp.sqrt(square_all)
    clipped = reduced * (CLIP / jnp.maximum(grad_norm, CLIP))
    first_out = BETA_ONE * first_moment + (1.0 - BETA_ONE) * clipped
    second_out = BETA_TWO * second_moment + (1.0 - BETA_TWO) * clipped * clipped
    corrected_one = first_out / (1.0 - BETA_ONE**ADAM_STEP)
    corrected_two = second_out / (1.0 - BETA_TWO**ADAM_STEP)
    master_out = master - RATE * (
        corrected_one / (jnp.sqrt(corrected_two) + ADAM_EPS) + DECAY * master
    )
    return (
        master_out,
        first_out,
        second_out,
        master_out.astype(jnp.bfloat16),
        loss_all,
        total_weight,
        grad_norm,
    )


def solution(mesh):
    in_specs = (
        P(None, "row", "col", None),
        P(None, None, "row", "col", None),
        P(),
        P(("row", "col")),
        P(("row", "col")),
        P(("row", "col")),
    )
    out_specs = (
        P(("row", "col")),
        P(("row", "col")),
        P(("row", "col")),
        P(("row", "col")),
        P(),
        P(),
        P(),
    )
    return jax.shard_map(local, mesh=mesh, in_specs=in_specs, out_specs=out_specs, check_vma=False)
```

profile of v0, /device:TPU:0, one launch (start us, length us, event | category | flops | bytes accessed | tf_op | source)
XLA Modules:
  0.0 2854.9 jit_solution(7874523617973032177)
XLA Ops:
  8.7 9.3 reshape.1188
  19.6 265.9 %all-gather.3.cloned.1.call-done = bf16[32,1,375552]{2,1,0:T(2,128)(2,1)} async-done(((bf16[1,1,375552]{2,1,0:T(2,128)(2,1)}), bf16[32,1,375552]{2,1,0:T(2,128)(2,1)}) %all-gather.3.cloned.1.call-update) | async-done | bytes 24035344 | tf_op jit(solution)/shard_map/all_gather | solution.py:295
  285.5 142.6 %reduce.37 = bf16[32,375552]{1,0:T(8,128)(2,1)} reduce(bf16[32,1,375552]{2,1,0:T(2,128)(2,1)} %all-gather.3.cloned.1.call-done, bf16[]{:T(256)} %constant.367), dimensions={1}, to_apply=%all-gather.reduce_sub_computation | reduce | bytes 48070656 | tf_op jit(solution)/shard_map/all_gather | solution.py:295
  428.1 57.0 %reshape.1189 = bf16[12017664]{0:T(1024)(128)(2,1)} reshape(bf16[32,375552]{1,0:T(8,128)(2,1)} %reduce.37) | data formatting | bytes 48070656
  585.7 6.8 all-to-all-done.3
  596.1 14.4 fusion.1452
  610.5 8.2 reshape.1201
  618.7 9.3 reshape.1202
  666.5 6.0 all-to-all-start.7
  740.0 6.8 all-to-all-done.9
  751.0 7.9 all-to-all-done.10
  764.5 8.2 reshape.1207
  772.7 9.2 reshape.1208
  805.3 8.4 all_to_all.792
  823.7 7.5 all-to-all-done.13
  837.4 6.2 all-to-all-done.14
  891.5 6.9 all-to-all-done.15
  902.5 7.9 all-to-all-done.16
  1037.0 6.6 all-to-all-done.21
  1048.7 6.5 all-to-all-done.22
  1060.3 5.9 all-to-all-done.23
  1228.9 5.9 all-to-all-start.28
  1237.2 5.9 all-to-all-done.28
  1307.4 6.3 fusion.999
  1329.8 6.1 all-to-all-done.31
  1424.6 5.9 all-to-all-start.34
  1432.1 6.7 all-to-all-done.34
  1508.4 14.3 fusion.3
  1522.7 14.7 fusion.1
  1542.8 9.4 copy.1900
  1552.2 10.7 reshape.1167
  1577.2 7.6 all-to-all-done.37
  1589.9 7.6 all-to-all-done.38
  1657.2 6.9 all-to-all-done.40
  1711.8 10.6 fusion.6
  1722.4 14.1 fusion.4
  1742.3 10.8 reshape.1161
  1762.4 8.1 all-to-all-done.43
  1775.6 7.5 all-to-all-done.44
  1836.2 6.2 all-to-all-done.46
  1888.8 80.5 %dynamic-update-slice.18 = f32[12017664]{0:T(1024)} dynamic-update-slice(f32[12017664]{0:T(1024)} %constant_dynamic-update-slice_fusion.21, f32[2359296]{0:T(1024)} %bitcast.1693, s32[]{} %constant.378) | dynamic-update-slice | bytes 18874372
  1970.7 80.5 %dynamic-update-slice.20 = f32[12017664]{0:T(1024)} dynamic-update-slice(f32[12017664]{0:T(1024)} %add_dynamic-update-slice_fusion.9, f32[2359296]{0:T(1024)} %reshape.1161, s32[]{} %constant.380) | dynamic-update-slice | bytes 18874372
  2063.2 80.3 %dynamic-update-slice.30 = f32[12017664]{0:T(1024)} dynamic-update-slice(f32[12017664]{0:T(1024)} %constant_dynamic-update-slice_fusion.12, f32[2359296]{0:T(1024)} %bitcast.1692, s32[]{} %constant.390) | dynamic-update-slice | bytes 18874372
  2144.8 80.6 %dynamic-update-slice.32 = f32[12017664]{0:T(1024)} dynamic-update-slice(f32[12017664]{0:T(1024)} %add_dynamic-update-slice_fusion.8, f32[2359296]{0:T(1024)} %reshape.1167, s32[]{} %constant.392) | dynamic-update-slice | bytes 18874372
  2229.4 34.3 %dynamic-update-slice.36 = f32[12017664]{0:T(1024)} dynamic-update-slice(f32[12017664]{0:T(1024)} %constant_dynamic-update-slice_fusion.9, f32[983040]{0:T(1024)} %reshape.1168, s32[]{} %constant.396) | dynamic-update-slice | bytes 7864324
  2265.6 499.3 %fusion = f32[2944,128]{1,0:T(8,128)S(1)} fusion(f32[93888,128]{1,0:T(8,128)} %bitcast.1691), kind=kCustom, calls=%all-reduce-scatter | all-reduce-scatter fusion | flops 12058625 | bytes 49577984
  2764.9 24.0 collective-permute-start
  2793.6 45.9 %all-reduce.50 = (f32[]{:T(128)}, f32[]{:T(128)}) all-reduce(f32[]{:T(128)} %multiply_reduce_fusion, f32[]{:T(128)S(6)} %add.1422), channel_id=1, replica_groups=mesh['row'=8,'col'=4] {'row','col'}, use_global_device_ids=true, to_apply=%region_95.96 | all-reduce | flops 2 | bytes 16 | tf_op jit(solution)/shard_map/psum | solution.py:364
  (1551 shorter events, 1131.5 us)
Async XLA Ops:
  7.2 278.3 %all-gather.3.cloned.1.call-start = ((), (), s32[]{:S(2)}) async-start(), calls=%async_computation.48 | async-start | bytes 49572864 | tf_op jit(solution)/shard_map/all_gather | solution.py:295
  500.8 8.7 all-to-all-start
  514.5 12.4 all-to-all-start.1
  527.0 12.4 all-to-all-start.2
  580.4 12.1 all-to-all-start.3
  592.6 36.0 %all-to-all-start.4 = ((bf16[2,16,16,192]{3,2,0,1:T(8,128)(2,1)}), bf16[2,16,16,192]{3,2,0,1:T(8,128)(2,1)S(1)}, u32[]{:S(2)}, u32[]{:S(2)}) async-start(bf16[2,16,16,192]{3,2,0,1:T(8,128)(2,1)} %copy.1446), calls=%async_computation.4 | async-start | bytes 524288 | tf_op jit(solution)/shard_map/all_to_all | solution.py:180
  630.2 9.4 all-to-all-start.5
  652.4 9.1 all-to-all-start.6
  666.5 14.7 all-to-all-start.7
  681.2 12.4 all-to-all-start.8
  734.7 12.1 all-to-all-start.9
  746.8 12.0 all-to-all-start.10
  760.4 26.3 all-to-all-start.11
  818.7 12.5 all-to-all-start.13
  831.2 12.4 all-to-all-start.14
  886.2 12.1 all-to-all-start.15
  898.4 12.0 all-to-all-start.16
  911.9 9.4 all-to-all-start.17
  938.3 8.7 all-to-all-start.18
  952.0 12.4 all-to-all-start.19
  964.3 12.8 all-to-all-start.20
  1031.4 12.3 all-to-all-start.21
  1043.7 11.6 all-to-all-start.22
  1056.8 9.4 all-to-all-start.23
  1132.0 12.4 all-to-all-start.25
  1144.4 12.7 all-to-all-start.26
  1216.0 13.0 all-to-all-start.27
  1228.9 14.1 all-to-all-start.28
  1248.9 10.1 all-to-all-start.29
  1304.0 11.3 all-to-all-start.30
  1322.0 13.9 all-to-all-start.31
  1335.9 13.0 all-to-all-start.32
  1410.8 13.7 all-to-all-start.33
  1424.6 14.2 all-to-all-start.34
  1442.9 10.1 all-to-all-start.35
  1504.3 63.3 %all-to-all-start.36 = ((bf16[4,2,12288]{2,1,0:T(2,128)(2,1)}), bf16[4,2,12288]{2,1,0:T(2,128)(2,1)}, u32[]{:S(2)}, u32[]{:S(2)}) async-start(bf16[4,2,12288]{2,1,0:T(2,128)(2,1)} %reshape.1305), calls=%async_computation.36 | async-start | bytes 393216 | tf_op jit(solution)/shard_map/all_to_all | solution.py:155
  1571.6 13.2 all-to-all-start.37
  1584.8 12.7 all-to-all-start.38
  1639.7 12.4 all-to-all-start.39
  1652.1 12.0 all-to-all-start.40
  1665.6 9.4 all-to-all-start.41
  1707.6 45.6 %all-to-all-start.42 = ((bf16[4,2,12288]{2,1,0:T(2,128)(2,1)}), bf16[4,2,12288]{2,1,0:T(2,128)(2,1)}, u32[]{:S(2)}, u32[]{:S(2)}) async-start(bf16[4,2,12288]{2,1,0:T(2,128)(2,1)} %reshape.1307), calls=%async_computation.42 | async-start | bytes 393216 | tf_op jit(solution)/shard_map/all_to_all | solution.py:155
  1757.3 13.2 all-to-all-start.43
  1770.4 12.7 all-to-all-start.44
  1818.2 12.2 all-to-all-start.45
  1830.3 12.1 all-to-all-start.46
  1844.0 9.5 all-to-all-start.47
  2764.9 26.0 collective-permute-start
  (344 other events, 10764.4 us)
Sparse Core Ops, SparseCore 0:
  18.2 267.2 all-gather.2
where the time goes:
time: 2900 us; the launch traced here: 2850 us
  local copies, waits for them, and re-layouts  879 us (30%)
  blocking collectives  554 us (19%)
  waiting for transfers between devices  479 us (17%)
  matrix products  434 us (15%)
  other arithmetic  280 us (10%)
  starting transfers between devices  205 us (7%)
    unnamed x1, blocking collectives  499 us
    unnamed x724, local copies, waits for them, and re-layouts  495 us
    all_gather x1, waiting for transfers between devices, local(): lax.all_gather(master.astype(jnp.bfloat16), ('row', 'col'), axis=0, tiled...  266 us
    dot_general x58, matrix products, mult(): jnp.einsum(form, left.astype(jnp.bfloat16), right.astype(jnp.bfloat16), p...  195 us
    all_gather x1, other arithmetic, local(): lax.all_gather(master.astype(jnp.bfloat16), ('row', 'col'), axis=0, tiled...  143 us
    dot_general x64, matrix products, contract(): return jnp.einsum(form, table, values, precision=highest)  78.3 us
  transfers between devices with their start and end apart: 49, of which 41 were waited for; matrix products, arithmetic and copies ran while one was open for 10% of the time, Pallas kernels for 0%

commit v1 on v0

--- a/solution.py
+++ b/solution.py
@@ -1,9 +1,13 @@
+import functools
 import math
 
 import jax
 import jax.numpy as jnp
+import numpy as np
 from jax import lax
 from jax.sharding import PartitionSpec as P
+from jax.experimental import pallas as pl
+from jax.experimental.pallas import tpu as pltpu
 
 D = 768
 FF = 3072
@@ -283,6 +287,1281 @@
 def add_into(gradients, start, values):
     middle = [left + right for left, right in zip(gradients[start : start + len(values)], values)]
     return gradients[:start] + middle + gradients[start + len(values) :]
+
+
+MESH = pl.DeviceIdType.MESH
+CH = 2944
+OWN = 2934
+CHR = 2960
+GROWS = 93904
+
+
+CHIPS = 16
+UNIT = 64
+PADC = 128
+f32 = jnp.float32
+bf16 = jnp.bfloat16
+
+
+def remote(src, dst, send_sem, recv_sem, device):
+    return pltpu.make_async_remote_copy(
+        src_ref=src,
+        dst_ref=dst,
+        send_sem=send_sem,
+        recv_sem=recv_sem,
+        device_id=device,
+        device_id_type=MESH,
+    )
+
+
+def chip_device(chip, core):
+    return chip // 2, (chip % 2) * 2 + core
+
+
+def place():
+    row = lax.axis_index("row")
+    col = lax.axis_index("col")
+    core = col % 2
+    return row, row * 2 + col // 2, core, (row, col + 1 - 2 * core)
+
+
+def greet_chips(me, core, sibling):
+    barrier = pltpu.get_barrier_semaphore()
+
+    def one(k, carry):
+        pl.semaphore_signal(
+            barrier,
+            inc=1,
+            device_id=chip_device(lax.rem(me + k, CHIPS), core),
+            device_id_type=MESH,
+        )
+        return carry
+
+    lax.fori_loop(1, CHIPS, one, 0)
+    pl.semaphore_signal(barrier, inc=1, device_id=sibling, device_id_type=MESH)
+    return barrier
+
+
+def split_units(values, units):
+    blank = jnp.zeros((UNIT, PADC - BS), f32)
+    for part in range(2):
+        for block in range(NBLK):
+            piece = values[part * UNIT : (part + 1) * UNIT, block * BS : (block + 1) * BS]
+            units[part * NBLK + block] = jnp.concatenate([piece, blank], axis=1).astype(bf16)
+
+
+def join_units(units, joined):
+    for part in range(2):
+        for block in range(NBLK):
+            joined[part * UNIT : (part + 1) * UNIT, block * BS : (block + 1) * BS] = units[
+                part * NBLK + block, :, 0:BS
+            ].astype(f32)
+
+
+def normalize(values):
+    center = values - jnp.mean(values, axis=-1, keepdims=True)
+    spread = jnp.mean(center * center, axis=-1, keepdims=True)
+    scale = lax.rsqrt(spread + NORM_EPS)
+    return center * scale, scale
+
+
+def gelu_of(value):
+    return 0.5 * value * (1.0 + lax.erf(value * math.sqrt(0.5)))
+
+
+def gelu_slope(value):
+    bell = jnp.exp(-0.5 * value * value) * (1.0 / math.sqrt(2.0 * math.pi))
+    return 0.5 * (1.0 + lax.erf(value * math.sqrt(0.5))) + value * bell
+
+
+def dot(left, right):
+    return jnp.dot(left, right, preferred_element_type=f32)
+
+
+def dot_rows(left, right):
+    return lax.dot_general(left, right, (((0,), (0,)), ((), ())), preferred_element_type=f32)
+
+
+def dot_cols(left, right):
+    return lax.dot_general(left, right, (((1,), (1,)), ((), ())), preferred_element_type=f32)
+
+
+def spread_units(me, core, sibling, units, mine, others, sems):
+    send_a, recv_a, send_f, recv_f, local_sem = sems
+
+    def out(k):
+        chip = lax.rem(me + k, CHIPS)
+        return remote(
+            units.at[chip], mine.at[me], send_a.at[k], recv_a.at[k], chip_device(chip, core)
+        )
+
+    def handed(k):
+        chip = lax.rem(me + CHIPS - k, CHIPS)
+        return remote(mine.at[chip], others.at[chip], send_f.at[k], recv_f.at[k], sibling)
+
+    own = pltpu.make_async_copy(units.at[me], mine.at[me], local_sem)
+    own.start()
+
+    def begin(k, carry):
+        out(k).start()
+        return carry
+
+    lax.fori_loop(1, CHIPS, begin, 0)
+    own.wait()
+    handed(0).start()
+
+    def hand(k, carry):
+        out(k).wait_recv()
+        handed(k).start()
+        return carry
+
+    lax.fori_loop(1, CHIPS, hand, 0)
+
+    def arrive(k, carry):
+        handed(k).wait_recv()
+        return carry
+
+    lax.fori_loop(0, CHIPS, arrive, 0)
+
+    def finish():
+        def sent(k, carry):
+            out(k).wait_send()
+            return carry
+
+        lax.fori_loop(1, CHIPS, sent, 0)
+
+        def sent_on(k, carry):
+            handed(k).wait_send()
+            return carry
+
+        lax.fori_loop(0, CHIPS, sent_on, 0)
+
+    return finish
+
+
+def to_spectrum(mine, others, column_table, row_table, waves):
+    for h in range(16):
+        pair, part = h // 2, pl.ds(32 * (h % 2), 32)
+        cells = jnp.concatenate(
+            [
+                mine[2 * pair, part],
+                mine[2 * pair + 1, part],
+                others[2 * pair, part],
+                others[2 * pair + 1, part],
+            ],
+            axis=0,
+        )
+        wave = dot(column_table[...], cells).astype(bf16)
+        for g in range(4):
+            rows = pl.ds(16 * h, 16)
+            waves[g, rows, 0:PADC] = wave[16 * g : 16 * g + 16]
+            waves[g, rows, PADC : 2 * PADC] = wave[64 + 16 * g : 80 + 16 * g]
+    results = []
+    for g in range(4):
+        both = dot(row_table[...], waves[g])
+        real = both[:256, :PADC] + both[256:, PADC:]
+        imag = both[:256, PADC:] - both[256:, :PADC]
+        results.append(jnp.concatenate([real, imag], axis=1).astype(bf16))
+    return results
+
+
+def from_spectrum(g, spec, row_table, back):
+    both = dot(row_table[...], spec)
+    real = (both[:256, :PADC] - both[256:, PADC:]).astype(bf16)
+    imag = (both[:256, PADC:] + both[256:, :PADC]).astype(bf16)
+    for h in range(16):
+        back[h, 16 * g : 16 * g + 16] = real[16 * h : 16 * h + 16]
+        back[h, 64 + 16 * g : 80 + 16 * g] = imag[16 * h : 16 * h + 16]
+
+
+def gather_units(row, me, core, sibling, back, inverse_table, bufs, sems):
+    own_sum, to_sib, from_sib, ready, landed = bufs
+    send_s, recv_s, send_b, recv_b, local_sem = sems
+
+    def swap(pair):
+        rows = pl.ds(2 * pair, 2)
+        return remote(
+            to_sib.at[rows], from_sib.at[rows], send_s.at[pair], recv_s.at[pair], sibling
+        )
+
+    def partial(j, carry):
+        pair = lax.rem(row + 1 + j, 8)
+        for half in range(2):
+            sums = dot(inverse_table[...], back[2 * pair + half])
+            part = pl.ds(32 * half, 32)
+            for x in range(2):
+                own_sum[2 * pair + x, part] = sums[32 * x : 32 * x + 32]
+                to_sib[2 * pair + x, part] = sums[64 + 32 * x : 96 + 32 * x].astype(bf16)
+        swap(pair).start()
+        return carry
+
+    lax.fori_loop(0, 8, partial, 0)
+
+    def home(chip, k):
+        return remote(
+            ready.at[chip], landed.at[me], send_b.at[k], recv_b.at[k], chip_device(chip, core)
+        )
+
+    own = pltpu.make_async_copy(ready.at[me], landed.at[me], local_sem)
+
+    def total(j, carry):
+        pair = lax.rem(row + 1 + j, 8)
+        swap(pair).wait_recv()
+        rows = pl.ds(2 * pair, 2)
+        ready[rows] = (own_sum[rows] + from_sib[rows].astype(f32)).astype(bf16)
+        for x in range(2):
+            chip = 2 * pair + x
+            k = lax.rem(chip - me + CHIPS, CHIPS)
+
+            @pl.when(k != 0)
+            def _():
+                home(chip, k).start()
+
+        return carry
+
+    lax.fori_loop(0, 8, total, 0)
+    own.start()
+
+    def landed_all(k, carry):
+        home(lax.rem(me + k, CHIPS), k).wait_recv()
+        return carry
+
+    lax.fori_loop(1, CHIPS, landed_all, 0)
+    own.wait()
+
+    def finish():
+        def sent(k, carry):
+            home(lax.rem(me + k, CHIPS), k).wait_send()
+            return carry
+
+        lax.fori_loop(1, CHIPS, sent, 0)
+
+        def swapped(pair, carry):
+            swap(pair).wait_send()
+            return carry
+
+        lax.fori_loop(0, 8, swapped, 0)
+
+    return finish
+
+
+def filter_forward_kernel(
+    stream,
+    gain,
+    shift,
+    column_table,
+    inverse_table,
+    row_table,
+    w1,
+    b1,
+    w2,
+    b2,
+    mixed,
+    saved,
+    units,
+    mine,
+    others,
+    waves,
+    back,
+    own_sum,
+    to_sib,
+    from_sib,
+    ready,
+    landed,
+    joined,
+    *sems,
+):
+    row, me, core, sibling = place()
+    barrier = greet_chips(me, core, sibling)
+    normed, _ = normalize(stream[...])
+    split_units(normed * gain[...] + shift[...], units)
+    pl.semaphore_wait(barrier, CHIPS)
+    finish_one = spread_units(me, core, sibling, units, mine, others, sems[:5])
+    groups = to_spectrum(mine, others, column_table, row_table, waves)
+    for g in range(4):
+        saved[g] = groups[g]
+        hidden = gelu_of(dot(groups[g], w1[...]) + b1[...]).astype(bf16)
+        spec = (dot(hidden, w2[...]) + b2[...]).astype(bf16)
+        from_spectrum(g, spec, row_table, back)
+    finish_two = gather_units(
+        row, me, core, sibling, back, inverse_table,
+        (own_sum, to_sib, from_sib, ready, landed), sems[5:],
+    )
+    join_units(landed, joined)
+    mixed[...] = stream[...] + joined[...]
+    finish_one()
+    finish_two()
+
+
+def filter_backward_kernel(
+    grad,
+    stream,
+    gain,
+    saved,
+    column_table,
+    inverse_table,
+    row_table,
+    w1,
+    b1,
+    w2,
+    grad_out,
+    grad_norm,
+    grad_w1,
+    grad_w2,
+    grad_b,
+    units,
+    mine,
+    others,
+    waves,
+    back,
+    own_sum,
+    to_sib,
+    from_sib,
+    ready,
+    landed,
+    joined,
+    *sems,
+):
+    row, me, core, sibling = place()
+    barrier = greet_chips(me, core, sibling)
+    split_units(grad[...], units)
+    pl.semaphore_wait(barrier, CHIPS)
+    finish_one = spread_units(me, core, sibling, units, mine, others, sems[:5])
+    groups = to_spectrum(mine, others, column_table, row_table, waves)
+    grad_w1[...] = jnp.zeros_like(grad_w1)
+    grad_w2[...] = jnp.zeros_like(grad_w2)
+    grad_b[...] = jnp.zeros_like(grad_b)
+    for g in range(4):
+        before = dot(saved[g], w1[...]) + b1[...]
+        hidden = gelu_of(before).astype(bf16)
+        grad_hidden = dot_cols(groups[g], w2[...]).astype(bf16).astype(f32)
+        grad_before = grad_hidden * gelu_slope(before)
+        grad_before16 = grad_before.astype(bf16)
+        grad_w2[...] += dot_rows(hidden, groups[g])
+        grad_w1[...] += dot_rows(saved[g], grad_before16)
+        grad_b[0:1] += jnp.sum(grad_before, axis=0, keepdims=True)
+        grad_b[1:2] += jnp.sum(groups[g].astype(f32), axis=0, keepdims=True)
+        from_spectrum(g, dot_cols(grad_before16, w1[...]).astype(bf16), row_table, back)
+    finish_two = gather_units(
+        row, me, core, sibling, back, inverse_table,
+        (own_sum, to_sib, from_sib, ready, landed), sems[5:],
+    )
+    join_units(landed, joined)
+    values = joined[...]
+    normed, scale = normalize(stream[...])
+    grad_norm[0:1] = jnp.sum(values * normed, axis=0, keepdims=True)
+    grad_norm[1:2] = jnp.sum(values, axis=0, keepdims=True)
+    grad_norm[2:8] = jnp.zeros((6, D), f32)
+    inner = values * gain[...]
+    along = jnp.mean(inner * normed, axis=-1, keepdims=True)
+    flat = jnp.mean(inner, axis=-1, keepdims=True)
+    grad_out[...] = grad[...] + scale * (inner - flat - normed * along)
+    finish_one()
+    finish_two()
+
+
+def filter_scratch():
+    vm = pltpu.VMEM
+    dma = pltpu.SemaphoreType.DMA
+    block = (CHIPS, UNIT, PADC)
+    return [
+        vm(block, bf16),
+        vm(block, bf16),
+        vm(block, bf16),
+        vm((4, 256, 256), bf16),
+        vm((16, 128, PADC), bf16),
+        vm(block, f32),
+        vm(block, bf16),
+        vm(block, bf16),
+        vm(block, bf16),
+        vm(block, bf16),
+        vm((2 * UNIT, D), f32),
+        dma((CHIPS,)),
+        dma((CHIPS,)),
+        dma((CHIPS,)),
+        dma((CHIPS,)),
+        dma,
+        dma((8,)),
+        dma((8,)),
+        dma((CHIPS,)),
+        dma((CHIPS,)),
+        dma,
+    ]
+
+
+def filter_call(kernel, outs, collective_id, name, *args):
+    spec = pl.BlockSpec(memory_space=pltpu.VMEM)
+    return pl.pallas_call(
+        kernel,
+        out_shape=outs,
+        in_specs=[spec] * len(args),
+        out_specs=[spec] * len(outs),
+        scratch_shapes=filter_scratch(),
+        compiler_params=pltpu.CompilerParams(
+            collective_id=collective_id, has_side_effects=True, vmem_limit_bytes=48 << 20
+        ),
+        name=name,
+    )(*args)
+
+
+def filter_forward(stream, gain, shift, tables, weights):
+    column, inverse, rows = tables
+    w1, b1, w2, b2 = weights
+    shape = jax.ShapeDtypeStruct
+    return filter_call(
+        filter_forward_kernel,
+        [shape((2 * UNIT, D), f32), shape((4, 256, 256), bf16)],
+        2,
+        "filter_forward",
+        stream, gain, shift, column, inverse, rows, w1, b1, w2, b2,
+    )
+
+
+def filter_backward(grad, stream, gain, saved, tables, weights):
+    column, inverse, rows = tables
+    w1, b1, w2, _ = weights
+    shape = jax.ShapeDtypeStruct
+    return filter_call(
+        filter_backward_kernel,
+        [
+            shape((2 * UNIT, D), f32),
+            shape((8, D), f32),
+            shape((256, 256), f32),
+            shape((256, 256), f32),
+            shape((8, 256), f32),
+        ],
+        3,
+        "filter_backward",
+        grad, stream, gain, saved, column, inverse, rows, w1, b1, w2,
+    )
+
+
+def transform_tables(core):
+    width, height = 128, 16
+    order = []
+    for side in range(2):
+        cols = [[32 * (2 * x + (c if side == 0 else 1 - c)) + i for x in range(2) for i in range(32)] for c in range(2)]
+        order.append(cols)
+    column, inverse = [], []
+    for c in range(2):
+        cells = np.array(order[0][c] + order[1][c])
+        waves = 64 * c + np.arange(64)
+        angle = 2.0 * np.pi * (np.outer(waves, cells) % width) / width
+        cos, sin = np.cos(angle) / np.sqrt(width), np.sin(angle) / np.sqrt(width)
+        column.append(np.concatenate([cos, -sin], axis=0))
+        inverse.append(np.concatenate([cos, -sin], axis=0).T)
+    steps = np.arange(height)
+    angle = 2.0 * np.pi * (np.outer(steps, steps) % height) / height
+    eye = np.eye(16)
+    rows = np.concatenate(
+        [np.kron(np.cos(angle), eye), np.kron(np.sin(angle), eye)], axis=0
+    ) / np.sqrt(height)
+    pick = lambda both: lax.dynamic_index_in_dim(jnp.asarray(np.stack(both), bf16), core, 0, False)
+    return pick(column), pick(inverse), jnp.asarray(rows, bf16)
+
+
+def spread_weight(re, im):
+    def at(block, top, left):
+        return jnp.pad(block, ((top, PADC - BS), (left, PADC - BS)))
+
+    pad = lambda m: jnp.pad(m, ((0, PADC - BS), (0, PADC - BS)))
+    re, im = pad(re), pad(im)
+    return jnp.concatenate(
+        [jnp.concatenate([re, im], axis=1), jnp.concatenate([-im, re], axis=1)], axis=0
+    )
+
+
+def spread_bias(bias):
+    return jnp.pad(bias, ((0, 0), (0, PADC - BS))).reshape(1, 2 * PADC)
+
+
+def fold_weight(grad):
+    a, b = grad[:BS, :BS], grad[PADC : PADC + BS, PADC : PADC + BS]
+    c, d = grad[:BS, PADC : PADC + BS], grad[PADC : PADC + BS, :BS]
+    return jnp.stack([a + b, c - d])
+
+
+def fold_bias(grad):
+    return jnp.stack([grad[:BS], grad[PADC : PADC + BS]])
+
+
+RING = 8
+GATHER_CUTS = (0, 640, 1280, 2112, 2944)
+SUM_CUTS = (0, 640, 1280, 2128, 2960)
+
+
+def ring_place(row):
+    return jnp.where(row % 2 == 0, row // 2, 7 - row // 2)
+
+
+def ring_row(spot):
+    return jnp.where(spot < 4, 2 * spot, 2 * (7 - spot) + 1)
+
+
+def gather_kernel(shard, flat, ring_s, ring_r, x_s, x_r, sib_s, sib_r, own_sem):
+    row, me, core, sibling = place()
+    x = me % 2
+    spot = ring_place(row)
+    beside = (row, (1 - x) * 2 + core)
+    ahead = (ring_row((spot + 1) % RING), x * 2 + core)
+    behind = (ring_row((spot + RING - 1) % RING), x * 2 + core)
+    ways = (ahead, behind)
+    barrier = pltpu.get_barrier_semaphore()
+    for device in (ahead, behind, beside, sibling):
+        pl.semaphore_signal(barrier, inc=1, device_id=device, device_id_type=MESH)
+
+    def span(part):
+        return GATHER_CUTS[part], GATHER_CUTS[part + 1] - GATHER_CUTS[part]
+
+    def piece(source_spot, source_x, part):
+        low, size = span(part)
+        base = (ring_row(source_spot) * 4 + source_x * 2 + core) * CH
+        return flat.at[pl.ds(pl.multiple_of(base + low, 16), size)]
+
+    def mine(part):
+        low, size = span(part)
+        return shard.at[pl.ds(low, size)]
+
+    def origin(hop, way):
+        return (spot - hop + RING) % RING if way == 0 else (spot + hop) % RING
+
+    def item(hop, way, what):
+        part = way if what else 2 + way
+        return origin(hop, way), (1 - x if what == 2 else x), part
+
+    def ring(hop, way, what, first=False):
+        to = piece(*item(hop, way, what))
+        source = mine(item(hop, way, what)[2]) if first and what < 2 else to
+        return remote(
+            source, to, ring_s.at[what, way, hop], ring_r.at[what, way, hop], ways[way]
+        )
+
+    def cross(slot, way, first=False):
+        if isinstance(slot, int) and slot == 8:
+            to, source = piece(spot, x, way), mine(way)
+        else:
+            to = piece(origin(slot, way), x, 2 + way)
+            source = mine(2 + way) if first else to
+        return remote(source, to, x_s.at[way, slot], x_r.at[way, slot], beside)
+
+    def share(where, slot, way, what):
+        return remote(where, where, sib_s.at[what, way, slot], sib_r.at[what, way, slot], sibling)
+
+    def from_beside(slot, way):
+        if isinstance(slot, int) and slot == 8:
+            return piece(spot, 1 - x, way)
+        return piece(origin(slot, way), 1 - x, 2 + way)
+
+    base = pl.multiple_of((row * 4 + x * 2 + core) * CH, 16)
+    whole = flat.at[pl.ds(base, CH)]
+    own = pltpu.make_async_copy(shard, whole, own_sem)
+    own.start()
+    pl.semaphore_wait(barrier, 4)
+    for way in range(2):
+        ring(0, way, 0, True).start()
+        cross(8, way).start()
+    for way in range(2):
+        ring(0, way, 1, True).start()
+        cross(0, way, True).start()
+    given = remote(shard, whole, sib_s.at[3, 0, 9], sib_r.at[3, 0, 9], sibling)
+    given.start()
+    for way in range(2):
+        cross(8, way).wait_recv()
+        ring(0, way, 2).start()
+        share(from_beside(8, way), 8, way, 3).start()
+
+    def step(hop, carry):
+        for what in range(3):
+            for way in range(2):
+                ring(hop - 1, way, what).wait_recv()
+
+                @pl.when(hop < RING - 1)
+                def _():
+                    ring(hop, way, what).start()
+
+                if what == 0:
+                    cross(hop, way).start()
+                share(piece(*item(hop, way, what)), hop - 1, way, what).start()
+        for way in range(2):
+            cross(hop - 1, way).wait_recv()
+            share(from_beside(hop - 1, way), hop - 1, way, 3).start()
+        return carry
+
+    lax.fori_loop(1, RING, step, 0)
+    for way in range(2):
+        cross(RING - 1, way).wait_recv()
+        share(from_beside(RING - 1, way), RING - 1, way, 3).start()
+    own.wait()
+
+    def settle(hop, carry):
+        for way in range(2):
+            for what in range(3):
+                ring(hop, way, what).wait_send()
+                share(piece(*item(hop + 1, way, what)), hop, way, what).wait()
+        return carry
+
+    lax.fori_loop(0, RING - 1, settle, 0)
+
+    def settle_cross(slot, carry):
+        for way in range(2):
+            cross(slot, way).wait_send()
+            share(from_beside(slot, way), slot, way, 3).wait()
+        return carry
+
+    lax.fori_loop(0, RING, settle_cross, 0)
+    for way in range(2):
+        cross(8, way).wait_send()
+        share(from_beside(8, way), 8, way, 3).wait()
+    given.wait()
+
+
+def ag(shard):
+    anywhere = pl.BlockSpec(memory_space=pl.ANY)
+    dma = pltpu.SemaphoreType.DMA
+    return pl.pallas_call(
+        gather_kernel,
+        out_shape=jax.ShapeDtypeStruct((32 * CH, 128), bf16),
+        in_specs=[anywhere],
+        out_specs=anywhere,
+        scratch_shapes=[
+            dma((3, 2, 7)),
+            dma((3, 2, 7)),
+            dma((2, 9)),
+            dma((2, 9)),
+            dma((4, 2, 10)),
+            dma((4, 2, 10)),
+            dma,
+        ],
+        compiler_params=pltpu.CompilerParams(collective_id=0, has_side_effects=True),
+        name="gather_weights",
+    )(shard)
+
+
+def sum_kernel(
+    grad, loss, total, stats,
+    own, sib, xin, rin_b, rin_a, xlast, st_mine, st_sib, st_sum, st_all,
+    own_s, sib_s, sib_r, x_s, x_r, last_s, last_r, ring_s, ring_r, tell_s, tell_r, pair_s, pair_r,
+):
+    row, me, core, sibling = place()
+    x = me % 2
+    spot = ring_place(row)
+    beside = (row, (1 - x) * 2 + core)
+    ahead = (ring_row((spot + 1) % RING), x * 2 + core)
+    behind = (ring_row((spot + RING - 1) % RING), x * 2 + core)
+    ways = (ahead, behind)
+    barrier = greet_chips(me, core, sibling)
+    sizes = [SUM_CUTS[k + 1] - SUM_CUTS[k] for k in range(4)]
+
+    def owner(turn, way):
+        return (spot - 1 - turn + 2 * RING) % RING if way == 0 else (spot + 1 + turn) % RING
+
+    def source(turn, way, other_x, part, side):
+        owner_x = (1 - x) if other_x else x
+        base = (ring_row(owner(turn, way)) * 4 + owner_x * 2 + side) * OWN // 16 * 16
+        return grad.at[pl.ds(pl.multiple_of(base + SUM_CUTS[part], 16), sizes[part])]
+
+    def part_of(way, what):
+        return way if what >= 2 else 2 + way
+
+    def held(buf, turn, way, what):
+        part = part_of(way, what)
+        return buf.at[what % 2, turn, pl.ds(SUM_CUTS[part], sizes[part])]
+
+    def load(turn, way, what):
+        return pltpu.make_async_copy(
+            source(turn, way, what % 2, part_of(way, what), core),
+            held(own, turn, way, what),
+            own_s.at[what, way, turn],
+        )
+
+    def give(turn, way, what):
+        return remote(
+            source(turn, way, what % 2, part_of(way, what), 1 - core),
+            held(sib, turn, way, what),
+            sib_s.at[what, way, turn],
+            sib_r.at[what, way, turn],
+            sibling,
+        )
+
+    def cross(turn, way):
+        return remote(
+            held(own, turn, way, 1),
+            xin.at[turn, pl.ds(SUM_CUTS[2 + way] - SUM_CUTS[2], sizes[2 + way])],
+            x_s.at[way, turn],
+            x_r.at[way, turn],
+            beside,
+        )
+
+    def got(way, slot, what):
+        if what == 0:
+            return rin_b.at[slot, pl.ds(SUM_CUTS[2 + way] - SUM_CUTS[2], sizes[2 + way])]
+        return rin_a.at[what - 2, slot, pl.ds(SUM_CUTS[way], sizes[way])]
+
+    def ring(turn, way, what, first=False):
+        where = held(own, turn, way, what) if first else got(way, turn - 1, what)
+        return remote(
+            where,
+            got(way, turn, what),
+            ring_s.at[what, way, turn],
+            ring_r.at[what, way, turn],
+            ways[way],
+        )
+
+    order = (1, 2, 3, 0)
+
+    def begin_own(turn, carry):
+        for what in order:
+            for way in range(2):
+                load(turn, way, what).start()
+        return carry
+
+    def begin_sib(turn, carry):
+        for what in order:
+            for way in range(2):
+                give(turn, way, what).start()
+        return carry
+
+    begin_own(0, 0)
+    pl.semaphore_wait(barrier, CHIPS)
+    begin_sib(0, 0)
+    lax.fori_loop(1, RING, lambda t, c: begin_sib(t, begin_own(t, c)), 0)
+
+    def both(turn, way, what):
+        load(turn, way, what).wait()
+        give(turn, way, what).wait_recv()
+        return held(own, turn, way, what)[...].astype(f32) + held(sib, turn, way, what)[...].astype(f32)
+
+    def send_across(turn):
+        for way in range(2):
+            held(own, turn, way, 1)[...] = both(turn, way, 1).astype(bf16)
+            cross(turn, way).start()
+
+    def across(turn, way):
+        cross(turn, way).wait_recv()
+        return xin[turn, pl.ds(SUM_CUTS[2 + way] - SUM_CUTS[2], sizes[2 + way])].astype(f32)
+
+    send_across(0)
+    for what in (2, 3):
+        for way in range(2):
+            held(own, 0, way, what)[...] = both(0, way, what).astype(bf16)
+            ring(0, way, what, True).start()
+    send_across(1)
+    for way in range(2):
+        held(own, 0, way, 0)[...] = (both(0, way, 0) + across(0, way)).astype(bf16)
+        ring(0, way, 0, True).start()
+
+    def step(turn, carry):
+        send_across(turn + 1)
+        for what in (2, 3, 0):
+            for way in range(2):
+                part = both(turn, way, what)
+                if what == 0:
+                    part = part + across(turn, way)
+                ring(turn - 1, way, what, True).wait_recv()
+                where = got(way, turn - 1, what)
+                where[...] = (where[...].astype(f32) + part).astype(bf16)
+                ring(turn, way, what).start()
+        return carry
+
+    lax.fori_loop(1, RING - 1, step, 0)
+    last = RING - 1
+    def to_beside(way):
+        return remote(
+            got(way, last - 1, 3),
+            xlast.at[pl.ds(SUM_CUTS[way], sizes[way])],
+            last_s.at[way],
+            last_r.at[way],
+            beside,
+        )
+
+    for way in range(2):
+        part = both(last, way, 3)
+        ring(last - 1, way, 3, True).wait_recv()
+        where = got(way, last - 1, 3)
+        where[...] = (where[...].astype(f32) + part).astype(bf16)
+        to_beside(way).start()
+    for what in (2, 0):
+        for way in range(2):
+            part = both(last, way, what)
+            if what == 0:
+                part = part + across(last, way)
+            ring(last - 1, way, what, True).wait_recv()
+            low = SUM_CUTS[part_of(way, what)]
+            total[low : low + sizes[part_of(way, what)]] = got(way, last - 1, what)[...].astype(f32) + part
+    for way in range(2):
+        to_beside(way).wait_recv()
+        low = SUM_CUTS[way]
+        total[low : low + sizes[way]] += xlast[low : low + sizes[way]].astype(f32)
+
+    first = ((row * 4 + x * 2 + core) * OWN) % 16
+    rows = lax.broadcasted_iota(jnp.int32, (CHR, 128), 0)
+    value = total[...]
+    squares = jnp.where((rows >= first) & (rows < first + OWN), value * value, 0.0)
+    st_mine[0:8] = jnp.sum(squares.reshape(CHR // 8, 8, 128), axis=0)
+    st_mine[8:16] = loss[...]
+    pair = remote(st_mine, st_sib, pair_s, pair_r, sibling)
+    pair.start()
+    pair.wait_recv()
+    st_sum[...] = st_mine[...] + st_sib[...]
+    st_all[me] = st_sum[...]
+
+    def tell(k):
+        return remote(
+            st_sum, st_all.at[me], tell_s.at[k], tell_r.at[k],
+            chip_device(lax.rem(me + k, CHIPS), core),
+        )
+
+    def tell_one(k, carry):
+        tell(k).start()
+        return carry
+
+    lax.fori_loop(1, CHIPS, tell_one, 0)
+
+    def settle(turn, carry):
+        for way in range(2):
+            for what in range(4):
+                give(turn, way, what).wait_send()
+            cross(turn, way).wait_send()
+
+            @pl.when(turn < RING - 1)
+            def _():
+                for what in (0, 2, 3):
+                    ring(turn, way, what, True).wait_send()
+
+        return carry
+
+    lax.fori_loop(0, RING, settle, 0)
+    for way in range(2):
+        to_beside(way).wait_send()
+
+    def told(k, carry):
+        tell(k).wait_recv()
+        return carry
+
+    lax.fori_loop(1, CHIPS, told, 0)
+    everything = st_all[0]
+    for k in range(1, CHIPS):
+        everything = everything + st_all[k]
+    stats[...] = everything
+
+    def tell_done(k, carry):
+        tell(k).wait_send()
+        return carry
+
+    lax.fori_loop(1, CHIPS, tell_done, 0)
+    pair.wait_send()
+
+
+def rs(grad, loss):
+    vm, dma = pltpu.VMEM, pltpu.SemaphoreType.DMA
+    first, second = SUM_CUTS[2], SUM_CUTS[4] - SUM_CUTS[2]
+    shape = jax.ShapeDtypeStruct
+    return pl.pallas_call(
+        sum_kernel,
+        out_shape=[shape((CHR, 128), f32), shape((16, 128), f32)],
+        in_specs=[pl.BlockSpec(memory_space=pl.ANY), pl.BlockSpec(memory_space=vm)],
+        out_specs=[pl.BlockSpec(memory_space=vm)] * 2,
+        scratch_shapes=[
+            vm((2, RING, CHR, 128), bf16),
+            vm((2, RING, CHR, 128), bf16),
+            vm((RING, second, 128), bf16),
+            vm((RING - 1, second, 128), bf16),
+            vm((2, RING - 1, first, 128), bf16),
+            vm((first, 128), bf16),
+            vm((16, 128), f32),
+            vm((16, 128), f32),
+            vm((16, 128), f32),
+            vm((CHIPS, 16, 128), f32),
+            dma((4, 2, RING)),
+            dma((4, 2, RING)),
+            dma((4, 2, RING)),
+            dma((2, RING)),
+            dma((2, RING)),
+            dma((2,)),
+            dma((2,)),
+            dma((4, 2, RING - 1)),
+            dma((4, 2, RING - 1)),
+            dma((CHIPS,)),
+            dma((CHIPS,)),
+            dma,
+            dma,
+        ],
+        compiler_params=pltpu.CompilerParams(
+            collective_id=1, has_side_effects=True, vmem_limit_bytes=56 << 20
+        ),
+        name="sum_gradients",
+    )(grad, loss)
+
+
+MATS = [(PIN, D), (D, FF), (FF, D), (D, FF), (FF, D), (D, PIN)]
+SMALL_LAYER = 2352
+SMALLS = [6 + SMALL_LAYER, 24, 6 + SMALL_LAYER, 24, 18, 10]
+PIECE = 256
+
+
+def flat_sections():
+    at = 0
+    found = []
+    for (depth, cols), small in zip(MATS, SMALLS):
+        per_row = cols // LANES
+        found.append((at, depth, per_row, at + depth * per_row, small))
+        at += depth * per_row + small
+    return found
+
+
+def piece_rows(depth, per_row):
+    rows = depth
+    while rows * per_row > 7680:
+        rows -= PIECE
+        while depth % rows:
+            rows -= PIECE
+    return rows
+
+
+def unpack_kernel(flat, *refs):
+    mats, smalls = refs[:6], refs[6:12]
+    raw, wide, out24, out6, out10, in_sem, out_sem = refs[12:]
+    outs = {24: out24, 6: out6, 10: out10}
+    steps = []
+    for i, (start, depth, per_row, small_at, small) in enumerate(flat_sections()):
+        rows = piece_rows(depth, per_row)
+        for top in range(0, depth, rows):
+            steps.append((i, start + top * per_row, rows * per_row, per_row, top, rows))
+        steps.append((i, small_at, small, 0, 0, 0))
+
+    def fetch(n):
+        _, at, count, *_ = steps[n]
+        low = at // 16 * 16
+        size = -(-(at + count - low) // 16) * 16
+        return pltpu.make_async_copy(
+            flat.at[pl.ds(low, size)], raw.at[n % 2, pl.ds(0, size)], in_sem.at[n % 2]
+        ), size
+
+    fetch(0)[0].start()
+    pending = {}
+    for n, (i, at, count, per_row, top, rows) in enumerate(steps):
+        if n + 1 < len(steps):
+            fetch(n + 1)[0].start()
+        copy, size = fetch(n)
+        copy.wait()
+        wide[0:size] = raw[n % 2, 0:size].astype(f32)
+        shift = at % 16
+        if not per_row:
+            smalls[i][0:count] = wide[shift : shift + count]
+            continue
+        out = outs[per_row]
+        if per_row in pending:
+            pending.pop(per_row).wait()
+        for part in range(0, rows, PIECE):
+            for j in range(per_row):
+                out[part : part + PIECE, j * LANES : (j + 1) * LANES] = wide[
+                    pl.ds(shift + part * per_row + j, PIECE, stride=per_row), :
+                ].astype(bf16)
+        done = pltpu.make_async_copy(
+            out.at[pl.ds(0, rows)], mats[i].at[pl.ds(top, rows)], out_sem.at[(24, 6, 10).index(per_row)]
+        )
+        done.start()
+        pending[per_row] = done
+    for done in pending.values():
+        done.wait()
+
+
+def unpack_flat(flat):
+    vm, anywhere = pltpu.VMEM, pl.BlockSpec(memory_space=pl.ANY)
+    shape = jax.ShapeDtypeStruct
+    padded = [-(-count // 8) * 8 for count in SMALLS]
+    return pl.pallas_call(
+        unpack_kernel,
+        out_shape=[shape(m, bf16) for m in MATS] + [shape((n, LANES), f32) for n in padded],
+        in_specs=[anywhere],
+        out_specs=[anywhere] * 6 + [pl.BlockSpec(memory_space=vm)] * 6,
+        scratch_shapes=[
+            vm((2, 7696, LANES), bf16),
+            vm((7696, LANES), f32),
+            vm((256, FF), bf16),
+            vm((1280, D), bf16),
+            vm((768, PIN), bf16),
+            pltpu.SemaphoreType.DMA((2,)),
+            pltpu.SemaphoreType.DMA((3,)),
+        ],
+        compiler_params=pltpu.CompilerParams(vmem_limit_bytes=48 << 20),
+        name="unpack_flat",
+    )(flat)
+
+
+def pack_kernel(counts, *refs):
+    pairs = [refs[4 * i : 4 * i + 4] for i in range(6)]
+    smalls, rest = [], refs[24:]
+    for number in counts:
+        smalls.append(rest[:number])
+        rest = rest[number:]
+    flat, across, side, wide, narrow, sem = rest
+    pending = []
+
+    def emit(at, full):
+        return pltpu.make_async_copy(narrow.at[pl.ds(0, full)], flat.at[pl.ds(at, full)], sem)
+
+    for i, (start, depth, per_row, small_at, small) in enumerate(flat_sections()):
+        x0, x1, g0, g1 = pairs[i]
+        cols = per_row * LANES
+        for half, (x, g) in enumerate(((x0, g0), (x1, g1))):
+            for part in range(0, depth, PIECE):
+                across[part : part + PIECE, half * 128 : half * 128 + 128] = x[
+                    :, part : part + PIECE
+                ].T
+            side[half * 128 : half * 128 + 128, 0:cols] = g[...]
+        rows = piece_rows(depth, per_row)
+        full = rows * per_row
+        shift = start % 16
+        before = pending.pop() if pending else None
+
+        def step(it, carry):
+            top = pl.multiple_of(it * rows, PIECE)
+            for part in range(0, rows, PIECE):
+                left = across[pl.ds(pl.multiple_of(top + part, PIECE), PIECE), :]
+                for j in range(0, per_row, 2):
+                    value = dot(left, side[:, j * LANES : (j + 2) * LANES])
+                    for side_by in range(2):
+                        wide[
+                            pl.ds(shift + part * per_row + j + side_by, PIECE, stride=per_row), :
+                        ] = value[:, side_by * LANES : (side_by + 1) * LANES]
+            if before is not None:
+                @pl.when(it == 0)
+                def _():
+                    before.wait()
+
+            @pl.when(it > 0)
+            def _():
+                emit(0, full).wait()
+
+            narrow[0:full] = wide[0:full].astype(bf16)
+            emit(pl.multiple_of(start - shift + it * full, 16), full).start()
+            wide[0:16] = wide[full : full + 16]
+            return carry
+
+        lax.fori_loop(0, depth // rows, step, 0)
+        shift = small_at % 16
+        into = shift
+        for piece in smalls[i]:
+            wide[into : into + piece.shape[0]] = piece[...]
+            into += piece.shape[0]
+        full = (shift + small) // 16 * 16
+        if i == 5:
+            wide[shift + small : GROWS - small_at + shift] = jnp.zeros(
+                (GROWS - small_at - small, LANES), f32
+            )
+            full = GROWS - small_at + shift
+        emit(0, rows * per_row).wait()
+        narrow[0:full] = wide[0:full].astype(bf16)
+        done = emit(small_at - shift, full)
+        done.start()
+        pending.append(done)
+        if i < 5:
+            wide[0:16] = wide[full : full + 16]
+    pending.pop().wait()
+
+
+def pack_flat(pairs, smalls):
+    vm, whole = pltpu.VMEM, pl.BlockSpec(memory_space=pltpu.VMEM)
+    args = [a for four in pairs for a in four] + [a for some in smalls for a in some]
+    return pl.pallas_call(
+        functools.partial(pack_kernel, [len(some) for some in smalls]),
+        out_shape=jax.ShapeDtypeStruct((GROWS, LANES), bf16),
+        in_specs=[whole] * len(args),
+        out_specs=pl.BlockSpec(memory_space=pl.ANY),
+        scratch_shapes=[
+            vm((FF, 256), bf16),
+            vm((256, FF), bf16),
+            vm((7712, LANES), f32),
+            vm((7712, LANES), bf16),
+            pltpu.SemaphoreType.DMA,
+        ],
+        compiler_params=pltpu.CompilerParams(vmem_limit_bytes=52 << 20),
+        name="pack_flat",
+    )(*args)
+
+
+def split_small(rows, layouts):
+    found, at = [], 0
+    for layout in layouts:
+        count = math.prod(layout) // LANES
+        found.append(rows[at : at + count].reshape(layout))
+        at += count
+    return found
+
+
+SPEC_ROWS = (2, NBLK, BS * BS // LANES, LANES)
+LAYER_SMALL = [(D,), (D,), SPEC_ROWS, (2, NBLK, BS), SPEC_ROWS, (2, NBLK, BS), (D,), (D,)]
+
+
+def local_fast(frames, targets, regions, master, first_moment, second_moment):
+    height, width = 16, 128
+    device = lax.axis_index("row") * 4 + lax.axis_index("col")
+    _, chip, core, _ = place()
+    block = chip % NBLK
+    shard = master.astype(bf16).reshape(OWN, LANES)
+    halo = lax.ppermute(shard[:320], ("row", "col"), [(k + 1, k) for k in range(31)])
+    chunk = lax.dynamic_slice_in_dim(jnp.concatenate([shard, halo]), 10 * device, CH, 0)
+    unpacked = unpack_flat(ag(chunk))
+    embed, in0, out0, in1, out1, head = unpacked[:6]
+    smalls = unpacked[6:]
+    embed_bias, *layer0 = split_small(smalls[0], [(D,)] + LAYER_SMALL)
+    (c1_0,) = split_small(smalls[1], [(FF,)])
+    c2_0, *layer1 = split_small(smalls[2], [(D,)] + LAYER_SMALL)
+    (c1_1,) = split_small(smalls[3], [(FF,)])
+    c2_1, gain3, shift3 = split_small(smalls[4], [(D,)] * 3)
+    (head_bias,) = split_small(smalls[5], [(PIN,)])
+    layers = [(layer0, in0, c1_0, out0, c2_0), (layer1, in1, c1_1, out1, c2_1)]
+    tables = transform_tables(core)
+    row_ids = lax.axis_index("row") * 2 + jnp.arange(2, dtype=jnp.int32)
+    col_ids = lax.axis_index("col") * 32 + jnp.arange(32, dtype=jnp.int32)
+    cell_masks = region_masks(regions, row_ids, col_ids, width)
+    weighted = latitude(row_ids, height)[None, :, None] * cell_masks
+    every_row = jnp.arange(height, dtype=jnp.int32)
+    every_col = jnp.arange(width, dtype=jnp.int32)
+    total_weight = (
+        jnp.sum(
+            latitude(every_row, height)[None, :, None]
+            * region_masks(regions, every_row, every_col, width)
+        )
+        * STEPS
+    )
+    flat_mask = cell_masks.reshape(128, 1)
+    flat_weight = weighted.reshape(128, 1)
+    inputs = (frames.reshape(128, PIN).astype(f32) * flat_mask).astype(bf16)
+    goals = [targets[:, s].reshape(128, PIN).astype(f32) for s in range(STEPS)]
+    spectral_weights = []
+    for small, *_ in layers:
+        found = []
+        for j in (2, 4):
+            w = lax.dynamic_index_in_dim(small[j], block, 1, False).reshape(2, BS, BS)
+            b = lax.dynamic_index_in_dim(small[j + 1], block, 1, False)
+            found += [spread_weight(w[0], w[1]).astype(bf16), spread_bias(b)]
+        spectral_weights.append(found)
+
+    def lin(values, weight16, bias_vec):
+        return mult("ci,io->co", values, weight16) + bias_vec
+
+    loss_cells = jnp.zeros((128,), f32)
+    history = []
+    for roll_step in range(STEPS):
+        stream = lin(inputs, embed, embed_bias)
+        saved = []
+        for (small, w_in, c1, w_out, c2), spectral_w in zip(layers, spectral_weights):
+            mixed, waves = filter_forward(
+                stream, small[0][None], small[1][None], tables, spectral_w
+            )
+            normed = layer_norm(mixed, small[6], small[7]).astype(bf16)
+            before = lin(normed, w_in, c1)
+            hidden = jax.nn.gelu(before, approximate=False).astype(bf16)
+            saved.append((stream, waves, mixed, normed, before, hidden))
+            stream = mixed + lin(hidden, w_out, c2)
+        normed = layer_norm(stream, gain3, shift3).astype(bf16)
+        predicted = lin(normed, head, head_bias)
+        errors = predicted - goals[roll_step]
+        loss_cells = loss_cells + flat_weight[:, 0] * jnp.sum(errors * errors, axis=-1)
+        history.append((inputs, saved, stream, normed, errors))
+        inputs = (predicted * flat_mask).astype(bf16)
+    carried = jnp.zeros((128, PIN), f32)
+    pairs = [[None] * 4 for _ in range(6)]
+    parts = []
+
+    def keep(i, step, values, grad):
+        pairs[i][step] = values.astype(bf16)
+        pairs[i][2 + step] = grad.astype(bf16)
+
+    for roll_step in reversed(range(STEPS)):
+        inputs, saved, stream, normed, errors = history[roll_step]
+        grad_pred = 2.0 * flat_weight * errors / total_weight + carried
+        keep(5, roll_step, normed, grad_pred)
+        _, pullback = jax.vjp(layer_norm, stream, gain3, shift3)
+        grad_stream, grad_gain3, grad_shift3 = pullback(
+            rounded(mult("co,io->ci", grad_pred, head))
+        )
+        found = {"hb": jnp.sum(grad_pred, axis=0), "g3": grad_gain3, "s3": grad_shift3}
+        for idx in reversed(range(LAYERS)):
+            small, w_in, c1, w_out, c2 = layers[idx]
+            stream, waves, mixed, normed, before, hidden = saved[idx]
+            keep(2 + 2 * idx, roll_step, hidden, grad_stream)
+            grad_hidden = mult("co,io->ci", grad_stream, w_out)
+            _, pullback = jax.vjp(lambda value: jax.nn.gelu(value, approximate=False), before)
+            (grad_before,) = pullback(rounded(grad_hidden))
+            keep(1 + 2 * idx, roll_step, normed, grad_before)
+            _, pullback = jax.vjp(layer_norm, mixed, small[6], small[7])
+            grad_extra, grad_gain2, grad_shift2 = pullback(
+                rounded(mult("co,io->ci", grad_before, w_in))
+            )
+            found[f"c2{idx}"] = jnp.sum(grad_stream, axis=0)
+            found[f"c1{idx}"] = jnp.sum(grad_before, axis=0)
+            grad_stream, norm_grads, gw1, gw2, gb = filter_backward(
+                grad_stream + grad_extra, stream, small[0][None], waves, tables,
+                spectral_weights[idx],
+            )
+            found[f"layer{idx}"] = (norm_grads, gw1, gw2, gb, grad_gain2, grad_shift2)
+        keep(0, roll_step, inputs, grad_stream)
+        found["eb"] = jnp.sum(grad_stream, axis=0)
+        parts.append(found)
+        if roll_step:
+            carried = flat_mask * rounded(mult("co,io->ci", grad_stream, embed))
+    sums = jax.tree.map(jnp.add, parts[0], parts[1])
+
+    def as_rows(value):
+        return value.reshape(-1, LANES)
+
+    def placed(local_grad):
+        local_grad = local_grad.reshape(2, 1, -1)
+        whole = jnp.zeros((2, NBLK, local_grad.shape[2]), f32)
+        return as_rows(lax.dynamic_update_slice_in_dim(whole, local_grad, block, 1))
+
+    def layer_rows(idx):
+        norm_grads, gw1, gw2, gb, gain2, shift2 = sums[f"layer{idx}"]
+        return [
+            as_rows(norm_grads[0]),
+            as_rows(norm_grads[1]),
+            placed(fold_weight(gw1)),
+            placed(fold_bias(gb[0])),
+            placed(fold_weight(gw2)),
+            placed(fold_bias(gb[1])),
+            as_rows(gain2),
+            as_rows(shift2),
+        ]
+
+    small_grads = [
+        [as_rows(sums["eb"])] + layer_rows(0),
+        [as_rows(sums["c10"])],
+        [as_rows(sums["c20"])] + layer_rows(1),
+        [as_rows(sums["c11"])],
+        [as_rows(sums[k]) for k in ("c21", "g3", "s3")],
+        [as_rows(sums["hb"])],
+    ]
+    flat_grad = pack_flat(pairs, small_grads)
+    loss_tile = jnp.concatenate([loss_cells[None], jnp.zeros((7, LANES), f32)])
+    summed, stats = rs(flat_grad, loss_tile)
+    reduced = lax.dynamic_slice_in_dim(summed, (device * OWN) % 16, OWN, 0).reshape(-1)
+    grad_norm = jnp.sqrt(jnp.sum(stats[:8]))
+    return finish_step(
+        reduced, grad_norm, master, first_moment, second_moment, jnp.sum(stats[8:]), total_weight
+    )
+
+
+def finish_step(reduced, grad_norm, master, first_moment, second_moment, loss_all, total_weight):
+    clipped = reduced * (CLIP / jnp.maximum(grad_norm, CLIP))
+    first_out = BETA_ONE * first_moment + (1.0 - BETA_ONE) * clipped
+    second_out = BETA_TWO * second_moment + (1.0 - BETA_TWO) * clipped * clipped
+    corrected_one = first_out / (1.0 - BETA_ONE**ADAM_STEP)
+    corrected_two = second_out / (1.0 - BETA_TWO**ADAM_STEP)
+    master_out = master - RATE * (
+        corrected_one / (jnp.sqrt(corrected_two) + ADAM_EPS) + DECAY * master
+    )
+    return (
+        master_out,
+        first_out,
+        second_out,
+        master_out.astype(bf16),
+        loss_all,
+        total_weight,
+        grad_norm,
+    )
 
 
 def local(frames, targets, regions, master, first_moment, second_moment):
@@ -400,4 +1679,5 @@
         P(),
         P(),
     )
-    return jax.shard_map(local, mesh=mesh, in_specs=in_specs, out_specs=out_specs, check_vma=False)
+    body = local_fast if dict(mesh.shape) == {"row": 8, "col": 4} else local
+    return jax.shard_map(body, mesh=mesh, in_specs=in_specs, out_specs=out_specs, check_vma=False)

time: 2900 us -> 607 us (0.21); the launches traced: 2850 us -> 602 us
  local copies, waits for them, and re-layouts: 879 us -> 35.7 us
  blocking collectives: 554 us -> 0 us
  waiting for transfers between devices: 479 us -> 0.01 us
  Pallas kernels: 0 us -> 455 us
  matrix products: 434 us -> 69 us
  other arithmetic: 280 us -> 32.5 us
  starting transfers between devices: 205 us -> 1.42 us
    unnamed x1 -> x0, blocking collectives: 499 us -> none
    unnamed x724 -> x398, local copies, waits for them, and re-layouts: 495 us -> 12.5 us
    pallas_call x0 -> x12, Pallas kernels: none -> 455 us  [the longest x8 195 us: filter_call(): pl.pallas_call(kernel, out_shape=outs, in_specs=[spec] * len(args), out_s...]
    all_gather x1 -> x0, waiting for transfers between devices: 266 us -> none  [local(): lax.all_gather(master.astype(jnp.bfloat16), ('row', 'col'), axis=0, tiled...]
    dot_general x192 -> x0, matrix products: 239 us -> none  [the longest x64 78.3 us: contract(): return jnp.einsum(form, table, values, precision=highest)]
    all_to_all x47 -> x0, waiting for transfers between devices: 213 us -> none  [the longest x8 47.9 us: grid(): lax.all_to_all(back_im.astype(jnp.bfloat16), 'row', split_axis=1, concat_...]
    all_to_all x47 -> x0, starting transfers between devices: 181 us -> none  [the longest x8 32.7 us: grid(): lax.all_to_all(back_im.astype(jnp.bfloat16), 'row', split_axis=1, concat_...]
    all_gather x1 -> x0, other arithmetic: 143 us -> none  [local(): lax.all_gather(master.astype(jnp.bfloat16), ('row', 'col'), axis=0, tiled...]
  transfers between devices with their start and end apart: 49 -> 1, of which waited for: 41 -> 0; matrix products, arithmetic and copies ran while one was open for 10% -> 1% of each run, Pallas kernels for 0% -> 0%
where the time goes in v1:
time: 607 us; the launch traced here: 602 us
  Pallas kernels  455 us (75%)
  matrix products  69 us (11%)
  local copies, waits for them, and re-layouts  35.7 us (6%)
  other arithmetic  32.5 us (5%)
  between operations  7.95 us (1%)
    pallas_call x8, Pallas kernels, filter_call(): pl.pallas_call(kernel, out_shape=outs, in_specs=[spec] * len(args), out_s...  195 us
    pallas_call x1, Pallas kernels, rs(): pl.pallas_call(sum_kernel, out_shape=[shape((CHR, 128), f32), shape((16,...  107 us
    pallas_call x1, Pallas kernels, ag(): pl.pallas_call(gather_kernel, out_shape=jax.ShapeDtypeStruct((32 * CH, 12...  96.3 us
    dot_general x23, matrix products, mult(): jnp.einsum(form, left.astype(jnp.bfloat16), right.astype(jnp.bfloat16), p...  69 us
    pallas_call x1, Pallas kernels, pack_flat(): pl.pallas_call(functools.partial(pack_kernel, [len(some) for some in smal...  29.9 us
    pallas_call x1, Pallas kernels, unpack_flat(): pl.pallas_call(unpack_kernel, out_shape=[shape(m, bf16) for m in MATS] +...  27.5 us
    unnamed x398, local copies, waits for them, and re-layouts  12.5 us
  transfers between devices with their start and end apart: 1, of which 0 were waited for; matrix products, arithmetic and copies ran while one was open for 1% of the time, Pallas kernels for 0%

profile of v1, /device:TPU:0, one launch (start us, length us, event | category | flops | bytes accessed | tf_op | source)
XLA Modules:
  0.0 601.9 jit_solution(1079801307406754235)
XLA Ops:
  0.6 1.6 convert_element_type.221
  2.3 1.4 collective-permute-start
  5.4 0.9 fusion.123
  8.5 2.7 fusion.55.shard
  11.2 96.3 %gather_weights.1.flat = bf16[94208,128]{1,0:T(8,128)(2,1)} custom-call(bf16[2944,128]{1,0:T(8,128)(2,1)} %fusion.55.shard), custom_call_target="tpu_custom_call" | custom-call | tf_op jit(solution)/shard_map/gather_weights/pallas_call | solution.py:921
  107.5 27.5 %unpack_flat.1 = (bf16[1280,768]{1,0:T(8,128)(2,1)S(1)}, bf16[768,3072]{1,0:T(8,128)(2,1)}, bf16[3072,768]{1,0:T(8,128)(2,1)}, bf16[768,3072]{1,0:T(8,128)(2,1)}...) custom-call(bf16[94208,128]{1,0:T(8,128)(2,1)} %gather_weights.1.flat), custom_call_target="tpu_custom_call" | custom-call | tf_op jit(solution)/shard_map/unpack_flat/pallas_call | solution.py:1273
  135.1 1.0 copy-done.37
  136.0 1.2 fusion.120
  140.7 1.4 fusion.119
  146.3 22.3 %filter_forward.4 = (f32[128,768]{1,0:T(8,128)S(1)}, bf16[4,256,256]{2,1,0:T(8,128)(2,1)S(1)}) custom-call(f32[128,768]{1,0:T(8,128)S(1)} %convolution_add_fusion.7.stream, f32[1,768]{1,0:T(1,128)S(1)} %get-tuple-element.226.gain, f32[1,768]{1,0:T(1,128)S(1)} %get-tuple-element.225.shift, bf16[128,128]{1,0:T(8,128)(2,1)S(1)} %get-tuple-element.228.column_table, ...), custom_call_target="tpu_custom_call" | custom-call | tf_op jit(solution)/shard_map/filter_forward/pallas_call | solution.py:694
  172.4 8.5 %multiply_convert_fusion.3 = (bf16[128,3072]{1,0:T(8,128)(2,1)S(1)}, f32[128,3072]{1,0:T(8,128)}, f32[128,3072]{1,0:T(8,128)}) fusion(f32[3072]{0:T(1024)S(1)} %bitcast.209, bf16[128,768]{1,0:T(8,128)(2,1)S(1)} %add_convert_fusion.5.refs_4_, bf16[768,3072]{1,0:T(8,128)(2,1)} %get-tuple-element.52), kind=kOutput, calls=%fused_computation.92 | convolution fusion | flops 629932032 | bytes 8859648 | tf_op jit(solution)/shard_map/ci,io->co/dot_general | solution.py:69
  181.8 24.1 %filter_forward.5 = (f32[128,768]{1,0:T(8,128)S(1)}, bf16[4,256,256]{2,1,0:T(8,128)(2,1)S(1)}) custom-call(f32[128,768]{1,0:T(8,128)S(1)} %fusion.54.stream, f32[1,768]{1,0:T(1,128)S(1)} %bitcast.185, f32[1,768]{1,0:T(1,128)S(1)} %bitcast.189, bf16[128,128]{1,0:T(8,128)(2,1)S(1)} %get-tuple-element.228.column_table, ...), custom_call_target="tpu_custom_call" | custom-call | tf_op jit(solution)/shard_map/filter_forward/pallas_call | solution.py:694
  208.0 8.5 %multiply_convert_fusion.2 = (bf16[128,3072]{1,0:T(8,128)(2,1)S(1)}, f32[128,3072]{1,0:T(8,128)}, f32[128,3072]{1,0:T(8,128)}) fusion(f32[3072]{0:T(1024)S(1)} %bitcast.207, bf16[128,768]{1,0:T(8,128)(2,1)S(1)} %add_convert_fusion.4.refs_12_, bf16[768,3072]{1,0:T(8,128)(2,1)} %get-tuple-element.57), kind=kOutput, calls=%fused_computation.79 | convolution fusion | flops 629932032 | bytes 8859648 | tf_op jit(solution)/shard_map/ci,io->co/dot_general | solution.py:69
  216.7 3.5 fusion.130
  221.0 1.3 multiply_convert_fusion.4
  223.5 23.9 %filter_forward.6 = (f32[128,768]{1,0:T(8,128)S(1)}, bf16[4,256,256]{2,1,0:T(8,128)(2,1)S(1)}) custom-call(f32[128,768]{1,0:T(8,128)S(1)} %convolution_add_fusion.6.stream, f32[1,768]{1,0:T(1,128)S(1)} %get-tuple-element.226.gain, f32[1,768]{1,0:T(1,128)S(1)} %get-tuple-element.225.shift, bf16[128,128]{1,0:T(8,128)(2,1)S(1)} %copy-done.31, ...), custom_call_target="tpu_custom_call" | custom-call | tf_op jit(solution)/shard_map/filter_forward/pallas_call | solution.py:694
  249.5 8.4 %multiply_convert_fusion.1 = (bf16[128,3072]{1,0:T(8,128)(2,1)S(1)}, f32[128,3072]{1,0:T(8,128)}, f32[128,3072]{1,0:T(8,128)}) fusion(f32[3072]{0:T(1024)} %bitcast.210, bf16[128,768]{1,0:T(8,128)(2,1)S(1)} %add_convert_fusion.2.refs_5_, bf16[768,3072]{1,0:T(8,128)(2,1)} %get-tuple-element.52), kind=kOutput, calls=%fused_computation.66 | convolution fusion | flops 629932032 | bytes 8859648 | tf_op jit(solution)/shard_map/ci,io->co/dot_general | solution.py:69
  258.8 3.2 fusion.52.stream
  262.1 23.8 %filter_forward.7 = (f32[128,768]{1,0:T(8,128)S(1)}, bf16[4,256,256]{2,1,0:T(8,128)(2,1)S(1)}) custom-call(f32[128,768]{1,0:T(8,128)S(1)} %fusion.52.stream, f32[1,768]{1,0:T(1,128)S(1)} %bitcast.186, f32[1,768]{1,0:T(1,128)S(1)} %bitcast.190, bf16[128,128]{1,0:T(8,128)(2,1)S(1)} %copy-done.32, bf16[128,128]{1,0:T(8,128)(2,1)S(1)} %copy-done.27, ...), custom_call_target="tpu_custom_call" | custom-call | tf_op jit(solution)/shard_map/filter_forward/pallas_call | solution.py:694
  287.9 6.1 %multiply_convert_fusion = (bf16[128,3072]{1,0:T(8,128)(2,1)S(1)}, f32[128,3072]{1,0:T(8,128)S(1)}, f32[128,3072]{1,0:T(8,128)S(1)}) fusion(f32[3072]{0:T(1024)} %bitcast.208, bf16[128,768]{1,0:T(8,128)(2,1)S(1)} %add_convert_fusion.1.refs_13_, bf16[768,3072]{1,0:T(8,128)(2,1)} %get-tuple-element.57), kind=kOutput, calls=%fused_computation.53 | convolution fusion | flops 629932032 | bytes 8859648 | tf_op jit(solution)/shard_map/ci,io->co/dot_general | solution.py:69
  294.1 3.5 fusion.131
  298.1 1.2 multiply_reduce_fusion
  301.8 1.6 convolution_convert_fusion.3
  303.5 1.4 fusion.107
  304.9 1.7 convolution_convert_fusion.9
  308.5 25.4 %filter_backward.4 = (f32[128,768]{1,0:T(8,128)S(1)}, f32[8,768]{1,0:T(8,128)S(1)}, f32[256,256]{1,0:T(8,128)S(1)}, f32[256,256]{1,0:T(8,128)S(1)}, f32[8,256]{1,0:T(8,128)S(1)}) custom-call(f32[128,768]{1,0:T(8,128)S(1)} %add_add_fusion.9.grad, f32[128,768]{1,0:T(8,128)S(1)} %copy-done.11, f32[1,768]{1,0:T(1,128)S(1)} %bitcast.187, ...), custom_call_target="tpu_custom_call" | custom-call | tf_op jit(solution)/shard_map/filter_backward/pallas_call | solution.py:694
  334.0 1.6 convolution_convert_fusion.2
  336.1 1.4 fusion.111
  338.3 4.1 convolution_convert_fusion.8
  344.8 25.3 %filter_backward.5 = (f32[128,768]{1,0:T(8,128)S(1)}, f32[8,768]{1,0:T(8,128)S(1)}, f32[256,256]{1,0:T(8,128)S(1)}, f32[256,256]{1,0:T(8,128)S(1)}, f32[8,256]{1,0:T(8,128)S(1)}) custom-call(f32[128,768]{1,0:T(8,128)S(1)} %get-tuple-element.180.grad, f32[128,768]{1,0:T(8,128)S(1)} %copy-done.7, f32[1,768]{1,0:T(1,128)S(1)} %get-tuple-element.226.gain, ...), custom_call_target="tpu_custom_call" | custom-call | tf_op jit(solution)/shard_map/filter_backward/pallas_call | solution.py:694
  371.6 1.1 fusion.104
  375.6 1.6 convolution_convert_fusion.1
  378.3 1.7 convolution_convert_fusion.6
  381.8 24.9 %filter_backward.6 = (f32[128,768]{1,0:T(8,128)S(1)}, f32[8,768]{1,0:T(8,128)S(1)}, f32[256,256]{1,0:T(8,128)S(1)}, f32[256,256]{1,0:T(8,128)S(1)}, f32[8,256]{1,0:T(8,128)S(1)}) custom-call(f32[128,768]{1,0:T(8,128)S(1)} %add_add_fusion.7.grad, f32[128,768]{1,0:T(8,128)S(1)} %copy-done.9, f32[1,768]{1,0:T(1,128)S(1)} %bitcast.188, ...), custom_call_target="tpu_custom_call" | custom-call | tf_op jit(solution)/shard_map/filter_backward/pallas_call | solution.py:694
  407.4 1.3 dynamic_update_slice.30
  408.6 0.9 reshape.791.refs_39_
  410.1 1.7 dynamic_update_slice.28
  411.8 0.9 reshape.788.refs_37_
  412.8 4.1 convolution_convert_fusion
  417.8 4.3 convolution_convert_fusion.5
  423.5 25.1 %filter_backward.7 = (f32[128,768]{1,0:T(8,128)S(1)}, f32[8,768]{1,0:T(8,128)S(1)}, f32[256,256]{1,0:T(8,128)S(1)}, f32[256,256]{1,0:T(8,128)S(1)}, f32[8,256]{1,0:T(8,128)S(1)}) custom-call(f32[128,768]{1,0:T(8,128)S(1)} %get-tuple-element.178.grad, f32[128,768]{1,0:T(8,128)S(1)} %copy-done.5, f32[1,768]{1,0:T(1,128)S(1)} %get-tuple-element.226.gain, ...), custom_call_target="tpu_custom_call" | custom-call | tf_op jit(solution)/shard_map/filter_backward/pallas_call | solution.py:694
  449.2 1.3 dynamic_update_slice.26
  450.5 0.9 reshape.785.refs_29_
  452.2 1.4 dynamic_update_slice.24
  455.6 29.9 %pack_flat.1.grad = bf16[93904,128]{1,0:T(8,128)(2,1)} custom-call(bf16[128,1280]{1,0:T(8,128)(2,1)} %copy-done.97, bf16[128,1280]{1,0:T(8,128)(2,1)} %copy-done.98, bf16[128,768]{1,0:T(8,128)(2,1)S(1)} %get-tuple-element.182.refs_2_, bf16[128,768]{1,0:T(8,128)(2,1)S(1)} %get-tuple-element.184.refs_3_, bf16[128,768]{1,0:T(8,128)(2,1)S(1)} %copy-done.40, ...), custom_call_target="tpu_custom_call" | custom-call | tf_op jit(solution)/shard_map/pack_flat/pallas_call | solution.py:1367
  485.5 106.8 %sum_gradients.1 = (f32[2960,128]{1,0:T(8,128)}, f32[16,128]{1,0:T(8,128)}) custom-call(bf16[93904,128]{1,0:T(8,128)(2,1)} %pack_flat.1.grad, f32[8,128]{1,0:T(8,128)} %concatenate.71.loss), custom_call_target="tpu_custom_call" | custom-call | tf_op jit(solution)/shard_map/sum_gradients/pallas_call | solution.py:1159
  592.3 1.3 slice_reduce_fusion
  594.4 5.0 fusion.101
  (604 shorter events, 44.8 us)
Async XLA Ops:
  2.3 6.2 %collective-permute-start = (bf16[320,128]{1,0:T(8,128)(2,1)S(1)}, bf16[320,128]{1,0:T(8,128)(2,1)S(1)}, u32[]{:S(2)}, u32[]{:S(2)}) collective-permute-start(bf16[320,128]{1,0:T(8,128)(2,1)S(1)} %slice_bitcast_fusion), channel_id=1, source_target_pairs={{1,0},{2,1},{3,2},{4,3},{5,4},{6,5},{7,6},{8,7},{9,8},{10,9},{11,1... | collective-permute-start | bytes 245768 | tf_op jit(solution)/shard_map/ppermute | solution.py:1403
  4.7 6.5 %copy-start.165 = (f32[128]{0:T(128)}, f32[128]{0:T(128)S(1)}, u32[]{:S(2)}) copy-start(f32[128]{0:T(128)S(1)} %reshape.795) | copy-start | bytes 1540
  7.1 138.3 %copy-start.97 = (bf16[128,1280]{1,0:T(8,128)(2,1)}, bf16[128,1280]{1,0:T(8,128)(2,1)S(1)}, u32[]{:S(2)}) copy-start(bf16[128,1280]{1,0:T(8,128)(2,1)S(1)} %fusion.56.refs_0_) | copy-start | bytes 983044
  8.5 173.3 %copy-start.25 = (bf16[128,128]{1,0:T(8,128)(2,1)}, bf16[128,128]{1,0:T(8,128)(2,1)S(1)}, u32[]{:S(2)}) copy-start(bf16[128,128]{1,0:T(8,128)(2,1)S(1)} %get-tuple-element.227.inverse_table) | copy-start | bytes 98308
  8.5 173.3 %copy-start.30 = (bf16[128,128]{1,0:T(8,128)(2,1)}, bf16[128,128]{1,0:T(8,128)(2,1)S(1)}, u32[]{:S(2)}) copy-start(bf16[128,128]{1,0:T(8,128)(2,1)S(1)} %get-tuple-element.228.column_table) | copy-start | bytes 98308
  135.0 37.3 %copy-start.80 = (f32[24,128]{1,0:T(8,128)}, f32[24,128]{1,0:T(8,128)S(1)}, u32[]{:S(2)}) copy-start(f32[24,128]{1,0:T(8,128)S(1)} %get-tuple-element.53) | copy-start | bytes 36868
  135.1 73.0 %copy-start.79 = (f32[24,128]{1,0:T(8,128)}, f32[24,128]{1,0:T(8,128)S(1)}, u32[]{:S(2)}) copy-start(f32[24,128]{1,0:T(8,128)S(1)} %get-tuple-element.58) | copy-start | bytes 36868
  144.6 27.5 %copy-start.114 = (f32[768]{0:T(1024)}, f32[768]{0:T(1024)S(1)}, u32[]{:S(2)}) copy-start(f32[768]{0:T(1024)S(1)} %get-tuple-element.160) | copy-start | bytes 9220
  144.6 27.5 %copy-start.124 = (f32[768]{0:T(1024)}, f32[768]{0:T(1024)S(1)}, u32[]{:S(2)}) copy-start(f32[768]{0:T(1024)S(1)} %get-tuple-element.161) | copy-start | bytes 9220
  145.4 78.1 %copy-start.12 = (bf16[256,256]{1,0:T(8,128)(2,1)}, bf16[256,256]{1,0:T(8,128)(2,1)S(1)}, u32[]{:S(2)}) copy-start(bf16[256,256]{1,0:T(8,128)(2,1)S(1)} %maximum_maximum_fusion.1.w2) | copy-start | bytes 393220
  145.4 23.2 %copy-start.15 = (bf16[256,256]{1,0:T(8,128)(2,1)}, bf16[256,256]{1,0:T(8,128)(2,1)S(1)}, u32[]{:S(2)}) copy-start(bf16[256,256]{1,0:T(8,128)(2,1)S(1)} %maximum_maximum_fusion.w1) | copy-start | bytes 393220
  145.9 26.0 %copy-start.138 = (f32[12,128]{1,0:T(8,128)S(1)}, f32[12,128]{1,0:T(8,128)}, u32[]{:S(2)}) copy-start(f32[12,128]{1,0:T(8,128)} %get-tuple-element.157) | copy-start | bytes 18436
  145.9 26.1 %copy-start.137 = (f32[12,128]{1,0:T(8,128)S(1)}, f32[12,128]{1,0:T(8,128)}, u32[]{:S(2)}) copy-start(f32[12,128]{1,0:T(8,128)} %get-tuple-element.156) | copy-start | bytes 18436
  170.3 10.6 %copy-start.158 = (f32[128]{0:T(128)}, f32[128]{0:T(128)S(1)}, u32[]{:S(2)}) copy-start(f32[128]{0:T(128)S(1)} %broadcast_multiply_fusion.6) | copy-start | bytes 1540
  171.0 9.8 %copy-start.170 = (f32[128]{0:T(128)}, f32[128]{0:T(128)S(1)}, u32[]{:S(2)}) copy-start(f32[128]{0:T(128)S(1)} %fusion.91) | copy-start | bytes 1540
  171.8 9.1 %copy-start.132 = (f32[768]{0:T(1024)}, f32[768]{0:T(1024)S(1)}, u32[]{:S(2)}) copy-start(f32[768]{0:T(1024)S(1)} %get-tuple-element.216) | copy-start | bytes 9220
  171.8 36.0 %copy-start.116 = (f32[768]{0:T(1024)}, f32[768]{0:T(1024)S(1)}, u32[]{:S(2)}) copy-start(f32[768]{0:T(1024)S(1)} %get-tuple-element.220) | copy-start | bytes 9220
  171.8 36.0 %copy-start.129 = (f32[768]{0:T(1024)}, f32[768]{0:T(1024)S(1)}, u32[]{:S(2)}) copy-start(f32[768]{0:T(1024)S(1)} %get-tuple-element.219) | copy-start | bytes 9220
  171.8 44.8 %copy-start.130 = (f32[768]{0:T(1024)}, f32[768]{0:T(1024)S(1)}, u32[]{:S(2)}) copy-start(f32[768]{0:T(1024)S(1)} %get-tuple-element.195) | copy-start | bytes 9220
  171.8 48.6 %copy-start.120 = (f32[768]{0:T(1024)}, f32[768]{0:T(1024)S(1)}, u32[]{:S(2)}) copy-start(f32[768]{0:T(1024)S(1)} %get-tuple-element.193) | copy-start | bytes 9220
  171.9 48.6 %copy-start.127 = (f32[768]{0:T(1024)}, f32[768]{0:T(1024)S(1)}, u32[]{:S(2)}) copy-start(f32[768]{0:T(1024)S(1)} %get-tuple-element.194) | copy-start | bytes 9220
  172.1 9.7 %copy-start.66 = (f32[2,128]{1,0:T(2,128)}, f32[2,128]{1,0:T(2,128)S(1)}, u32[]{:S(2)}) copy-start(f32[2,128]{1,0:T(2,128)S(1)} %pad.47) | copy-start | bytes 3076
  172.1 9.7 %copy-start.75 = (f32[2,128]{1,0:T(2,128)}, f32[2,128]{1,0:T(2,128)S(1)}, u32[]{:S(2)}) copy-start(f32[2,128]{1,0:T(2,128)S(1)} %pad.50) | copy-start | bytes 3076
  172.1 9.7 %copy-start.19 = (bf16[256,256]{1,0:T(8,128)(2,1)}, bf16[256,256]{1,0:T(8,128)(2,1)S(1)}, u32[]{:S(2)}) copy-start(bf16[256,256]{1,0:T(8,128)(2,1)S(1)} %maximum_maximum_fusion.3.w2) | copy-start | bytes 393220
  172.2 9.6 %copy-start.22 = (bf16[256,256]{1,0:T(8,128)(2,1)}, bf16[256,256]{1,0:T(8,128)(2,1)S(1)}, u32[]{:S(2)}) copy-start(bf16[256,256]{1,0:T(8,128)(2,1)S(1)} %maximum_maximum_fusion.2.w1) | copy-start | bytes 393220
  172.2 8.7 %slice-start.2 = ((s8[4718592]{0:T(1024)(128)(4,1)}), s8[4194304]{0:T(1024)(128)(4,1)S(1)}, s32[]{:S(2)}) async-start(s8[4718592]{0:T(1024)(128)(4,1)} %bitcast.213), calls=%async_computation.2 | async-start | bytes 8388608
  172.4 8.5 %copy-start.39 = (bf16[128,768]{1,0:T(8,128)(2,1)}, bf16[128,768]{1,0:T(8,128)(2,1)S(1)}, u32[]{:S(2)}) copy-start(bf16[128,768]{1,0:T(8,128)(2,1)S(1)} %add_convert_fusion.5.refs_4_) | copy-start | bytes 589828
  172.4 8.5 %slice-start.3 = ((s8[4718592]{0:T(1024)(128)(4,1)}), s8[524288]{0:T(1024)(128)(4,1)S(1)}, s32[]{:S(2)}) async-start(s8[4718592]{0:T(1024)(128)(4,1)} %bitcast.213), calls=%async_computation.3 | async-start | bytes 1048576
  207.6 9.0 %copy-start.156 = (f32[128]{0:T(128)}, f32[128]{0:T(128)S(1)}, u32[]{:S(2)}) copy-start(f32[128]{0:T(128)S(1)} %broadcast_multiply_fusion.5) | copy-start | bytes 1540
  207.8 8.8 %copy-start.181 = (f32[128]{0:T(128)}, f32[128]{0:T(128)S(1)}, u32[]{:S(2)}) copy-start(f32[128]{0:T(128)S(1)} %multiply_reduce_fusion.6) | copy-start | bytes 1540
  207.9 8.8 %copy-start.168 = (f32[128]{0:T(128)}, f32[128]{0:T(128)S(1)}, u32[]{:S(2)}) copy-start(f32[128]{0:T(128)S(1)} %fusion.92) | copy-start | bytes 1540
  208.0 8.6 %copy-start.41 = (bf16[128,768]{1,0:T(8,128)(2,1)}, bf16[128,768]{1,0:T(8,128)(2,1)S(1)}, u32[]{:S(2)}) copy-start(bf16[128,768]{1,0:T(8,128)(2,1)S(1)} %add_convert_fusion.4.refs_12_) | copy-start | bytes 589828
  223.5 23.9 %copy-start.6 = (f32[128,768]{1,0:T(8,128)}, f32[128,768]{1,0:T(8,128)S(1)}, u32[]{:S(2)}) copy-start(f32[128,768]{1,0:T(8,128)S(1)} %convolution_add_fusion.6.stream) | copy-start | bytes 1179652
  248.4 9.5 %copy-start.160 = (f32[128]{0:T(128)}, f32[128]{0:T(128)S(1)}, u32[]{:S(2)}) copy-start(f32[128]{0:T(128)S(1)} %broadcast_multiply_fusion.3) | copy-start | bytes 1540
  248.6 9.3 %copy-start.185 = (f32[128]{0:T(128)}, f32[128]{0:T(128)S(1)}, u32[]{:S(2)}) copy-start(f32[128]{0:T(128)S(1)} %multiply_reduce_fusion.4) | copy-start | bytes 1540
  248.6 9.2 %copy-start.172 = (f32[128]{0:T(128)}, f32[128]{0:T(128)S(1)}, u32[]{:S(2)}) copy-start(f32[128]{0:T(128)S(1)} %fusion.94) | copy-start | bytes 1540
  249.5 8.4 %copy-start.43 = (bf16[128,768]{1,0:T(8,128)(2,1)}, bf16[128,768]{1,0:T(8,128)(2,1)S(1)}, u32[]{:S(2)}) copy-start(bf16[128,768]{1,0:T(8,128)(2,1)S(1)} %add_convert_fusion.2.refs_5_) | copy-start | bytes 589828
  249.5 9.3 %copy-start.133 = (f32[768]{0:T(1024)S(1)}, f32[768]{0:T(1024)}, u32[]{:S(2)}) copy-start(f32[768]{0:T(1024)} %copy-done.132) | copy-start | bytes 9220
  262.1 23.8 %copy-start.10 = (f32[128,768]{1,0:T(8,128)}, f32[128,768]{1,0:T(8,128)S(1)}, u32[]{:S(2)}) copy-start(f32[128,768]{1,0:T(8,128)S(1)} %fusion.52.stream) | copy-start | bytes 1179652
  287.9 6.2 %copy-start.45 = (bf16[128,768]{1,0:T(8,128)(2,1)}, bf16[128,768]{1,0:T(8,128)(2,1)S(1)}, u32[]{:S(2)}) copy-start(bf16[128,768]{1,0:T(8,128)(2,1)S(1)} %add_convert_fusion.1.refs_13_) | copy-start | bytes 589828
  287.9 6.2 %copy-start.131 = (f32[768]{0:T(1024)S(1)}, f32[768]{0:T(1024)}, u32[]{:S(2)}) copy-start(f32[768]{0:T(1024)} %copy-done.130) | copy-start | bytes 9220
  299.3 34.6 %slice-start.4 = ((s8[4718592]{0:T(1024)(128)(4,1)}), s8[4194304]{0:T(1024)(128)(4,1)S(1)}, s32[]{:S(2)}) async-start(s8[4718592]{0:T(1024)(128)(4,1)} %bitcast.215), calls=%async_computation.4 | async-start | bytes 8388608
  303.5 30.5 %slice-start.5 = ((s8[4718592]{0:T(1024)(128)(4,1)}), s8[524288]{0:T(1024)(128)(4,1)S(1)}, s32[]{:S(2)}) async-start(s8[4718592]{0:T(1024)(128)(4,1)} %bitcast.215), calls=%async_computation.5 | async-start | bytes 1048576
  381.6 25.3 %copy-start.62 = (f32[256,256]{1,0:T(8,128)S(1)}, f32[256,256]{1,0:T(8,128)}, u32[]{:S(2)}) copy-start(f32[256,256]{1,0:T(8,128)} %copy-done.61) | copy-start | bytes 786436
  422.7 25.9 %copy-start.78 = (f32[8,256]{1,0:T(8,128)S(1)}, f32[8,256]{1,0:T(8,128)}, u32[]{:S(2)}) copy-start(f32[8,256]{1,0:T(8,128)} %copy-done.77) | copy-start | bytes 24580
  422.7 26.0 %copy-start.58 = (f32[256,256]{1,0:T(8,128)S(1)}, f32[256,256]{1,0:T(8,128)}, u32[]{:S(2)}) copy-start(f32[256,256]{1,0:T(8,128)} %copy-done.57) | copy-start | bytes 786436
  485.5 108.9 %copy-start.85 = (f32[375552]{0:T(1024)S(1)}, f32[375552]{0:T(1024)}, u32[]{:S(2)}) copy-start(f32[375552]{0:T(1024)} %param.12) | copy-start | bytes 4506628
  485.5 108.9 %copy-start.108 = (f32[375552]{0:T(1024)S(1)}, f32[375552]{0:T(1024)}, u32[]{:S(2)}) copy-start(f32[375552]{0:T(1024)} %param.13) | copy-start | bytes 4506628
  (151 other events, 381.0 us)

commit v2 on v1

--- a/solution.py
+++ b/solution.py
@@ -474,7 +474,7 @@
         back[h, 64 + 16 * g : 80 + 16 * g] = imag[16 * h : 16 * h + 16]
 
 
-def gather_units(row, me, core, sibling, back, inverse_table, bufs, sems):
+def gather_units(row, me, core, sibling, back, inverse_table, bufs, sems, settle):
     own_sum, to_sib, from_sib, ready, landed = bufs
     send_s, recv_s, send_b, recv_b, local_sem = sems
 
@@ -496,6 +496,7 @@
         return carry
 
     lax.fori_loop(0, 8, partial, 0)
+    settle()
 
     def home(chip, k):
         return remote(
@@ -543,121 +544,6 @@
         lax.fori_loop(0, 8, swapped, 0)
 
     return finish
-
-
-def filter_forward_kernel(
-    stream,
-    gain,
-    shift,
-    column_table,
-    inverse_table,
-    row_table,
-    w1,
-    b1,
-    w2,
-    b2,
-    mixed,
-    saved,
-    units,
-    mine,
-    others,
-    waves,
-    back,
-    own_sum,
-    to_sib,
-    from_sib,
-    ready,
-    landed,
-    joined,
-    *sems,
-):
-    row, me, core, sibling = place()
-    barrier = greet_chips(me, core, sibling)
-    normed, _ = normalize(stream[...])
-    split_units(normed * gain[...] + shift[...], units)
-    pl.semaphore_wait(barrier, CHIPS)
-    finish_one = spread_units(me, core, sibling, units, mine, others, sems[:5])
-    groups = to_spectrum(mine, others, column_table, row_table, waves)
-    for g in range(4):
-        saved[g] = groups[g]
-        hidden = gelu_of(dot(groups[g], w1[...]) + b1[...]).astype(bf16)
-        spec = (dot(hidden, w2[...]) + b2[...]).astype(bf16)
-        from_spectrum(g, spec, row_table, back)
-    finish_two = gather_units(
-        row, me, core, sibling, back, inverse_table,
-        (own_sum, to_sib, from_sib, ready, landed), sems[5:],
-    )
-    join_units(landed, joined)
-    mixed[...] = stream[...] + joined[...]
-    finish_one()
-    finish_two()
-
-
-def filter_backward_kernel(
-    grad,
-    stream,
-    gain,
-    saved,
-    column_table,
-    inverse_table,
-    row_table,
-    w1,
-    b1,
-    w2,
-    grad_out,
-    grad_norm,
-    grad_w1,
-    grad_w2,
-    grad_b,
-    units,
-    mine,
-    others,
-    waves,
-    back,
-    own_sum,
-    to_sib,
-    from_sib,
-    ready,
-    landed,
-    joined,
-    *sems,
-):
-    row, me, core, sibling = place()
-    barrier = greet_chips(me, core, sibling)
-    split_units(grad[...], units)
-    pl.semaphore_wait(barrier, CHIPS)
-    finish_one = spread_units(me, core, sibling, units, mine, others, sems[:5])
-    groups = to_spectrum(mine, others, column_table, row_table, waves)
-    grad_w1[...] = jnp.zeros_like(grad_w1)
-    grad_w2[...] = jnp.zeros_like(grad_w2)
-    grad_b[...] = jnp.zeros_like(grad_b)
-    for g in range(4):
-        before = dot(saved[g], w1[...]) + b1[...]
-        hidden = gelu_of(before).astype(bf16)
-        grad_hidden = dot_cols(groups[g], w2[...]).astype(bf16).astype(f32)
-        grad_before = grad_hidden * gelu_slope(before)
-        grad_before16 = grad_before.astype(bf16)
-        grad_w2[...] += dot_rows(hidden, groups[g])
-        grad_w1[...] += dot_rows(saved[g], grad_before16)
-        grad_b[0:1] += jnp.sum(grad_before, axis=0, keepdims=True)
-        grad_b[1:2] += jnp.sum(groups[g].astype(f32), axis=0, keepdims=True)
-        from_spectrum(g, dot_cols(grad_before16, w1[...]).astype(bf16), row_table, back)
-    finish_two = gather_units(
-        row, me, core, sibling, back, inverse_table,
-        (own_sum, to_sib, from_sib, ready, landed), sems[5:],
-    )
-    join_units(landed, joined)
-    values = joined[...]
-    normed, scale = normalize(stream[...])
-    grad_norm[0:1] = jnp.sum(values * normed, axis=0, keepdims=True)
-    grad_norm[1:2] = jnp.sum(values, axis=0, keepdims=True)
-    grad_norm[2:8] = jnp.zeros((6, D), f32)
-    inner = values * gain[...]
-    along = jnp.mean(inner * normed, axis=-1, keepdims=True)
-    flat = jnp.mean(inner, axis=-1, keepdims=True)
-    grad_out[...] = grad[...] + scale * (inner - flat - normed * along)
-    finish_one()
-    finish_two()
 
 
 def filter_scratch():
@@ -687,53 +573,6 @@
         dma((CHIPS,)),
         dma,
     ]
-
-
-def filter_call(kernel, outs, collective_id, name, *args):
-    spec = pl.BlockSpec(memory_space=pltpu.VMEM)
-    return pl.pallas_call(
-        kernel,
-        out_shape=outs,
-        in_specs=[spec] * len(args),
-        out_specs=[spec] * len(outs),
-        scratch_shapes=filter_scratch(),
-        compiler_params=pltpu.CompilerParams(
-            collective_id=collective_id, has_side_effects=True, vmem_limit_bytes=48 << 20
-        ),
-        name=name,
-    )(*args)
-
-
-def filter_forward(stream, gain, shift, tables, weights):
-    column, inverse, rows = tables
-    w1, b1, w2, b2 = weights
-    shape = jax.ShapeDtypeStruct
-    return filter_call(
-        filter_forward_kernel,
-        [shape((2 * UNIT, D), f32), shape((4, 256, 256), bf16)],
-        2,
-        "filter_forward",
-        stream, gain, shift, column, inverse, rows, w1, b1, w2, b2,
-    )
-
-
-def filter_backward(grad, stream, gain, saved, tables, weights):
-    column, inverse, rows = tables
-    w1, b1, w2, _ = weights
-    shape = jax.ShapeDtypeStruct
-    return filter_call(
-        filter_backward_kernel,
-        [
-            shape((2 * UNIT, D), f32),
-            shape((8, D), f32),
-            shape((256, 256), f32),
-            shape((256, 256), f32),
-            shape((8, 256), f32),
-        ],
-        3,
-        "filter_backward",
-        grad, stream, gain, saved, column, inverse, rows, w1, b1, w2,
-    )
 
 
 def transform_tables(core):
@@ -1193,6 +1032,439 @@
     )(grad, loss)
 
 
+CELLS = 2 * UNIT
+FCHUNK = 768
+FILTER_SEMS = 10
+
+
+def norm_adjoint(values, gain, grad):
+    normed, scale = normalize(values)
+    inner = grad * gain
+    along = jnp.mean(inner * normed, axis=-1, keepdims=True)
+    flat = jnp.mean(inner, axis=-1, keepdims=True)
+    return (
+        scale * (inner - flat - normed * along),
+        jnp.sum(grad * normed, axis=0, keepdims=True),
+        jnp.sum(grad, axis=0, keepdims=True),
+    )
+
+
+def forward_kernel(*refs):
+    (x0, goals, mask, weight, embed_b, norms, c1, c2, tail, head_b, column, inverse, rows,
+     w1, b1, w2, b2, embed_h, in0, out0, in1, out1, head_h) = refs[:23]
+    streams, waves_o, mixeds, normeds, befores, hiddens, lasts, tails, errors, x1, loss = refs[23:34]
+    (embed, w_in, w_out, head, flow, x_now, s_stream, s_waves, s_mixed, s_norm, s_before, s_hidden,
+     s_tail, s_error, weight_sem, out_sem, tail_sem) = refs[34:51]
+    units, mine, others, waves, back, own_sum, to_sib, from_sib, ready, landed, joined = refs[51:62]
+    sems = refs[62:]
+    row, me, core, sibling = place()
+    barrier = greet_chips(me, core, sibling)
+    loads = [
+        pltpu.make_async_copy(source, target, weight_sem.at[k])
+        for k, (source, target) in enumerate(
+            [(embed_h, embed), (in0, w_in.at[0]), (out0, w_out.at[0]), (in1, w_in.at[1]),
+             (out1, w_out.at[1]), (head_h, head)]
+        )
+    ]
+    for load in loads:
+        load.start()
+    x_now[...] = x0[...]
+    loss[...] = jnp.zeros_like(loss)
+
+    def saves(it):
+        pairs = [(s_stream, streams), (s_waves, waves_o), (s_mixed, mixeds), (s_norm, normeds),
+                 (s_before, befores), (s_hidden, hiddens)]
+        return [
+            pltpu.make_async_copy(source, target.at[it], out_sem.at[k])
+            for k, (source, target) in enumerate(pairs)
+        ]
+
+    def tail_saves(step):
+        pairs = [(flow, lasts), (s_tail, tails), (s_error, errors)]
+        return [
+            pltpu.make_async_copy(source, target.at[step], tail_sem.at[k])
+            for k, (source, target) in enumerate(pairs)
+        ]
+
+    def when_it(cond, action):
+        @pl.when(cond)
+        def _():
+            action()
+
+    def body(it, carry):
+        step, layer = it // 2, it % 2
+
+        def start_step():
+            flow[...] = dot(x_now[...], embed[...]) + embed_b[...]
+
+        when_it(it == 0, loads[0].wait)
+
+        def tail_done():
+            for save in tail_saves(0):
+                save.wait()
+
+        when_it(it == 2, tail_done)
+        when_it(layer == 0, start_step)
+
+        def saved():
+            for save in saves(it):
+                save.wait()
+
+        when_it(it > 0, saved)
+        s_stream[...] = flow[...]
+        normed, _ = normalize(flow[...])
+        split_units(normed * norms[layer, 0:1] + norms[layer, 1:2], units)
+        when_it(it == 0, lambda: pl.semaphore_wait(barrier, CHIPS))
+        finish_one = spread_units(me, core, sibling, units, mine, others, sems[:5])
+        groups = to_spectrum(mine, others, column, rows, waves)
+        for g in range(4):
+            s_waves[g] = groups[g]
+            hidden = gelu_of(dot(groups[g], w1[layer]) + b1[layer]).astype(bf16)
+            spec = (dot(hidden, w2[layer]) + b2[layer]).astype(bf16)
+            from_spectrum(g, spec, rows, back)
+        finish_two = gather_units(
+            row, me, core, sibling, back, inverse,
+            (own_sum, to_sib, from_sib, ready, landed), sems[5:], finish_one,
+        )
+        join_units(landed, joined)
+        mixed = flow[...] + joined[...]
+        s_mixed[...] = mixed
+        normed, _ = normalize(mixed)
+        s_norm[...] = (normed * norms[layer, 2:3] + norms[layer, 3:4]).astype(bf16)
+        flow[...] = mixed + c2[layer]
+
+        def first_layer():
+            loads[1].wait()
+            loads[2].wait()
+
+        def second_layer():
+            loads[3].wait()
+            loads[4].wait()
+
+        when_it(it == 0, first_layer)
+        when_it(it == 1, second_layer)
+
+        def chunk(c, carry):
+            part = pl.ds(pl.multiple_of(c * FCHUNK, FCHUNK), FCHUNK)
+            before = dot(s_norm[...], w_in[layer, :, part]) + c1[layer, :, part]
+            s_before[:, part] = before.astype(bf16)
+            hidden = gelu_of(before).astype(bf16)
+            s_hidden[:, part] = hidden
+            flow[...] += dot(hidden, w_out[layer, part, :])
+            return carry
+
+        lax.fori_loop(0, FF // FCHUNK, chunk, 0)
+        for save in saves(it):
+            save.start()
+        finish_two()
+        when_it(it == 1, loads[5].wait)
+
+        def end_step():
+            normed, _ = normalize(flow[...])
+            s_tail[...] = (normed * tail[0:1] + tail[1:2]).astype(bf16)
+            predicted = dot(s_tail[...], head[...]) + head_b[...]
+            error = predicted - goals[step].astype(f32)
+            s_error[...] = error
+            loss[...] += weight[...] * jnp.sum(error * error, axis=-1, keepdims=True)
+            x_now[...] = (predicted * mask[...]).astype(bf16)
+            for save in tail_saves(step):
+                save.start()
+
+        when_it(layer == 1, end_step)
+        when_it(it == 1, lambda: x1.__setitem__(Ellipsis, x_now[...]))
+        return carry
+
+    lax.fori_loop(0, 4, body, 0)
+    for save in saves(3):
+        save.wait()
+    for save in tail_saves(1):
+        save.wait()
+
+
+def forward_pass(*args):
+    vm, dma = pltpu.VMEM, pltpu.SemaphoreType.DMA
+    whole, anywhere = pl.BlockSpec(memory_space=vm), pl.BlockSpec(memory_space=pl.ANY)
+    shape = jax.ShapeDtypeStruct
+    return pl.pallas_call(
+        forward_kernel,
+        out_shape=[
+            shape((4, CELLS, D), f32),
+            shape((4, 4, 256, 256), bf16),
+            shape((4, CELLS, D), f32),
+            shape((4, CELLS, D), bf16),
+            shape((4, CELLS, FF), bf16),
+            shape((4, CELLS, FF), bf16),
+            shape((2, CELLS, D), f32),
+            shape((2, CELLS, D), bf16),
+            shape((2, CELLS, PIN), f32),
+            shape((CELLS, PIN), bf16),
+            shape((CELLS, 1), f32),
+        ],
+        in_specs=[whole] * 17 + [anywhere] * 6,
+        out_specs=[anywhere] * 9 + [whole] * 2,
+        scratch_shapes=[
+            vm((PIN, D), bf16),
+            vm((2, D, FF), bf16),
+            vm((2, FF, D), bf16),
+            vm((D, PIN), bf16),
+            vm((CELLS, D), f32),
+            vm((CELLS, PIN), bf16),
+            vm((CELLS, D), f32),
+            vm((4, 256, 256), bf16),
+            vm((CELLS, D), f32),
+            vm((CELLS, D), bf16),
+            vm((CELLS, FF), bf16),
+            vm((CELLS, FF), bf16),
+            vm((CELLS, D), bf16),
+            vm((CELLS, PIN), f32),
+            dma((6,)),
+            dma((6,)),
+            dma((3,)),
+        ]
+        + filter_scratch(),
+        compiler_params=pltpu.CompilerParams(
+            collective_id=2, has_side_effects=True, vmem_limit_bytes=56 << 20
+        ),
+        name="forward_pass",
+    )(*args)
+
+
+def backward_kernel(*refs):
+    (gscale, mask, norms, tail, column, inverse, rows, w1, b1, w2,
+     embed_h, in0, out0, in1, out1, head_h,
+     streams, waves_h, mixeds, befores, lasts, errors) = refs[:22]
+    (g_pred, g_out, g_pre, g_embed, sum_norm, sum_c1, sum_tail, sum_head, grad_w1, grad_w2, grad_b) = refs[22:33]
+    (embed, w_in, w_out, head, flow, carried, i_stream, i_waves, i_mixed, i_before, i_last, i_error,
+     s_pred, s_out, s_pre, s_embed, g_norm, weight_sem, in_sem, tail_in, out_sem, tail_sem) = refs[33:55]
+    units, mine, others, waves, back, own_sum, to_sib, from_sib, ready, landed, joined = refs[55:66]
+    sems = refs[66:]
+    row, me, core, sibling = place()
+    barrier = greet_chips(me, core, sibling)
+
+    def when_it(cond, action):
+        @pl.when(cond)
+        def _():
+            action()
+
+    loads = [
+        pltpu.make_async_copy(source, target, weight_sem.at[k])
+        for k, (source, target) in enumerate(
+            [(head_h, head), (out1, w_out.at[1]), (in1, w_in.at[1]), (out0, w_out.at[0]),
+             (in0, w_in.at[0]), (embed_h, embed)]
+        )
+    ]
+
+    def inst(it):
+        return 3 - it
+
+    def fetch(it):
+        slot = it % 2
+        pairs = [(streams, i_stream), (waves_h, i_waves), (mixeds, i_mixed), (befores, i_before)]
+        return [
+            pltpu.make_async_copy(source.at[inst(it)], target.at[slot], in_sem.at[k, slot])
+            for k, (source, target) in enumerate(pairs)
+        ]
+
+    tail_loads = [
+        pltpu.make_async_copy(lasts, i_last, tail_in.at[0]),
+        pltpu.make_async_copy(errors, i_error, tail_in.at[1]),
+    ]
+    for load in tail_loads:
+        load.start()
+    loads[0].start()
+    for load in fetch(0):
+        load.start()
+    for load in loads[1:]:
+        load.start()
+    for target in (sum_norm, sum_c1, sum_tail, sum_head, grad_w1, grad_w2, grad_b, carried):
+        target[...] = jnp.zeros_like(target)
+
+    def saves(it):
+        pairs = [(s_out, g_out), (s_pre, g_pre)]
+        return [
+            pltpu.make_async_copy(source, target.at[inst(it)], out_sem.at[k])
+            for k, (source, target) in enumerate(pairs)
+        ]
+
+    def pred_save(step):
+        return pltpu.make_async_copy(s_pred, g_pred.at[step], tail_sem.at[0])
+
+    def embed_save(step):
+        return pltpu.make_async_copy(s_embed, g_embed.at[step], tail_sem.at[1])
+
+    def body(it, carry):
+        step, layer, slot = 1 - it // 2, 1 - it % 2, it % 2
+
+        def first():
+            for load in tail_loads:
+                load.wait()
+            loads[0].wait()
+
+        when_it(it == 0, first)
+        when_it(it == 2, lambda: pred_save(1).wait())
+
+        def head_adjoint():
+            grad = i_error[step] * gscale[...] + carried[...]
+            grad16 = grad.astype(bf16)
+            s_pred[...] = grad16
+            pred_save(step).start()
+            sum_head[0:1] += jnp.sum(grad, axis=0, keepdims=True)
+            back_n = dot_cols(grad16, head[...]).astype(bf16).astype(f32)
+            value, gain, shift = norm_adjoint(i_last[step], tail[0:1], back_n)
+            flow[...] = value
+            sum_tail[0:1] += gain
+            sum_tail[1:2] += shift
+
+        when_it(layer == 1, head_adjoint)
+
+        def prefetch():
+            for load in fetch(it + 1):
+                load.start()
+
+        when_it(it < 3, prefetch)
+
+        def saved():
+            for save in saves(it):
+                save.wait()
+
+        when_it(it > 0, saved)
+        s_out[...] = flow[...].astype(bf16)
+        sum_norm[layer, 4:5] += jnp.sum(flow[...], axis=0, keepdims=True)
+        for load in fetch(it):
+            load.wait()
+
+        def second_layer():
+            loads[1].wait()
+            loads[2].wait()
+
+        def first_layer():
+            loads[3].wait()
+            loads[4].wait()
+
+        when_it(it == 0, second_layer)
+        when_it(it == 1, first_layer)
+        g_norm[...] = jnp.zeros_like(g_norm)
+
+        def chunk(c, carry):
+            part = pl.ds(pl.multiple_of(c * FCHUNK, FCHUNK), FCHUNK)
+            grad = dot_cols(s_out[...], w_out[layer, part, :]).astype(bf16).astype(f32)
+            grad = grad * gelu_slope(i_before[slot, :, part].astype(f32))
+            sum_c1[layer, 0:1, part] += jnp.sum(grad, axis=0, keepdims=True)
+            grad16 = grad.astype(bf16)
+            s_pre[:, part] = grad16
+            g_norm[...] += dot_cols(grad16, w_in[layer, :, part])
+            return carry
+
+        lax.fori_loop(0, FF // FCHUNK, chunk, 0)
+        for save in saves(it):
+            save.start()
+        value, gain, shift = norm_adjoint(
+            i_mixed[slot], norms[layer, 2:3], g_norm[...].astype(bf16).astype(f32)
+        )
+        flow[...] += value
+        sum_norm[layer, 2:3] += gain
+        sum_norm[layer, 3:4] += shift
+        split_units(flow[...], units)
+        when_it(it == 0, lambda: pl.semaphore_wait(barrier, CHIPS))
+        finish_one = spread_units(me, core, sibling, units, mine, others, sems[:5])
+        groups = to_spectrum(mine, others, column, rows, waves)
+        for g in range(4):
+            before = dot(i_waves[slot, g], w1[layer]) + b1[layer]
+            hidden = gelu_of(before).astype(bf16)
+            grad_hidden = dot_cols(groups[g], w2[layer]).astype(bf16).astype(f32)
+            grad_before = grad_hidden * gelu_slope(before)
+            grad_before16 = grad_before.astype(bf16)
+            grad_w2[layer] += dot_rows(hidden, groups[g])
+            grad_w1[layer] += dot_rows(i_waves[slot, g], grad_before16)
+            grad_b[layer, 0:1] += jnp.sum(grad_before, axis=0, keepdims=True)
+            grad_b[layer, 1:2] += jnp.sum(groups[g].astype(f32), axis=0, keepdims=True)
+            from_spectrum(g, dot_cols(grad_before16, w1[layer]).astype(bf16), rows, back)
+        finish_two = gather_units(
+            row, me, core, sibling, back, inverse,
+            (own_sum, to_sib, from_sib, ready, landed), sems[5:], finish_one,
+        )
+        join_units(landed, joined)
+        value, gain, shift = norm_adjoint(i_stream[slot], norms[layer, 0:1], joined[...])
+        flow[...] += value
+        sum_norm[layer, 0:1] += gain
+        sum_norm[layer, 1:2] += shift
+        when_it(it == 1, loads[5].wait)
+        when_it(it == 3, lambda: embed_save(1).wait())
+
+        def embed_adjoint():
+            s_embed[...] = flow[...].astype(bf16)
+            sum_tail[2:3] += jnp.sum(flow[...], axis=0, keepdims=True)
+            embed_save(step).start()
+
+        when_it(layer == 0, embed_adjoint)
+
+        def carry_back():
+            carried[...] = mask[...] * dot_cols(s_embed[...], embed[...]).astype(bf16).astype(f32)
+
+        when_it(it == 1, carry_back)
+        finish_two()
+        return carry
+
+    lax.fori_loop(0, 4, body, 0)
+    for save in saves(3):
+        save.wait()
+    pred_save(0).wait()
+    embed_save(0).wait()
+
+
+def backward_pass(*args):
+    vm, dma = pltpu.VMEM, pltpu.SemaphoreType.DMA
+    whole, anywhere = pl.BlockSpec(memory_space=vm), pl.BlockSpec(memory_space=pl.ANY)
+    shape = jax.ShapeDtypeStruct
+    return pl.pallas_call(
+        backward_kernel,
+        out_shape=[
+            shape((2, CELLS, PIN), bf16),
+            shape((4, CELLS, D), bf16),
+            shape((4, CELLS, FF), bf16),
+            shape((2, CELLS, D), bf16),
+            shape((2, 8, D), f32),
+            shape((2, 8, FF), f32),
+            shape((8, D), f32),
+            shape((8, PIN), f32),
+            shape((2, 256, 256), f32),
+            shape((2, 256, 256), f32),
+            shape((2, 8, 256), f32),
+        ],
+        in_specs=[whole] * 10 + [anywhere] * 12,
+        out_specs=[anywhere] * 4 + [whole] * 7,
+        scratch_shapes=[
+            vm((PIN, D), bf16),
+            vm((2, D, FF), bf16),
+            vm((2, FF, D), bf16),
+            vm((D, PIN), bf16),
+            vm((CELLS, D), f32),
+            vm((CELLS, PIN), f32),
+            vm((2, CELLS, D), f32),
+            vm((2, 4, 256, 256), bf16),
+            vm((2, CELLS, D), f32),
+            vm((2, CELLS, FF), bf16),
+            vm((2, CELLS, D), f32),
+            vm((2, CELLS, PIN), f32),
+            vm((CELLS, PIN), bf16),
+            vm((CELLS, D), bf16),
+            vm((CELLS, FF), bf16),
+            vm((CELLS, D), bf16),
+            vm((CELLS, D), f32),
+            dma((6,)),
+            dma((4, 2)),
+            dma((2,)),
+            dma((2,)),
+            dma((2,)),
+        ]
+        + filter_scratch(),
+        compiler_params=pltpu.CompilerParams(
+            collective_id=3, has_side_effects=True, vmem_limit_bytes=56 << 20
+        ),
+        name="backward_pass",
+    )(*args)
+
+
 MATS = [(PIN, D), (D, FF), (FF, D), (D, FF), (FF, D), (D, PIN)]
 SMALL_LAYER = 2352
 SMALLS = [6 + SMALL_LAYER, 24, 6 + SMALL_LAYER, 24, 18, 10]
@@ -1429,7 +1701,7 @@
     flat_mask = cell_masks.reshape(128, 1)
     flat_weight = weighted.reshape(128, 1)
     inputs = (frames.reshape(128, PIN).astype(f32) * flat_mask).astype(bf16)
-    goals = [targets[:, s].reshape(128, PIN).astype(f32) for s in range(STEPS)]
+    goals = jnp.stack([targets[:, s].reshape(128, PIN) for s in range(STEPS)])
     spectral_weights = []
     for small, *_ in layers:
         found = []
@@ -1438,72 +1710,26 @@
             b = lax.dynamic_index_in_dim(small[j + 1], block, 1, False)
             found += [spread_weight(w[0], w[1]).astype(bf16), spread_bias(b)]
         spectral_weights.append(found)
-
-    def lin(values, weight16, bias_vec):
-        return mult("ci,io->co", values, weight16) + bias_vec
-
-    loss_cells = jnp.zeros((128,), f32)
-    history = []
-    for roll_step in range(STEPS):
-        stream = lin(inputs, embed, embed_bias)
-        saved = []
-        for (small, w_in, c1, w_out, c2), spectral_w in zip(layers, spectral_weights):
-            mixed, waves = filter_forward(
-                stream, small[0][None], small[1][None], tables, spectral_w
-            )
-            normed = layer_norm(mixed, small[6], small[7]).astype(bf16)
-            before = lin(normed, w_in, c1)
-            hidden = jax.nn.gelu(before, approximate=False).astype(bf16)
-            saved.append((stream, waves, mixed, normed, before, hidden))
-            stream = mixed + lin(hidden, w_out, c2)
-        normed = layer_norm(stream, gain3, shift3).astype(bf16)
-        predicted = lin(normed, head, head_bias)
-        errors = predicted - goals[roll_step]
-        loss_cells = loss_cells + flat_weight[:, 0] * jnp.sum(errors * errors, axis=-1)
-        history.append((inputs, saved, stream, normed, errors))
-        inputs = (predicted * flat_mask).astype(bf16)
-    carried = jnp.zeros((128, PIN), f32)
-    pairs = [[None] * 4 for _ in range(6)]
-    parts = []
-
-    def keep(i, step, values, grad):
-        pairs[i][step] = values.astype(bf16)
-        pairs[i][2 + step] = grad.astype(bf16)
-
-    for roll_step in reversed(range(STEPS)):
-        inputs, saved, stream, normed, errors = history[roll_step]
-        grad_pred = 2.0 * flat_weight * errors / total_weight + carried
-        keep(5, roll_step, normed, grad_pred)
-        _, pullback = jax.vjp(layer_norm, stream, gain3, shift3)
-        grad_stream, grad_gain3, grad_shift3 = pullback(
-            rounded(mult("co,io->ci", grad_pred, head))
-        )
-        found = {"hb": jnp.sum(grad_pred, axis=0), "g3": grad_gain3, "s3": grad_shift3}
-        for idx in reversed(range(LAYERS)):
-            small, w_in, c1, w_out, c2 = layers[idx]
-            stream, waves, mixed, normed, before, hidden = saved[idx]
-            keep(2 + 2 * idx, roll_step, hidden, grad_stream)
-            grad_hidden = mult("co,io->ci", grad_stream, w_out)
-            _, pullback = jax.vjp(lambda value: jax.nn.gelu(value, approximate=False), before)
-            (grad_before,) = pullback(rounded(grad_hidden))
-            keep(1 + 2 * idx, roll_step, normed, grad_before)
-            _, pullback = jax.vjp(layer_norm, mixed, small[6], small[7])
-            grad_extra, grad_gain2, grad_shift2 = pullback(
-                rounded(mult("co,io->ci", grad_before, w_in))
-            )
-            found[f"c2{idx}"] = jnp.sum(grad_stream, axis=0)
-            found[f"c1{idx}"] = jnp.sum(grad_before, axis=0)
-            grad_stream, norm_grads, gw1, gw2, gb = filter_backward(
-                grad_stream + grad_extra, stream, small[0][None], waves, tables,
-                spectral_weights[idx],
-            )
-            found[f"layer{idx}"] = (norm_grads, gw1, gw2, gb, grad_gain2, grad_shift2)
-        keep(0, roll_step, inputs, grad_stream)
-        found["eb"] = jnp.sum(grad_stream, axis=0)
-        parts.append(found)
-        if roll_step:
-            carried = flat_mask * rounded(mult("co,io->ci", grad_stream, embed))
-    sums = jax.tree.map(jnp.add, parts[0], parts[1])
+    w1, b1, w2, b2 = (jnp.stack(both) for both in zip(*spectral_weights))
+    norms = jnp.stack([jnp.stack([small[k] for k in (0, 1, 6, 7)]) for small, *_ in layers])
+    tail = jnp.stack([gain3, shift3])
+    mats = (embed, in0, out0, in1, out1, head)
+    streams, waves, mixeds, normeds, befores, hiddens, lasts, tails, errors, x1, loss = forward_pass(
+        inputs, goals, flat_mask, flat_weight, embed_bias[None], norms,
+        jnp.stack([c1_0, c1_1])[:, None], jnp.stack([c2_0, c2_1])[:, None], tail, head_bias[None],
+        *tables, w1, b1, w2, b2, *mats,
+    )
+    (g_pred, g_out, g_pre, g_embed, sum_norm, sum_c1, sum_tail, sum_head, grad_w1, grad_w2, grad_b) = (
+        backward_pass(
+            flat_weight * (2.0 / total_weight), flat_mask, norms, tail, *tables, w1, b1, w2, *mats,
+            streams, waves, mixeds, befores, lasts, errors,
+        )
+    )
+    pairs = [[inputs, x1, g_embed[0], g_embed[1]]]
+    for idx in range(LAYERS):
+        pairs.append([normeds[idx], normeds[2 + idx], g_pre[idx], g_pre[2 + idx]])
+        pairs.append([hiddens[idx], hiddens[2 + idx], g_out[idx], g_out[2 + idx]])
+    pairs.append([tails[0], tails[1], g_pred[0], g_pred[1]])
 
     def as_rows(value):
         return value.reshape(-1, LANES)
@@ -1514,28 +1740,28 @@
         return as_rows(lax.dynamic_update_slice_in_dim(whole, local_grad, block, 1))
 
     def layer_rows(idx):
-        norm_grads, gw1, gw2, gb, gain2, shift2 = sums[f"layer{idx}"]
+        gb = grad_b[idx]
         return [
-            as_rows(norm_grads[0]),
-            as_rows(norm_grads[1]),
-            placed(fold_weight(gw1)),
+            as_rows(sum_norm[idx, 0]),
+            as_rows(sum_norm[idx, 1]),
+            placed(fold_weight(grad_w1[idx])),
             placed(fold_bias(gb[0])),
-            placed(fold_weight(gw2)),
+            placed(fold_weight(grad_w2[idx])),
             placed(fold_bias(gb[1])),
-            as_rows(gain2),
-            as_rows(shift2),
+            as_rows(sum_norm[idx, 2]),
+            as_rows(sum_norm[idx, 3]),
         ]
 
     small_grads = [
-        [as_rows(sums["eb"])] + layer_rows(0),
-        [as_rows(sums["c10"])],
-        [as_rows(sums["c20"])] + layer_rows(1),
-        [as_rows(sums["c11"])],
-        [as_rows(sums[k]) for k in ("c21", "g3", "s3")],
-        [as_rows(sums["hb"])],
+        [as_rows(sum_tail[2])] + layer_rows(0),
+        [as_rows(sum_c1[0, 0])],
+        [as_rows(sum_norm[0, 4])] + layer_rows(1),
+        [as_rows(sum_c1[1, 0])],
+        [as_rows(v) for v in (sum_norm[1, 4], sum_tail[0], sum_tail[1])],
+        [as_rows(sum_head[0])],
     ]
     flat_grad = pack_flat(pairs, small_grads)
-    loss_tile = jnp.concatenate([loss_cells[None], jnp.zeros((7, LANES), f32)])
+    loss_tile = jnp.concatenate([loss.reshape(1, LANES), jnp.zeros((7, LANES), f32)])
     summed, stats = rs(flat_grad, loss_tile)
     reduced = lax.dynamic_slice_in_dim(summed, (device * OWN) % 16, OWN, 0).reshape(-1)
     grad_norm = jnp.sqrt(jnp.sum(stats[:8]))

time: 607 us -> 553 us (0.911)
  matrix products: 69 us -> 0 us
  Pallas kernels: 455 us -> 481 us
  other arithmetic: 32.5 us -> 18.7 us
    dot_general x23 -> x0, matrix products: 69 us -> none  [mult(): jnp.einsum(form, left.astype(jnp.bfloat16), right.astype(jnp.bfloat16), p...]
    pallas_call x8 -> x2, Pallas kernels: 195 us -> 221 us  [the longest x1 118 us: backward_pass(): pl.pallas_call(backward_kernel, out_shape=[shape((2, CELLS, PIN), bf16),...]
    reduce_sum x33 -> x0, other arithmetic: 17 us -> none  [the longest x10 6.58 us: layer_norm(): return center * lax.rsqrt(spread + NORM_EPS) * gain_vec + shift_vec]
    unnamed x398 -> x53, local copies, waits for them, and re-layouts: 12.5 us -> 2.94 us
    squeeze x0 -> x9, local copies, waits for them, and re-layouts: none -> 7.06 us  [the longest x2 2.51 us: local_fast(): pairs.append([hiddens[idx], hiddens[2 + idx], g_out[idx], g_out[2 + idx]])]
where the time goes in v2:
time: 553 us; the launch traced here: 548 us
  Pallas kernels  481 us (87%)
  local copies, waits for them, and re-layouts  41.4 us (7%)
  other arithmetic  18.7 us (3%)
  between operations  5.63 us (1%)
    pallas_call x1, Pallas kernels, backward_pass(): pl.pallas_call(backward_kernel, out_shape=[shape((2, CELLS, PIN), bf16),...  118 us
    pallas_call x1, Pallas kernels, rs(): pl.pallas_call(sum_kernel, out_shape=[shape((CHR, 128), f32), shape((16,...  106 us
    pallas_call x1, Pallas kernels, forward_pass(): pl.pallas_call(forward_kernel, out_shape=[shape((4, CELLS, D), f32), shap...  103 us
    pallas_call x1, Pallas kernels, ag(): pl.pallas_call(gather_kernel, out_shape=jax.ShapeDtypeStruct((32 * CH, 12...  96.1 us
    pallas_call x1, Pallas kernels, pack_flat(): pl.pallas_call(functools.partial(pack_kernel, [len(some) for some in smal...  29.8 us
    pallas_call x1, Pallas kernels, unpack_flat(): pl.pallas_call(unpack_kernel, out_shape=[shape(m, bf16) for m in MATS] +...  27.3 us
  transfers between devices with their start and end apart: 1, of which 0 were waited for; matrix products, arithmetic and copies ran while one was open for 1% of the time, Pallas kernels for 0%

profile of v2, /device:TPU:0, one launch (start us, length us, event | category | flops | bytes accessed | tf_op | source)
XLA Modules:
  0.0 547.8 jit_solution(16698763038626201420)
XLA Ops:
  0.6 1.6 convert_element_type.103
  2.3 1.4 collective-permute-start
  4.5 0.7 reshape.663.refs_2_.refs_1_
  5.7 0.7 select_reduce_fusion
  7.1 0.9 fusion.3.refs_0_
  8.0 0.9 pad_maximum_fusion.refs_1_
  8.9 0.6 broadcast_multiply_fusion.refs_0_
  9.5 0.6 dynamic-slice_bitcast_fusion
  10.1 2.7 fusion.2.shard
  12.8 96.1 %gather_weights.1.flat = bf16[94208,128]{1,0:T(8,128)(2,1)} custom-call(bf16[2944,128]{1,0:T(8,128)(2,1)} %fusion.2.shard), custom_call_target="tpu_custom_call" | custom-call | tf_op jit(solution)/shard_map/gather_weights/pallas_call | solution.py:760
  108.9 27.3 %unpack_flat.1 = (bf16[1280,768]{1,0:T(8,128)(2,1)S(1)}, bf16[768,3072]{1,0:T(8,128)(2,1)}, bf16[3072,768]{1,0:T(8,128)(2,1)}, bf16[768,3072]{1,0:T(8,128)(2,1)}...) custom-call(bf16[94208,128]{1,0:T(8,128)(2,1)} %gather_weights.1.flat), custom_call_target="tpu_custom_call" | custom-call | tf_op jit(solution)/shard_map/unpack_flat/pallas_call | solution.py:1545
  136.2 1.5 fusion.17
  138.1 0.8 constant_dynamic-slice_fusion.1
  138.8 0.8 constant_dynamic-slice_fusion.6
  139.7 0.8 constant_dynamic-slice_fusion.3
  140.5 0.8 constant_dynamic-slice_fusion.11
  143.1 0.6 broadcast_in_dim.4.refs_6_
  146.1 0.6 pad_maximum_fusion.5.refs_5_.refs_2_
  147.4 0.7 maximum_maximum_fusion.1.refs_15_.refs_9_
  148.2 0.7 maximum_maximum_fusion.refs_13_.refs_7_
  148.9 102.9 %forward_pass.1 = (f32[4,128,768]{2,1,0:T(8,128)}, bf16[4,4,256,256]{3,2,1,0:T(8,128)(2,1)}, f32[4,128,768]{2,1,0:T(8,128)}, bf16[4,128,768]{2,1,0:T(8,128)(2,1)...) custom-call(bf16[128,1280]{1,0:T(8,128)(2,1)} %fusion.3.refs_0_, ...), custom_call_target="tpu_custom_call" | custom-call | tf_op jit(solution)/shard_map/forward_pass/pallas_call | solution.py:1188
  251.8 118.4 %backward_pass.1 = (bf16[2,128,1280]{2,1,0:T(8,128)(2,1)}, bf16[4,128,768]{2,1,0:T(8,128)(2,1)}, bf16[4,128,3072]{2,1,0:T(8,128)(2,1)}, bf16[2,128,768]{2,1,0:T(...) custom-call(f32[128,1]{1,0:T(8,128)} %broadcast_multiply_fusion.refs, ...), custom_call_target="tpu_custom_call" | custom-call | tf_op jit(solution)/shard_map/backward_pass/pallas_call | solution.py:1419
  370.2 0.8 slice_bitcast_fusion.42
  371.1 1.1 slice_bitcast_fusion.10
  372.6 1.3 dynamic_update_slice.30
  373.9 0.9 reshape.656.refs_39_
  375.3 1.3 dynamic_update_slice.28
  376.6 1.0 reshape.653.refs_37_
  378.0 0.9 broadcast.334.clone.1
  378.9 3.3 dynamic_update_slice.26
  382.2 2.1 reshape.650.refs_29_
  385.0 0.9 broadcast.334.clone
  385.9 3.3 dynamic_update_slice.24
  389.2 2.0 reshape.647.refs_27_
  391.2 1.7 slice_bitcast_fusion.2
  392.9 0.7 slice_bitcast_fusion.16
  394.1 0.9 slice_bitcast_fusion.8
  395.1 1.0 fusion.20
  396.0 0.9 slice_reduce_fusion.3
  396.9 0.8 slice_reduce_fusion
  397.7 1.8 slice_bitcast_fusion
  399.6 0.9 copy-done.12
  400.5 0.8 slice_bitcast_fusion.14
  401.4 0.6 concatenate.123.loss
  402.0 29.8 %pack_flat.1.grad = bf16[93904,128]{1,0:T(8,128)(2,1)} custom-call(bf16[128,1280]{1,0:T(8,128)(2,1)} %fusion.3.refs_0_, bf16[128,1280]{1,0:T(8,128)(2,1)} %get-tuple-element.55.refs_1_, bf16[128,768]{1,0:T(8,128)(2,1)S(1)} %get-tuple-element.147.refs_2_, bf16[128,768]{1,0:T(8,128)(2,1)S(1)} %get-tuple-element.146.refs_3_, ...), custom_call_target="tpu_custom_call" | custom-call | tf_op jit(solution)/shard_map/pack_flat/pallas_call | solution.py:1639
  431.8 106.2 %sum_gradients.1 = (f32[2960,128]{1,0:T(8,128)}, f32[16,128]{1,0:T(8,128)}) custom-call(bf16[93904,128]{1,0:T(8,128)(2,1)} %pack_flat.1.grad, f32[8,128]{1,0:T(8,128)} %concatenate.123.loss), custom_call_target="tpu_custom_call" | custom-call | tf_op jit(solution)/shard_map/sum_gradients/pallas_call | solution.py:998
  538.0 1.3 slice_reduce_fusion.1
  540.1 5.0 fusion.12
  (160 shorter events, 9.1 us)
Async XLA Ops:
  0.6 3.1 copy-start.1
  2.2 1.7 copy-start.17
  2.2 3.4 copy-start.8
  2.3 7.9 %collective-permute-start = (bf16[320,128]{1,0:T(8,128)(2,1)S(1)}, bf16[320,128]{1,0:T(8,128)(2,1)S(1)}, u32[]{:S(2)}, u32[]{:S(2)}) collective-permute-start(bf16[320,128]{1,0:T(8,128)(2,1)S(1)} %slice_bitcast_fusion.26), channel_id=1, source_target_pairs={{1,0},{2,1},{3,2},{4,3},{5,4},{6,5},{7,6},{8,7},{9,8},{10,9},{11,1... | collective-permute-start | bytes 245768 | tf_op jit(solution)/shard_map/ppermute | solution.py:1675
  3.7 3.4 copy-start.14
  5.6 3.2 copy-start.10
  5.6 3.9 copy-start.18
  5.6 3.8 copy-start.19
  136.2 1.7 copy-start
  372.2 2.7 copy-start.11
  382.2 9.0 %copy-start.4 = (bf16[4,128,3072]{2,1,0:T(8,128)(2,1)S(1)}, bf16[4,128,3072]{2,1,0:T(8,128)(2,1)}, u32[]{:S(2)}) copy-start(bf16[4,128,3072]{2,1,0:T(8,128)(2,1)} %get-tuple-element.64) | copy-start | bytes 9437188
  391.2 1.7 copy-start.7
  391.2 3.8 copy-start.13
  391.2 3.8 copy-start.16
  392.9 1.2 copy-start.9
  392.9 4.8 copy-start.3
  397.7 1.8 copy-start.6
  399.5 1.0 copy-start.12
  399.5 1.8 copy-start.15
  431.8 108.3 %copy-start.2 = (f32[375552]{0:T(1024)S(1)}, f32[375552]{0:T(1024)}, u32[]{:S(2)}) copy-start(f32[375552]{0:T(1024)} %param.12) | copy-start | bytes 4506628
  431.8 108.2 %copy-start.5 = (f32[375552]{0:T(1024)S(1)}, f32[375552]{0:T(1024)}, u32[]{:S(2)}) copy-start(f32[375552]{0:T(1024)} %param.13) | copy-start | bytes 4506628

commit v3 on v2

--- a/solution.py
+++ b/solution.py
@@ -386,7 +386,7 @@
     return lax.dot_general(left, right, (((1,), (1,)), ((), ())), preferred_element_type=f32)
 
 
-def spread_units(me, core, sibling, units, mine, others, sems):
+def spread_units(me, core, sibling, units, mine, others, sems, meanwhile):
     send_a, recv_a, send_f, recv_f, local_sem = sems
 
     def out(k):
@@ -407,6 +407,7 @@
         return carry
 
     lax.fori_loop(1, CHIPS, begin, 0)
+    meanwhile()
     own.wait()
     handed(0).start()
 
@@ -474,7 +475,7 @@
         back[h, 64 + 16 * g : 80 + 16 * g] = imag[16 * h : 16 * h + 16]
 
 
-def gather_units(row, me, core, sibling, back, inverse_table, bufs, sems, settle):
+def gather_units(row, me, core, sibling, back, inverse_table, bufs, sems, settle, meanwhile):
     own_sum, to_sib, from_sib, ready, landed = bufs
     send_s, recv_s, send_b, recv_b, local_sem = sems
 
@@ -522,6 +523,7 @@
 
     lax.fori_loop(0, 8, total, 0)
     own.start()
+    meanwhile()
 
     def landed_all(k, carry):
         home(lax.rem(me + k, CHIPS), k).wait_recv()
@@ -597,31 +599,6 @@
     ) / np.sqrt(height)
     pick = lambda both: lax.dynamic_index_in_dim(jnp.asarray(np.stack(both), bf16), core, 0, False)
     return pick(column), pick(inverse), jnp.asarray(rows, bf16)
-
-
-def spread_weight(re, im):
-    def at(block, top, left):
-        return jnp.pad(block, ((top, PADC - BS), (left, PADC - BS)))
-
-    pad = lambda m: jnp.pad(m, ((0, PADC - BS), (0, PADC - BS)))
-    re, im = pad(re), pad(im)
-    return jnp.concatenate(
-        [jnp.concatenate([re, im], axis=1), jnp.concatenate([-im, re], axis=1)], axis=0
-    )
-
-
-def spread_bias(bias):
-    return jnp.pad(bias, ((0, 0), (0, PADC - BS))).reshape(1, 2 * PADC)
-
-
-def fold_weight(grad):
-    a, b = grad[:BS, :BS], grad[PADC : PADC + BS, PADC : PADC + BS]
-    c, d = grad[:BS, PADC : PADC + BS], grad[PADC : PADC + BS, :BS]
-    return jnp.stack([a + b, c - d])
-
-
-def fold_bias(grad):
-    return jnp.stack([grad[:BS], grad[PADC : PADC + BS]])
 
 
 RING = 8
@@ -1032,6 +1009,195 @@
     )(grad, loss)
 
 
+MATS = [(PIN, D), (D, FF), (FF, D), (D, FF), (FF, D), (D, PIN)]
+SMALL_LAYER = 2352
+SMALLS = [6 + SMALL_LAYER, 24, 6 + SMALL_LAYER, 24, 18, 10]
+PIECE = 256
+
+
+def flat_sections():
+    at = 0
+    found = []
+    for (depth, cols), small in zip(MATS, SMALLS):
+        per_row = cols // LANES
+        found.append((at, depth, per_row, at + depth * per_row, small))
+        at += depth * per_row + small
+    return found
+
+
+def piece_rows(depth, per_row):
+    rows = depth
+    while rows * per_row > 7680:
+        rows -= PIECE
+        while depth % rows:
+            rows -= PIECE
+    return rows
+
+
+def put_rows(wide, at, value):
+    for k in range(value.shape[1] // LANES):
+        wide[at + k : at + k + 1] = value[:, k * LANES : (k + 1) * LANES]
+
+
+def put_block_weight(wide, at, block, grad, square):
+    wide[at : at + 2 * NBLK * BLOCK_ROWS] = jnp.zeros((2 * NBLK * BLOCK_ROWS, LANES), f32)
+    square[0] = grad[:PADC, :PADC] + grad[PADC:, PADC:]
+    square[1] = grad[:PADC, PADC:] - grad[PADC:, :PADC]
+    for part in range(2):
+        a, b, c, d = (square[part, pl.ds(q, 24, stride=4), :] for q in range(4))
+        rows = (
+            jnp.concatenate([a[:, :96], b[:, :32]], axis=1),
+            jnp.concatenate([b[:, 32:96], c[:, :64]], axis=1),
+            jnp.concatenate([c[:, 64:96], d[:, :96]], axis=1),
+        )
+        for q, value in enumerate(rows):
+            wide[pl.ds(at + (part * NBLK + block) * BLOCK_ROWS + q, 24, stride=3), :] = value
+
+
+def put_block_bias(wide, at, block, grad):
+    found = []
+    for part in range(2):
+        piece = grad[:, part * PADC : part * PADC + BS]
+        found += [jnp.where(block == k, piece, 0.0) for k in range(NBLK)]
+    put_rows(wide, at, jnp.concatenate(found, axis=1))
+
+
+def pack_kernel(*refs):
+    sources, refs = refs[:9], refs[9:]
+    sum_norm, sum_c1, sum_tail, sum_head, grad_w1, grad_w2, grad_b = refs[:7]
+    flat = refs[7]
+    held, refs = refs[8:17], refs[17:]
+    across, side, wide, narrow, square, sem, in_sem = refs
+    inputs, x1, normeds, hiddens, tails, g_embed, g_pre, g_out, g_pred = held
+    _, me, _, _ = place()
+    block = me % NBLK
+    loads = [
+        pltpu.make_async_copy(source, target, in_sem.at[k])
+        for k, (source, target) in enumerate(zip(sources, held))
+    ]
+    order = (0, 1, 5, 2, 6, 3, 7, 4, 8)
+    for k in order:
+        loads[k].start()
+    needs = ((0, 1, 5), (2, 6), (3, 7), (), (), (4, 8))
+    pairs = [(inputs, x1, g_embed.at[0], g_embed.at[1])]
+    for idx in range(LAYERS):
+        pairs.append((normeds.at[idx], normeds.at[2 + idx], g_pre.at[idx], g_pre.at[2 + idx]))
+        pairs.append((hiddens.at[idx], hiddens.at[2 + idx], g_out.at[idx], g_out.at[2 + idx]))
+    pairs.append((tails.at[0], tails.at[1], g_pred.at[0], g_pred.at[1]))
+
+    def put_layer(at, idx):
+        put_rows(wide, at, sum_norm[idx, 0:1])
+        put_rows(wide, at + 6, sum_norm[idx, 1:2])
+        put_block_weight(wide, at + AT_W1, block, grad_w1[idx], square)
+        put_block_bias(wide, at + AT_B1, block, grad_b[idx, 0:1])
+        put_block_weight(wide, at + AT_W2, block, grad_w2[idx], square)
+        put_block_bias(wide, at + AT_B2, block, grad_b[idx, 1:2])
+        put_rows(wide, at + AT_NORM[2], sum_norm[idx, 2:3])
+        put_rows(wide, at + AT_NORM[3], sum_norm[idx, 3:4])
+
+    def put_small(i, at):
+        if i == 0:
+            put_rows(wide, at, sum_tail[2:3])
+            put_layer(at + 6, 0)
+        elif i == 2:
+            put_rows(wide, at, sum_norm[0, 4:5])
+            put_layer(at + 6, 1)
+        elif i == 4:
+            put_rows(wide, at, sum_norm[1, 4:5])
+            put_rows(wide, at + 6, sum_tail[0:1])
+            put_rows(wide, at + 12, sum_tail[1:2])
+        elif i == 5:
+            put_rows(wide, at, sum_head[0:1])
+        else:
+            put_rows(wide, at, sum_c1[i // 2, 0:1])
+
+    pending = []
+
+    def emit(at, full):
+        return pltpu.make_async_copy(narrow.at[pl.ds(0, full)], flat.at[pl.ds(at, full)], sem)
+
+    for i, (start, depth, per_row, small_at, small) in enumerate(flat_sections()):
+        for k in needs[i]:
+            loads[k].wait()
+        x0, x1_, g0, g1 = pairs[i]
+        cols = per_row * LANES
+        for half, (x, g) in enumerate(((x0, g0), (x1_, g1))):
+            for part in range(0, depth, PIECE):
+                across[part : part + PIECE, half * 128 : half * 128 + 128] = x[
+                    :, part : part + PIECE
+                ].T
+            side[half * 128 : half * 128 + 128, 0:cols] = g[...]
+        rows = piece_rows(depth, per_row)
+        full = rows * per_row
+        shift = start % 16
+        before = pending.pop() if pending else None
+
+        def step(it, carry):
+            top = pl.multiple_of(it * rows, PIECE)
+            for part in range(0, rows, PIECE):
+                left = across[pl.ds(pl.multiple_of(top + part, PIECE), PIECE), :]
+                for j in range(0, per_row, 2):
+                    value = dot(left, side[:, j * LANES : (j + 2) * LANES])
+                    for side_by in range(2):
+                        wide[
+                            pl.ds(shift + part * per_row + j + side_by, PIECE, stride=per_row), :
+                        ] = value[:, side_by * LANES : (side_by + 1) * LANES]
+            if before is not None:
+                @pl.when(it == 0)
+                def _():
+                    before.wait()
+
+            @pl.when(it > 0)
+            def _():
+                emit(0, full).wait()
+
+            narrow[0:full] = wide[0:full].astype(bf16)
+            emit(pl.multiple_of(start - shift + it * full, 16), full).start()
+            wide[0:16] = wide[full : full + 16]
+            return carry
+
+        lax.fori_loop(0, depth // rows, step, 0)
+        shift = small_at % 16
+        put_small(i, shift)
+        full = (shift + small) // 16 * 16
+        if i == 5:
+            wide[shift + small : GROWS - small_at + shift] = jnp.zeros(
+                (GROWS - small_at - small, LANES), f32
+            )
+            full = GROWS - small_at + shift
+        emit(0, rows * per_row).wait()
+        narrow[0:full] = wide[0:full].astype(bf16)
+        done = emit(small_at - shift, full)
+        done.start()
+        pending.append(done)
+        if i < 5:
+            wide[0:16] = wide[full : full + 16]
+    pending.pop().wait()
+
+
+def pack_flat(*args):
+    vm, whole = pltpu.VMEM, pl.BlockSpec(memory_space=pltpu.VMEM)
+    anywhere = pl.BlockSpec(memory_space=pl.ANY)
+    return pl.pallas_call(
+        pack_kernel,
+        out_shape=jax.ShapeDtypeStruct((GROWS, LANES), bf16),
+        in_specs=[anywhere] * 9 + [whole] * 7,
+        out_specs=anywhere,
+        scratch_shapes=[vm(a.shape, a.dtype) for a in args[:9]]
+        + [
+            vm((FF, 256), bf16),
+            vm((256, FF), bf16),
+            vm((7712, LANES), f32),
+            vm((7712, LANES), bf16),
+            vm((2, PADC, PADC), f32),
+            pltpu.SemaphoreType.DMA,
+            pltpu.SemaphoreType.DMA((9,)),
+        ],
+        compiler_params=pltpu.CompilerParams(vmem_limit_bytes=52 << 20),
+        name="pack_flat",
+    )(*args)
+
+
 CELLS = 2 * UNIT
 FCHUNK = 768
 FILTER_SEMS = 10
@@ -1049,25 +1215,145 @@
     )
 
 
+SMALL_AT = []
+for _count in SMALLS:
+    SMALL_AT.append(SMALL_AT[-1] + -(-SMALLS[len(SMALL_AT) - 1] // 8) * 8 if SMALL_AT else 0)
+SMALL_ROWS = SMALL_AT[-1] + 16
+AT_NORM = (0, 6, 2340, 2346)
+AT_W1, AT_B1, AT_W2, AT_B2 = 12, 1164, 1176, 2328
+BLOCK_ROWS = BS * BS // LANES
+
+
+def aligned_part(at, count):
+    low = at // 16 * 16
+    return low, -(-(at + count - low) // 16) * 16
+
+
+def unpack_sections(flat, raw, wide, in_sem, wanted):
+    steps = []
+    for i, target in wanted:
+        start, depth, per_row, _, _ = flat_sections()[i]
+        rows = piece_rows(depth, per_row)
+        for top in range(0, depth, rows):
+            steps.append((start + top * per_row, per_row, top, rows, target))
+
+    def fetch(n):
+        at, per_row, _, rows, _ = steps[n]
+        low, size = aligned_part(at, rows * per_row)
+        return pltpu.make_async_copy(
+            flat.at[pl.ds(low, size)], raw.at[n % 2, pl.ds(0, size)], in_sem.at[n % 2]
+        ), size
+
+    fetch(0)[0].start()
+    for n, (at, per_row, top, rows, target) in enumerate(steps):
+        if n + 1 < len(steps):
+            fetch(n + 1)[0].start()
+        copy, size = fetch(n)
+        copy.wait()
+        wide[0:size] = raw[n % 2, 0:size].astype(f32)
+        for part in range(0, rows, PIECE):
+            for j in range(per_row):
+                target[top + part : top + part + PIECE, j * LANES : (j + 1) * LANES] = wide[
+                    pl.ds(at % 16 + part * per_row + j, PIECE, stride=per_row), :
+                ].astype(bf16)
+
+
+def unpack_small(flat, raw, wide, in_sem, small):
+    def fetch(n):
+        _, _, _, at, count = flat_sections()[n]
+        low, size = aligned_part(at, count)
+        return pltpu.make_async_copy(
+            flat.at[pl.ds(low, size)], raw.at[n % 2, pl.ds(0, size)], in_sem.at[n % 2]
+        ), size, at - low, count
+
+    fetch(0)[0].start()
+    for n in range(6):
+        if n < 5:
+            fetch(n + 1)[0].start()
+        copy, size, shift, count = fetch(n)
+        copy.wait()
+        wide[0:size] = raw[n % 2, 0:size].astype(f32)
+        small[SMALL_AT[n] : SMALL_AT[n] + count] = wide[shift : shift + count]
+
+
+def long_row(small, at, count):
+    return jnp.concatenate([small[at + k : at + k + 1] for k in range(count)], axis=1)
+
+
+def block_weight(small, at, block, square, out):
+    blank = jnp.zeros((24, PADC - BS), f32)
+    square[...] = jnp.zeros_like(square)
+    for part in range(2):
+        base = at + (part * NBLK + block) * BLOCK_ROWS
+        a, b, c = (small[pl.ds(base + q, 24, stride=3), :] for q in range(3))
+        pieces = (
+            a[:, :96],
+            jnp.concatenate([a[:, 96:], b[:, :64]], axis=1),
+            jnp.concatenate([b[:, 64:], c[:, :32]], axis=1),
+            c[:, 32:],
+        )
+        for q, piece in enumerate(pieces):
+            piece = jnp.concatenate([piece, blank], axis=1)
+            if part == 0:
+                square[0, pl.ds(q, 24, stride=4), :] = piece
+                square[3, pl.ds(q, 24, stride=4), :] = piece
+            else:
+                square[1, pl.ds(q, 24, stride=4), :] = piece
+                square[2, pl.ds(q, 24, stride=4), :] = -piece
+    for quarter in range(4):
+        top, left = quarter // 2 * PADC, quarter % 2 * PADC
+        out[top : top + PADC, left : left + PADC] = square[quarter].astype(bf16)
+
+
+def block_bias(small, at, block):
+    blank = jnp.zeros((1, PADC - BS), f32)
+    both = long_row(small, at, 12)
+    found = []
+    for part in range(2):
+        value = jnp.zeros((1, BS), f32)
+        for k in range(NBLK):
+            low = (part * NBLK + k) * BS
+            value = value + jnp.where(block == k, both[:, low : low + BS], 0.0)
+        found += [value, blank]
+    return jnp.concatenate(found, axis=1)
+
+
 def forward_kernel(*refs):
-    (x0, goals, mask, weight, embed_b, norms, c1, c2, tail, head_b, column, inverse, rows,
-     w1, b1, w2, b2, embed_h, in0, out0, in1, out1, head_h) = refs[:23]
-    streams, waves_o, mixeds, normeds, befores, hiddens, lasts, tails, errors, x1, loss = refs[23:34]
+    x0, goals, mask, weight, column, inverse, rows, flat = refs[:8]
+    (streams, waves_o, mixeds, normeds, befores, hiddens, lasts, tails, errors,
+     embed_h, in0, out0, in1, out1, head_h, x1, loss, norms, tail, w1, b1, w2) = refs[8:30]
     (embed, w_in, w_out, head, flow, x_now, s_stream, s_waves, s_mixed, s_norm, s_before, s_hidden,
-     s_tail, s_error, weight_sem, out_sem, tail_sem) = refs[34:51]
-    units, mine, others, waves, back, own_sum, to_sib, from_sib, ready, landed, joined = refs[51:62]
-    sems = refs[62:]
+     s_tail, s_error, raw, wide, small, square, b2, c1, c2, embed_b, head_b,
+     weight_sem, out_sem, tail_sem, in_sem) = refs[30:57]
+    units, mine, others, waves, back, own_sum, to_sib, from_sib, ready, landed, joined = refs[57:68]
+    sems = refs[68:]
     row, me, core, sibling = place()
     barrier = greet_chips(me, core, sibling)
-    loads = [
+    stores = [
         pltpu.make_async_copy(source, target, weight_sem.at[k])
         for k, (source, target) in enumerate(
-            [(embed_h, embed), (in0, w_in.at[0]), (out0, w_out.at[0]), (in1, w_in.at[1]),
-             (out1, w_out.at[1]), (head_h, head)]
+            [(embed, embed_h), (w_in.at[0], in0), (w_out.at[0], out0), (w_in.at[1], in1),
+             (w_out.at[1], out1), (head, head_h)]
         )
     ]
-    for load in loads:
-        load.start()
+    block = me % NBLK
+    unpack_small(flat, raw, wide, in_sem, small)
+    embed_b[...] = long_row(small, SMALL_AT[0], 6)
+    head_b[...] = long_row(small, SMALL_AT[5], 10)
+    for layer in range(LAYERS):
+        base = SMALL_AT[2 * layer] + 6
+        for k, at in enumerate(AT_NORM):
+            norms[layer, k : k + 1] = long_row(small, base + at, 6)
+        c1[layer] = long_row(small, SMALL_AT[2 * layer + 1], 24)
+        c2[layer] = long_row(small, SMALL_AT[2 * layer + 2], 6)
+        block_weight(small, base + AT_W1, block, square, w1.at[layer])
+        block_weight(small, base + AT_W2, block, square, w2.at[layer])
+        b1[layer] = block_bias(small, base + AT_B1, block)
+        b2[layer] = block_bias(small, base + AT_B2, block)
+    tail[0:1] = long_row(small, SMALL_AT[4] + 6, 6)
+    tail[1:2] = long_row(small, SMALL_AT[4] + 12, 6)
+    unpack_sections(flat, raw, wide, in_sem, [(0, embed)])
+    stores[0].start()
     x_now[...] = x0[...]
     loss[...] = jnp.zeros_like(loss)
 
@@ -1091,13 +1377,27 @@
         def _():
             action()
 
+    def unpack_when(it, number, wanted, done):
+        def go():
+            unpack_sections(flat, raw, wide, in_sem, wanted)
+            for k in done:
+                stores[k].start()
+
+        when_it(it == number, go)
+
+    def meanwhile_in(it):
+        unpack_when(it, 0, [(1, w_in.at[0])], [1])
+        unpack_when(it, 1, [(3, w_in.at[1])], [3])
+
+    def meanwhile_out(it):
+        unpack_when(it, 0, [(2, w_out.at[0])], [2])
+        unpack_when(it, 1, [(4, w_out.at[1]), (5, head)], [4, 5])
+
     def body(it, carry):
         step, layer = it // 2, it % 2
 
         def start_step():
             flow[...] = dot(x_now[...], embed[...]) + embed_b[...]
-
-        when_it(it == 0, loads[0].wait)
 
         def tail_done():
             for save in tail_saves(0):
@@ -1115,7 +1415,10 @@
         normed, _ = normalize(flow[...])
         split_units(normed * norms[layer, 0:1] + norms[layer, 1:2], units)
         when_it(it == 0, lambda: pl.semaphore_wait(barrier, CHIPS))
-        finish_one = spread_units(me, core, sibling, units, mine, others, sems[:5])
+
+        finish_one = spread_units(
+            me, core, sibling, units, mine, others, sems[:5], lambda: meanwhile_in(it)
+        )
         groups = to_spectrum(mine, others, column, rows, waves)
         for g in range(4):
             s_waves[g] = groups[g]
@@ -1125,6 +1428,7 @@
         finish_two = gather_units(
             row, me, core, sibling, back, inverse,
             (own_sum, to_sib, from_sib, ready, landed), sems[5:], finish_one,
+            lambda: meanwhile_out(it),
         )
         join_units(landed, joined)
         mixed = flow[...] + joined[...]
@@ -1132,17 +1436,6 @@
         normed, _ = normalize(mixed)
         s_norm[...] = (normed * norms[layer, 2:3] + norms[layer, 3:4]).astype(bf16)
         flow[...] = mixed + c2[layer]
-
-        def first_layer():
-            loads[1].wait()
-            loads[2].wait()
-
-        def second_layer():
-            loads[3].wait()
-            loads[4].wait()
-
-        when_it(it == 0, first_layer)
-        when_it(it == 1, second_layer)
 
         def chunk(c, carry):
             part = pl.ds(pl.multiple_of(c * FCHUNK, FCHUNK), FCHUNK)
@@ -1157,8 +1450,6 @@
         for save in saves(it):
             save.start()
         finish_two()
-        when_it(it == 1, loads[5].wait)
-
         def end_step():
             normed, _ = normalize(flow[...])
             s_tail[...] = (normed * tail[0:1] + tail[1:2]).astype(bf16)
@@ -1179,6 +1470,8 @@
         save.wait()
     for save in tail_saves(1):
         save.wait()
+    for store in stores:
+        store.wait()
 
 
 def forward_pass(*args):
@@ -1197,11 +1490,17 @@
             shape((2, CELLS, D), f32),
             shape((2, CELLS, D), bf16),
             shape((2, CELLS, PIN), f32),
+            *[shape(dims, bf16) for dims in MATS],
             shape((CELLS, PIN), bf16),
             shape((CELLS, 1), f32),
+            shape((2, 4, D), f32),
+            shape((2, D), f32),
+            shape((2, 256, 256), bf16),
+            shape((2, 1, 256), f32),
+            shape((2, 256, 256), bf16),
         ],
-        in_specs=[whole] * 17 + [anywhere] * 6,
-        out_specs=[anywhere] * 9 + [whole] * 2,
+        in_specs=[whole] * 7 + [anywhere],
+        out_specs=[anywhere] * 15 + [whole] * 7,
         scratch_shapes=[
             vm((PIN, D), bf16),
             vm((2, D, FF), bf16),
@@ -1217,9 +1516,19 @@
             vm((CELLS, FF), bf16),
             vm((CELLS, D), bf16),
             vm((CELLS, PIN), f32),
+            vm((2, 7696, LANES), bf16),
+            vm((7696, LANES), f32),
+            vm((SMALL_ROWS, LANES), f32),
+            vm((4, PADC, PADC), f32),
+            vm((2, 1, 256), f32),
+            vm((2, 1, FF), f32),
+            vm((2, 1, D), f32),
+            vm((1, D), f32),
+            vm((1, PIN), f32),
             dma((6,)),
             dma((6,)),
             dma((3,)),
+            dma((2,)),
         ]
         + filter_scratch(),
         compiler_params=pltpu.CompilerParams(
@@ -1366,7 +1675,9 @@
         sum_norm[layer, 3:4] += shift
         split_units(flow[...], units)
         when_it(it == 0, lambda: pl.semaphore_wait(barrier, CHIPS))
-        finish_one = spread_units(me, core, sibling, units, mine, others, sems[:5])
+        finish_one = spread_units(
+            me, core, sibling, units, mine, others, sems[:5], lambda: None
+        )
         groups = to_spectrum(mine, others, column, rows, waves)
         for g in range(4):
             before = dot(i_waves[slot, g], w1[layer]) + b1[layer]
@@ -1381,7 +1692,7 @@
             from_spectrum(g, dot_cols(grad_before16, w1[layer]).astype(bf16), rows, back)
         finish_two = gather_units(
             row, me, core, sibling, back, inverse,
-            (own_sum, to_sib, from_sib, ready, landed), sems[5:], finish_one,
+            (own_sum, to_sib, from_sib, ready, landed), sems[5:], finish_one, lambda: None,
         )
         join_units(landed, joined)
         value, gain, shift = norm_adjoint(i_stream[slot], norms[layer, 0:1], joined[...])
@@ -1465,225 +1776,14 @@
     )(*args)
 
 
-MATS = [(PIN, D), (D, FF), (FF, D), (D, FF), (FF, D), (D, PIN)]
-SMALL_LAYER = 2352
-SMALLS = [6 + SMALL_LAYER, 24, 6 + SMALL_LAYER, 24, 18, 10]
-PIECE = 256
-
-
-def flat_sections():
-    at = 0
-    found = []
-    for (depth, cols), small in zip(MATS, SMALLS):
-        per_row = cols // LANES
-        found.append((at, depth, per_row, at + depth * per_row, small))
-        at += depth * per_row + small
-    return found
-
-
-def piece_rows(depth, per_row):
-    rows = depth
-    while rows * per_row > 7680:
-        rows -= PIECE
-        while depth % rows:
-            rows -= PIECE
-    return rows
-
-
-def unpack_kernel(flat, *refs):
-    mats, smalls = refs[:6], refs[6:12]
-    raw, wide, out24, out6, out10, in_sem, out_sem = refs[12:]
-    outs = {24: out24, 6: out6, 10: out10}
-    steps = []
-    for i, (start, depth, per_row, small_at, small) in enumerate(flat_sections()):
-        rows = piece_rows(depth, per_row)
-        for top in range(0, depth, rows):
-            steps.append((i, start + top * per_row, rows * per_row, per_row, top, rows))
-        steps.append((i, small_at, small, 0, 0, 0))
-
-    def fetch(n):
-        _, at, count, *_ = steps[n]
-        low = at // 16 * 16
-        size = -(-(at + count - low) // 16) * 16
-        return pltpu.make_async_copy(
-            flat.at[pl.ds(low, size)], raw.at[n % 2, pl.ds(0, size)], in_sem.at[n % 2]
-        ), size
-
-    fetch(0)[0].start()
-    pending = {}
-    for n, (i, at, count, per_row, top, rows) in enumerate(steps):
-        if n + 1 < len(steps):
-            fetch(n + 1)[0].start()
-        copy, size = fetch(n)
-        copy.wait()
-        wide[0:size] = raw[n % 2, 0:size].astype(f32)
-        shift = at % 16
-        if not per_row:
-            smalls[i][0:count] = wide[shift : shift + count]
-            continue
-        out = outs[per_row]
-        if per_row in pending:
-            pending.pop(per_row).wait()
-        for part in range(0, rows, PIECE):
-            for j in range(per_row):
-                out[part : part + PIECE, j * LANES : (j + 1) * LANES] = wide[
-                    pl.ds(shift + part * per_row + j, PIECE, stride=per_row), :
-                ].astype(bf16)
-        done = pltpu.make_async_copy(
-            out.at[pl.ds(0, rows)], mats[i].at[pl.ds(top, rows)], out_sem.at[(24, 6, 10).index(per_row)]
-        )
-        done.start()
-        pending[per_row] = done
-    for done in pending.values():
-        done.wait()
-
-
-def unpack_flat(flat):
-    vm, anywhere = pltpu.VMEM, pl.BlockSpec(memory_space=pl.ANY)
-    shape = jax.ShapeDtypeStruct
-    padded = [-(-count // 8) * 8 for count in SMALLS]
-    return pl.pallas_call(
-        unpack_kernel,
-        out_shape=[shape(m, bf16) for m in MATS] + [shape((n, LANES), f32) for n in padded],
-        in_specs=[anywhere],
-        out_specs=[anywhere] * 6 + [pl.BlockSpec(memory_space=vm)] * 6,
-        scratch_shapes=[
-            vm((2, 7696, LANES), bf16),
-            vm((7696, LANES), f32),
-            vm((256, FF), bf16),
-            vm((1280, D), bf16),
-            vm((768, PIN), bf16),
-            pltpu.SemaphoreType.DMA((2,)),
-            pltpu.SemaphoreType.DMA((3,)),
-        ],
-        compiler_params=pltpu.CompilerParams(vmem_limit_bytes=48 << 20),
-        name="unpack_flat",
-    )(flat)
-
-
-def pack_kernel(counts, *refs):
-    pairs = [refs[4 * i : 4 * i + 4] for i in range(6)]
-    smalls, rest = [], refs[24:]
-    for number in counts:
-        smalls.append(rest[:number])
-        rest = rest[number:]
-    flat, across, side, wide, narrow, sem = rest
-    pending = []
-
-    def emit(at, full):
-        return pltpu.make_async_copy(narrow.at[pl.ds(0, full)], flat.at[pl.ds(at, full)], sem)
-
-    for i, (start, depth, per_row, small_at, small) in enumerate(flat_sections()):
-        x0, x1, g0, g1 = pairs[i]
-        cols = per_row * LANES
-        for half, (x, g) in enumerate(((x0, g0), (x1, g1))):
-            for part in range(0, depth, PIECE):
-                across[part : part + PIECE, half * 128 : half * 128 + 128] = x[
-                    :, part : part + PIECE
-                ].T
-            side[half * 128 : half * 128 + 128, 0:cols] = g[...]
-        rows = piece_rows(depth, per_row)
-        full = rows * per_row
-        shift = start % 16
-        before = pending.pop() if pending else None
-
-        def step(it, carry):
-            top = pl.multiple_of(it * rows, PIECE)
-            for part in range(0, rows, PIECE):
-                left = across[pl.ds(pl.multiple_of(top + part, PIECE), PIECE), :]
-                for j in range(0, per_row, 2):
-                    value = dot(left, side[:, j * LANES : (j + 2) * LANES])
-                    for side_by in range(2):
-                        wide[
-                            pl.ds(shift + part * per_row + j + side_by, PIECE, stride=per_row), :
-                        ] = value[:, side_by * LANES : (side_by + 1) * LANES]
-            if before is not None:
-                @pl.when(it == 0)
-                def _():
-                    before.wait()
-
-            @pl.when(it > 0)
-            def _():
-                emit(0, full).wait()
-
-            narrow[0:full] = wide[0:full].astype(bf16)
-            emit(pl.multiple_of(start - shift + it * full, 16), full).start()
-            wide[0:16] = wide[full : full + 16]
-            return carry
-
-        lax.fori_loop(0, depth // rows, step, 0)
-        shift = small_at % 16
-        into = shift
-        for piece in smalls[i]:
-            wide[into : into + piece.shape[0]] = piece[...]
-            into += piece.shape[0]
-        full = (shift + small) // 16 * 16
-        if i == 5:
-            wide[shift + small : GROWS - small_at + shift] = jnp.zeros(
-                (GROWS - small_at - small, LANES), f32
-            )
-            full = GROWS - small_at + shift
-        emit(0, rows * per_row).wait()
-        narrow[0:full] = wide[0:full].astype(bf16)
-        done = emit(small_at - shift, full)
-        done.start()
-        pending.append(done)
-        if i < 5:
-            wide[0:16] = wide[full : full + 16]
-    pending.pop().wait()
-
-
-def pack_flat(pairs, smalls):
-    vm, whole = pltpu.VMEM, pl.BlockSpec(memory_space=pltpu.VMEM)
-    args = [a for four in pairs for a in four] + [a for some in smalls for a in some]
-    return pl.pallas_call(
-        functools.partial(pack_kernel, [len(some) for some in smalls]),
-        out_shape=jax.ShapeDtypeStruct((GROWS, LANES), bf16),
-        in_specs=[whole] * len(args),
-        out_specs=pl.BlockSpec(memory_space=pl.ANY),
-        scratch_shapes=[
-            vm((FF, 256), bf16),
-            vm((256, FF), bf16),
-            vm((7712, LANES), f32),
-            vm((7712, LANES), bf16),
-            pltpu.SemaphoreType.DMA,
-        ],
-        compiler_params=pltpu.CompilerParams(vmem_limit_bytes=52 << 20),
-        name="pack_flat",
-    )(*args)
-
-
-def split_small(rows, layouts):
-    found, at = [], 0
-    for layout in layouts:
-        count = math.prod(layout) // LANES
-        found.append(rows[at : at + count].reshape(layout))
-        at += count
-    return found
-
-
-SPEC_ROWS = (2, NBLK, BS * BS // LANES, LANES)
-LAYER_SMALL = [(D,), (D,), SPEC_ROWS, (2, NBLK, BS), SPEC_ROWS, (2, NBLK, BS), (D,), (D,)]
-
-
 def local_fast(frames, targets, regions, master, first_moment, second_moment):
     height, width = 16, 128
     device = lax.axis_index("row") * 4 + lax.axis_index("col")
-    _, chip, core, _ = place()
-    block = chip % NBLK
+    core = lax.axis_index("col") % 2
     shard = master.astype(bf16).reshape(OWN, LANES)
     halo = lax.ppermute(shard[:320], ("row", "col"), [(k + 1, k) for k in range(31)])
     chunk = lax.dynamic_slice_in_dim(jnp.concatenate([shard, halo]), 10 * device, CH, 0)
-    unpacked = unpack_flat(ag(chunk))
-    embed, in0, out0, in1, out1, head = unpacked[:6]
-    smalls = unpacked[6:]
-    embed_bias, *layer0 = split_small(smalls[0], [(D,)] + LAYER_SMALL)
-    (c1_0,) = split_small(smalls[1], [(FF,)])
-    c2_0, *layer1 = split_small(smalls[2], [(D,)] + LAYER_SMALL)
-    (c1_1,) = split_small(smalls[3], [(FF,)])
-    c2_1, gain3, shift3 = split_small(smalls[4], [(D,)] * 3)
-    (head_bias,) = split_small(smalls[5], [(PIN,)])
-    layers = [(layer0, in0, c1_0, out0, c2_0), (layer1, in1, c1_1, out1, c2_1)]
+    flat = ag(chunk)
     tables = transform_tables(core)
     row_ids = lax.axis_index("row") * 2 + jnp.arange(2, dtype=jnp.int32)
     col_ids = lax.axis_index("col") * 32 + jnp.arange(32, dtype=jnp.int32)
@@ -1702,65 +1802,20 @@
     flat_weight = weighted.reshape(128, 1)
     inputs = (frames.reshape(128, PIN).astype(f32) * flat_mask).astype(bf16)
     goals = jnp.stack([targets[:, s].reshape(128, PIN) for s in range(STEPS)])
-    spectral_weights = []
-    for small, *_ in layers:
-        found = []
-        for j in (2, 4):
-            w = lax.dynamic_index_in_dim(small[j], block, 1, False).reshape(2, BS, BS)
-            b = lax.dynamic_index_in_dim(small[j + 1], block, 1, False)
-            found += [spread_weight(w[0], w[1]).astype(bf16), spread_bias(b)]
-        spectral_weights.append(found)
-    w1, b1, w2, b2 = (jnp.stack(both) for both in zip(*spectral_weights))
-    norms = jnp.stack([jnp.stack([small[k] for k in (0, 1, 6, 7)]) for small, *_ in layers])
-    tail = jnp.stack([gain3, shift3])
-    mats = (embed, in0, out0, in1, out1, head)
-    streams, waves, mixeds, normeds, befores, hiddens, lasts, tails, errors, x1, loss = forward_pass(
-        inputs, goals, flat_mask, flat_weight, embed_bias[None], norms,
-        jnp.stack([c1_0, c1_1])[:, None], jnp.stack([c2_0, c2_1])[:, None], tail, head_bias[None],
-        *tables, w1, b1, w2, b2, *mats,
-    )
+    (streams, waves, mixeds, normeds, befores, hiddens, lasts, tails, errors, *rest) = forward_pass(
+        inputs, goals, flat_mask, flat_weight, *tables, flat
+    )
+    mats, (x1, loss, norms, tail, w1, b1, w2) = rest[:6], rest[6:]
     (g_pred, g_out, g_pre, g_embed, sum_norm, sum_c1, sum_tail, sum_head, grad_w1, grad_w2, grad_b) = (
         backward_pass(
             flat_weight * (2.0 / total_weight), flat_mask, norms, tail, *tables, w1, b1, w2, *mats,
             streams, waves, mixeds, befores, lasts, errors,
         )
     )
-    pairs = [[inputs, x1, g_embed[0], g_embed[1]]]
-    for idx in range(LAYERS):
-        pairs.append([normeds[idx], normeds[2 + idx], g_pre[idx], g_pre[2 + idx]])
-        pairs.append([hiddens[idx], hiddens[2 + idx], g_out[idx], g_out[2 + idx]])
-    pairs.append([tails[0], tails[1], g_pred[0], g_pred[1]])
-
-    def as_rows(value):
-        return value.reshape(-1, LANES)
-
-    def placed(local_grad):
-        local_grad = local_grad.reshape(2, 1, -1)
-        whole = jnp.zeros((2, NBLK, local_grad.shape[2]), f32)
-        return as_rows(lax.dynamic_update_slice_in_dim(whole, local_grad, block, 1))
-
-    def layer_rows(idx):
-        gb = grad_b[idx]
-        return [
-            as_rows(sum_norm[idx, 0]),
-            as_rows(sum_norm[idx, 1]),
-            placed(fold_weight(grad_w1[idx])),
-            placed(fold_bias(gb[0])),
-            placed(fold_weight(grad_w2[idx])),
-            placed(fold_bias(gb[1])),
-            as_rows(sum_norm[idx, 2]),
-            as_rows(sum_norm[idx, 3]),
-        ]
-
-    small_grads = [
-        [as_rows(sum_tail[2])] + layer_rows(0),
-        [as_rows(sum_c1[0, 0])],
-        [as_rows(sum_norm[0, 4])] + layer_rows(1),
-        [as_rows(sum_c1[1, 0])],
-        [as_rows(v) for v in (sum_norm[1, 4], sum_tail[0], sum_tail[1])],
-        [as_rows(sum_head[0])],
-    ]
-    flat_grad = pack_flat(pairs, small_grads)
+    flat_grad = pack_flat(
+        inputs, x1, normeds, hiddens, tails, g_embed, g_pre, g_out, g_pred,
+        sum_norm, sum_c1, sum_tail, sum_head, grad_w1, grad_w2, grad_b,
+    )
     loss_tile = jnp.concatenate([loss.reshape(1, LANES), jnp.zeros((7, LANES), f32)])
     summed, stats = rs(flat_grad, loss_tile)
     reduced = lax.dynamic_slice_in_dim(summed, (device * OWN) % 16, OWN, 0).reshape(-1)

time: 553 us -> 487 us (0.88)
  local copies, waits for them, and re-layouts: 41.4 us -> 9.29 us
  Pallas kernels: 481 us -> 455 us
    pallas_call x2 -> x1, Pallas kernels: 57 us -> 27.2 us  [pack_flat(): pl.pallas_call(pack_kernel, out_shape=jax.ShapeDtypeStruct((GROWS, LANES)...]
    dynamic_update_slice x8 -> x0, local copies, waits for them, and re-layouts: 9.55 us -> none  [placed(): return as_rows(lax.dynamic_update_slice_in_dim(whole, local_grad, block, 1))]
    squeeze x17 -> x0, local copies, waits for them, and re-layouts: 7.72 us -> none  [the longest x2 2.51 us: local_fast(): pairs.append([hiddens[idx], hiddens[2 + idx], g_out[idx], g_out[2 + idx]])]
    slice x14 -> x0, local copies, waits for them, and re-layouts: 7.32 us -> none  [the longest x8 3.13 us: local_fast(): found += [spread_weight(w[0], w[1]).astype(bf16), spread_bias(b)]]
    reshape x12 -> x0, local copies, waits for them, and re-layouts: 6.57 us -> none  [the longest x8 6.28 us: as_rows(): return value.reshape(-1, LANES)]
  transfers between devices with their start and end apart: 1 -> 1, of which waited for: 0 -> 0; matrix products, arithmetic and copies ran while one was open for 1% -> 2% of each run, Pallas kernels for 0% -> 0%
where the time goes in v3:
time: 487 us; the launch traced here: 486 us
  Pallas kernels  455 us (93%)
  other arithmetic  15.2 us (3%)
  local copies, waits for them, and re-layouts  9.29 us (2%)
    pallas_call x1, Pallas kernels, backward_pass(): pl.pallas_call(backward_kernel, out_shape=[shape((2, CELLS, PIN), bf16),...  118 us
    pallas_call x1, Pallas kernels, forward_pass(): pl.pallas_call(forward_kernel, out_shape=[shape((4, CELLS, D), f32), shap...  107 us
    pallas_call x1, Pallas kernels, rs(): pl.pallas_call(sum_kernel, out_shape=[shape((CHR, 128), f32), shape((16,...  107 us
    pallas_call x1, Pallas kernels, ag(): pl.pallas_call(gather_kernel, out_shape=jax.ShapeDtypeStruct((32 * CH, 12...  96.1 us
    pallas_call x1, Pallas kernels, pack_flat(): pl.pallas_call(pack_kernel, out_shape=jax.ShapeDtypeStruct((GROWS, LANES)...  27.2 us
  transfers between devices with their start and end apart: 1, of which 0 were waited for; matrix products, arithmetic and copies ran while one was open for 2% of the time, Pallas kernels for 0%

profile of v3, /device:TPU:0, one launch (start us, length us, event | category | flops | bytes accessed | tf_op | source)
XLA Modules:
  0.0 485.8 jit_solution(3534001528001504433)
XLA Ops:
  0.6 0.0 copy-start.9
  0.6 0.0 copy-start.13
  0.7 1.6 convert_element_type.57
  2.2 1.3 collective-permute-start
  3.6 0.0 copy-done.13
  3.6 0.2 slice_reduce_fusion.4
  3.9 0.1 compare_and_fusion.1
  3.9 0.1 fusion.5
  4.0 0.1 and_convert_fusion
  4.1 0.1 reshape.389
  4.2 0.7 reshape.391.refs_2_.refs_1_
  4.9 0.0 copy-done.9
  4.9 0.1 convert_bitcast_fusion
  5.0 0.1 compare_and_fusion
  5.1 0.1 fusion.7
  5.2 0.1 and_select_fusion
  5.3 0.1 mul.121.refs_3_
  5.4 0.0 copy-start.11
  5.4 0.0 copy-start.14
  5.4 1.2 fusion.11
  6.6 0.7 select_reduce_fusion
  8.0 0.0 copy-done.12
  8.0 0.8 fusion.3.refs_0_
  8.9 0.9 pad_maximum_fusion.refs_1_
  9.7 0.0 copy-done.11
  9.7 0.6 broadcast_multiply_fusion.refs_0_
  10.4 0.0 copy-done.14
  10.4 1.4 dynamic-slice_bitcast_fusion
  11.8 0.0 collective-permute-done
  11.8 2.7 fusion.2.shard
  14.4 96.1 %gather_weights.1.refs_7_ = bf16[94208,128]{1,0:T(8,128)(2,1)} custom-call(bf16[2944,128]{1,0:T(8,128)(2,1)} %fusion.2.shard), custom_call_target="tpu_custom_call" | custom-call | tf_op jit(solution)/shard_map/gather_weights/pallas_call | solution.py:737
  110.5 107.0 %forward_pass.1 = (f32[4,128,768]{2,1,0:T(8,128)}, bf16[4,4,256,256]{3,2,1,0:T(8,128)(2,1)}, f32[4,128,768]{2,1,0:T(8,128)}, bf16[4,128,768]{2,1,0:T(8,128)(2,1)...) custom-call(bf16[128,1280]{1,0:T(8,128)(2,1)} %fusion.3.refs_0_, ...), custom_call_target="tpu_custom_call" | custom-call | tf_op jit(solution)/shard_map/forward_pass/pallas_call | solution.py:1481
  217.5 0.9 reduce.4
  218.5 0.6 concatenate.7.loss
  219.1 118.5 %backward_pass.1 = (bf16[2,128,1280]{2,1,0:T(8,128)(2,1)}, bf16[4,128,768]{2,1,0:T(8,128)(2,1)}, bf16[4,128,3072]{2,1,0:T(8,128)(2,1)}, bf16[2,128,768]{2,1,0:T(...) custom-call(f32[128,1]{1,0:T(8,128)} %broadcast_multiply_fusion.refs, ...), custom_call_target="tpu_custom_call" | custom-call | tf_op jit(solution)/shard_map/backward_pass/pallas_call | solution.py:1730
  337.6 0.0 copy-done
  337.6 0.0 copy-done.1
  337.6 1.0 copy-done.2
  338.6 0.9 copy-done.4
  339.5 0.8 copy-done.5
  340.3 0.8 copy-done.6
  341.1 0.7 copy-done.7
  341.8 0.7 copy-done.8
  342.5 27.2 %pack_flat.1.grad = bf16[93904,128]{1,0:T(8,128)(2,1)} custom-call(bf16[128,1280]{1,0:T(8,128)(2,1)S(1)} %copy-done, bf16[128,1280]{1,0:T(8,128)(2,1)S(1)} %copy-done.3, bf16[4,128,768]{2,1,0:T(8,128)(2,1)} %get-tuple-element.43.refs_2_, bf16[4,128,3072]{2,1,0:T(8,128)(2,1)} %get-tuple-element.44.refs_3_, bf16[2,128,768]{2,1,0:T(8,128)(2,1)S(1)} %copy-done.1, ...), custom_call_target="tpu_custom_call" | custom-call | tf_op jit(solution)/shard_map/pack_flat/pallas_call | solution.py:1181
  369.8 0.0 copy-start.10
  369.8 106.6 %sum_gradients.1 = (f32[2960,128]{1,0:T(8,128)}, f32[16,128]{1,0:T(8,128)}) custom-call(bf16[93904,128]{1,0:T(8,128)(2,1)} %pack_flat.1.grad, f32[8,128]{1,0:T(8,128)} %concatenate.7.loss), custom_call_target="tpu_custom_call" | custom-call | tf_op jit(solution)/shard_map/sum_gradients/pallas_call | solution.py:975
  476.4 1.3 slice_reduce_fusion
  478.5 5.0 %fusion.8 = (bf16[375552]{0:T(1024)(128)(2,1)}, f32[375552]{0:T(1024)}, f32[375552]{0:T(1024)}, f32[375552]{0:T(1024)}) fusion(f32[375552]{0:T(1024)S(1)} %copy-done.9, f32[]{:T(128)S(6)} %div.36, f32[2960,128]{1,0:T(8,128)} %get-tuple-element.75, s32[]{:T(128)S(6)} %select_n.50, f32[375552]{0:T(1024)S(1)} %copy-done.10, f32[375552]{0:T(1024)} %param.14), kind=kLoop, calls=%fused_computation.42 | loop fusion | flops 6384384 | bytes 11266568 | tf_op jit(solution)/shard_map/convert_element_type | solution.py:1841
  (18 shorter events, 0.1 us)
Async XLA Ops:
  0.6 4.3 copy-start.9
  0.6 3.0 copy-start.13
  2.2 9.5 %collective-permute-start = (bf16[320,128]{1,0:T(8,128)(2,1)S(1)}, bf16[320,128]{1,0:T(8,128)(2,1)S(1)}, u32[]{:S(2)}, u32[]{:S(2)}) collective-permute-start(bf16[320,128]{1,0:T(8,128)(2,1)S(1)} %slice_bitcast_fusion), channel_id=1, source_target_pairs={{1,0},{2,1},{3,2},{4,3},{5,4},{6,5},{7,6},{8,7},{9,8},{10,9},{11,1... | collective-permute-start | bytes 245768 | tf_op jit(solution)/shard_map/ppermute | solution.py:1784
  4.9 3.1 copy-start.12
  5.4 4.3 copy-start.11
  5.4 4.9 %copy-start.14 = (bf16[2,128,128]{2,1,0:T(8,128)(2,1)S(1)}, bf16[2,128,128]{2,1,0:T(8,128)(2,1)}, u32[]{:S(2)}) copy-start(bf16[2,128,128]{2,1,0:T(8,128)(2,1)} %constant.121.clone) | copy-start | bytes 196612
  219.1 118.5 %copy-start = (bf16[128,1280]{1,0:T(8,128)(2,1)S(1)}, bf16[128,1280]{1,0:T(8,128)(2,1)}, u32[]{:S(2)}) copy-start(bf16[128,1280]{1,0:T(8,128)(2,1)} %fusion.3.refs_0_) | copy-start | bytes 983044
  219.1 118.5 %copy-start.1 = (bf16[2,128,768]{2,1,0:T(8,128)(2,1)S(1)}, bf16[2,128,768]{2,1,0:T(8,128)(2,1)}, u32[]{:S(2)}) copy-start(bf16[2,128,768]{2,1,0:T(8,128)(2,1)} %get-tuple-element.45.refs_4_) | copy-start | bytes 1179652
  219.1 118.5 %copy-start.3 = (bf16[128,1280]{1,0:T(8,128)(2,1)S(1)}, bf16[128,1280]{1,0:T(8,128)(2,1)}, u32[]{:S(2)}) copy-start(bf16[128,1280]{1,0:T(8,128)(2,1)} %get-tuple-element.42.refs_1_) | copy-start | bytes 983044
  337.6 1.0 copy-start.2
  338.6 0.9 copy-start.4
  339.5 0.8 copy-start.5
  340.3 0.8 copy-start.6
  341.1 0.7 copy-start.7
  341.8 0.7 copy-start.8
  369.8 108.7 %copy-start.10 = (f32[375552]{0:T(1024)S(1)}, f32[375552]{0:T(1024)}, u32[]{:S(2)}) copy-start(f32[375552]{0:T(1024)} %param.13) | copy-start | bytes 4506628

commit v4 on v3

--- a/solution.py
+++ b/solution.py
@@ -1062,140 +1062,83 @@
     put_rows(wide, at, jnp.concatenate(found, axis=1))
 
 
-def pack_kernel(*refs):
-    sources, refs = refs[:9], refs[9:]
-    sum_norm, sum_c1, sum_tail, sum_head, grad_w1, grad_w2, grad_b = refs[:7]
-    flat = refs[7]
-    held, refs = refs[8:17], refs[17:]
-    across, side, wide, narrow, square, sem, in_sem = refs
-    inputs, x1, normeds, hiddens, tails, g_embed, g_pre, g_out, g_pred = held
-    _, me, _, _ = place()
-    block = me % NBLK
-    loads = [
-        pltpu.make_async_copy(source, target, in_sem.at[k])
-        for k, (source, target) in enumerate(zip(sources, held))
-    ]
-    order = (0, 1, 5, 2, 6, 3, 7, 4, 8)
-    for k in order:
-        loads[k].start()
-    needs = ((0, 1, 5), (2, 6), (3, 7), (), (), (4, 8))
-    pairs = [(inputs, x1, g_embed.at[0], g_embed.at[1])]
-    for idx in range(LAYERS):
-        pairs.append((normeds.at[idx], normeds.at[2 + idx], g_pre.at[idx], g_pre.at[2 + idx]))
-        pairs.append((hiddens.at[idx], hiddens.at[2 + idx], g_out.at[idx], g_out.at[2 + idx]))
-    pairs.append((tails.at[0], tails.at[1], g_pred.at[0], g_pred.at[1]))
-
-    def put_layer(at, idx):
-        put_rows(wide, at, sum_norm[idx, 0:1])
-        put_rows(wide, at + 6, sum_norm[idx, 1:2])
-        put_block_weight(wide, at + AT_W1, block, grad_w1[idx], square)
-        put_block_bias(wide, at + AT_B1, block, grad_b[idx, 0:1])
-        put_block_weight(wide, at + AT_W2, block, grad_w2[idx], square)
-        put_block_bias(wide, at + AT_B2, block, grad_b[idx, 1:2])
-        put_rows(wide, at + AT_NORM[2], sum_norm[idx, 2:3])
-        put_rows(wide, at + AT_NORM[3], sum_norm[idx, 3:4])
-
-    def put_small(i, at):
-        if i == 0:
-            put_rows(wide, at, sum_tail[2:3])
-            put_layer(at + 6, 0)
-        elif i == 2:
-            put_rows(wide, at, sum_norm[0, 4:5])
-            put_layer(at + 6, 1)
-        elif i == 4:
-            put_rows(wide, at, sum_norm[1, 4:5])
-            put_rows(wide, at + 6, sum_tail[0:1])
-            put_rows(wide, at + 12, sum_tail[1:2])
-        elif i == 5:
-            put_rows(wide, at, sum_head[0:1])
-        else:
-            put_rows(wide, at, sum_c1[i // 2, 0:1])
-
-    pending = []
-
-    def emit(at, full):
-        return pltpu.make_async_copy(narrow.at[pl.ds(0, full)], flat.at[pl.ds(at, full)], sem)
-
-    for i, (start, depth, per_row, small_at, small) in enumerate(flat_sections()):
-        for k in needs[i]:
-            loads[k].wait()
-        x0, x1_, g0, g1 = pairs[i]
-        cols = per_row * LANES
-        for half, (x, g) in enumerate(((x0, g0), (x1_, g1))):
-            for part in range(0, depth, PIECE):
-                across[part : part + PIECE, half * 128 : half * 128 + 128] = x[
-                    :, part : part + PIECE
-                ].T
-            side[half * 128 : half * 128 + 128, 0:cols] = g[...]
-        rows = piece_rows(depth, per_row)
-        full = rows * per_row
-        shift = start % 16
-        before = pending.pop() if pending else None
-
-        def step(it, carry):
-            top = pl.multiple_of(it * rows, PIECE)
-            for part in range(0, rows, PIECE):
-                left = across[pl.ds(pl.multiple_of(top + part, PIECE), PIECE), :]
-                for j in range(0, per_row, 2):
-                    value = dot(left, side[:, j * LANES : (j + 2) * LANES])
-                    for side_by in range(2):
-                        wide[
-                            pl.ds(shift + part * per_row + j + side_by, PIECE, stride=per_row), :
-                        ] = value[:, side_by * LANES : (side_by + 1) * LANES]
-            if before is not None:
-                @pl.when(it == 0)
-                def _():
-                    before.wait()
-
-            @pl.when(it > 0)
-            def _():
-                emit(0, full).wait()
-
-            narrow[0:full] = wide[0:full].astype(bf16)
-            emit(pl.multiple_of(start - shift + it * full, 16), full).start()
-            wide[0:16] = wide[full : full + 16]
-            return carry
-
-        lax.fori_loop(0, depth // rows, step, 0)
-        shift = small_at % 16
-        put_small(i, shift)
-        full = (shift + small) // 16 * 16
-        if i == 5:
-            wide[shift + small : GROWS - small_at + shift] = jnp.zeros(
-                (GROWS - small_at - small, LANES), f32
-            )
-            full = GROWS - small_at + shift
-        emit(0, rows * per_row).wait()
+def write_section(i, xs, gs, bufs):
+    across, side, wide, narrow, edge, flat, sem = bufs
+    start, depth, per_row, _, _ = flat_sections()[i]
+    cols = per_row * LANES
+    for half in range(2):
+        for part in range(0, depth, PIECE):
+            across[part : part + PIECE, half * 128 : half * 128 + 128] = xs[half][
+                :, part : part + PIECE
+            ].T
+        side[half * 128 : half * 128 + 128, 0:cols] = gs[half][...]
+    rows = piece_rows(depth, per_row)
+    full = rows * per_row
+    shift = start % 16
+    skip = 16 if shift else 0
+    turns = depth // rows
+
+    def emit(at, low):
+        return pltpu.make_async_copy(
+            narrow.at[pl.ds(low, full - low)], flat.at[pl.ds(at + low, full - low)], sem
+        )
+
+    def step(it, carry):
+        top = pl.multiple_of(it * rows, PIECE)
+        for part in range(0, rows, PIECE):
+            left = across[pl.ds(pl.multiple_of(top + part, PIECE), PIECE), :]
+            for j in range(0, per_row, 2):
+                value = dot(left, side[:, j * LANES : (j + 2) * LANES])
+                for by in range(2):
+                    wide[pl.ds(shift + part * per_row + j + by, PIECE, stride=per_row), :] = value[
+                        :, by * LANES : (by + 1) * LANES
+                    ]
+
+        @pl.when(it == 1)
+        def _():
+            emit(0, skip).wait()
+
+        @pl.when(it > 1)
+        def _():
+            emit(0, 0).wait()
+
         narrow[0:full] = wide[0:full].astype(bf16)
-        done = emit(small_at - shift, full)
-        done.start()
-        pending.append(done)
-        if i < 5:
-            wide[0:16] = wide[full : full + 16]
-    pending.pop().wait()
-
-
-def pack_flat(*args):
-    vm, whole = pltpu.VMEM, pl.BlockSpec(memory_space=pltpu.VMEM)
-    anywhere = pl.BlockSpec(memory_space=pl.ANY)
-    return pl.pallas_call(
-        pack_kernel,
-        out_shape=jax.ShapeDtypeStruct((GROWS, LANES), bf16),
-        in_specs=[anywhere] * 9 + [whole] * 7,
-        out_specs=anywhere,
-        scratch_shapes=[vm(a.shape, a.dtype) for a in args[:9]]
-        + [
-            vm((FF, 256), bf16),
-            vm((256, FF), bf16),
-            vm((7712, LANES), f32),
-            vm((7712, LANES), bf16),
-            vm((2, PADC, PADC), f32),
-            pltpu.SemaphoreType.DMA,
-            pltpu.SemaphoreType.DMA((9,)),
-        ],
-        compiler_params=pltpu.CompilerParams(vmem_limit_bytes=52 << 20),
-        name="pack_flat",
-    )(*args)
+
+        @pl.when(it == 0)
+        def _():
+            edge[2 * i] = wide[0:16]
+            emit(start - shift, skip).start()
+
+        @pl.when(it > 0)
+        def _():
+            emit(pl.multiple_of(start - shift + it * full, 16), 0).start()
+
+        wide[0:16] = wide[full : full + 16]
+        return carry
+
+    lax.fori_loop(0, turns, step, 0)
+    edge[2 * i + 1] = wide[0:16]
+    emit(0, skip if turns == 1 else 0).wait()
+
+
+def write_small(i, put, bufs):
+    _, _, wide, narrow, edge, flat, sem = bufs
+    _, _, _, at, count = flat_sections()[i]
+    shift = at % 16
+    wide[0:16] = edge[2 * i + 1]
+    put(i, shift)
+    end = shift + count
+    total = GROWS - at + shift if i == 5 else -(-end // 16) * 16
+    if i == 5:
+        wide[end:total] = jnp.zeros((total - end, LANES), f32)
+    elif total > end:
+        wide[end:total] = edge[2 * i + 2, 16 - (total - end) : 16]
+    narrow[0:total] = wide[0:total].astype(bf16)
+    done = pltpu.make_async_copy(
+        narrow.at[pl.ds(0, total)], flat.at[pl.ds(at - shift, total)], sem
+    )
+    done.start()
+    done.wait()
 
 
 CELLS = 2 * UNIT
@@ -1541,12 +1484,16 @@
 def backward_kernel(*refs):
     (gscale, mask, norms, tail, column, inverse, rows, w1, b1, w2,
      embed_h, in0, out0, in1, out1, head_h,
-     streams, waves_h, mixeds, befores, lasts, errors) = refs[:22]
-    (g_pred, g_out, g_pre, g_embed, sum_norm, sum_c1, sum_tail, sum_head, grad_w1, grad_w2, grad_b) = refs[22:33]
-    (embed, w_in, w_out, head, flow, carried, i_stream, i_waves, i_mixed, i_before, i_last, i_error,
-     s_pred, s_out, s_pre, s_embed, g_norm, weight_sem, in_sem, tail_in, out_sem, tail_sem) = refs[33:55]
-    units, mine, others, waves, back, own_sum, to_sib, from_sib, ready, landed, joined = refs[55:66]
-    sems = refs[66:]
+     streams, waves_h, mixeds, befores, lasts, errors, inputs, x1, normeds, hiddens, tails) = refs[:27]
+    flat = refs[27]
+    (sum_norm, sum_c1, sum_tail, sum_head, grad_w1, grad_w2, grad_b,
+     embed, w_in, w_out, head, flow, carried, i_stream, i_waves, i_mixed, i_before, i_last, i_error,
+     s_pred, s_out, s_pre, s_embed, g_norm, x_in, x_out, x_tail,
+     across, side, wide, narrow, edge, square,
+     weight_sem, in_sem, tail_in, section_sem, flat_sem) = refs[28:66]
+    units, mine, others, waves, back, own_sum, to_sib, from_sib, ready, landed, joined = refs[66:77]
+    sems = refs[77:]
+    bufs = (across, side, wide, narrow, edge, flat, flat_sem)
     row, me, core, sibling = place()
     barrier = greet_chips(me, core, sibling)
 
@@ -1578,6 +1525,7 @@
         pltpu.make_async_copy(lasts, i_last, tail_in.at[0]),
         pltpu.make_async_copy(errors, i_error, tail_in.at[1]),
     ]
+    late_load = pltpu.make_async_copy(tails, x_tail, tail_in.at[2])
     for load in tail_loads:
         load.start()
     loads[0].start()
@@ -1588,21 +1536,42 @@
     for target in (sum_norm, sum_c1, sum_tail, sum_head, grad_w1, grad_w2, grad_b, carried):
         target[...] = jnp.zeros_like(target)
 
-    def saves(it):
-        pairs = [(s_out, g_out), (s_pre, g_pre)]
+    late_load.start()
+
+    def section_loads(layer):
         return [
-            pltpu.make_async_copy(source, target.at[inst(it)], out_sem.at[k])
-            for k, (source, target) in enumerate(pairs)
+            pltpu.make_async_copy(source.at[2 * step + layer], target.at[step], section_sem.at[n, step])
+            for n, (source, target) in enumerate([(normeds, x_in), (hiddens, x_out)])
+            for step in range(2)
         ]
 
-    def pred_save(step):
-        return pltpu.make_async_copy(s_pred, g_pred.at[step], tail_sem.at[0])
-
-    def embed_save(step):
-        return pltpu.make_async_copy(s_embed, g_embed.at[step], tail_sem.at[1])
+    def write_when(it, number, work):
+        when_it(it == number, lambda: [write_section(i, xs, gs, bufs) for i, xs, gs in work] and None)
+
+    def pairs_out(layer):
+        return (2 + 2 * layer, (x_out.at[0], x_out.at[1]), (s_out.at[2], s_out.at[layer]))
+
+    def pairs_in(layer):
+        return (1 + 2 * layer, (x_in.at[0], x_in.at[1]), (s_pre.at[2], s_pre.at[layer]))
+
+    def meanwhile_in(it):
+        write_when(it, 2, [(5, (x_tail.at[0], x_tail.at[1]), (s_pred.at[0], s_pred.at[1])), pairs_out(1)])
+        write_when(it, 3, [pairs_out(0)])
+
+    def meanwhile_out(it):
+        write_when(it, 2, [pairs_in(1)])
+        write_when(it, 3, [pairs_in(0)])
 
     def body(it, carry):
         step, layer, slot = 1 - it // 2, 1 - it % 2, it % 2
+        keep = jnp.where(step == 1, layer, 2)
+
+        def fetch_section(wanted):
+            for load in section_loads(wanted):
+                load.start()
+
+        when_it(it == 2, lambda: fetch_section(1))
+        when_it(it == 3, lambda: fetch_section(0))
 
         def first():
             for load in tail_loads:
@@ -1610,13 +1579,11 @@
             loads[0].wait()
 
         when_it(it == 0, first)
-        when_it(it == 2, lambda: pred_save(1).wait())
 
         def head_adjoint():
             grad = i_error[step] * gscale[...] + carried[...]
             grad16 = grad.astype(bf16)
-            s_pred[...] = grad16
-            pred_save(step).start()
+            s_pred[step] = grad16
             sum_head[0:1] += jnp.sum(grad, axis=0, keepdims=True)
             back_n = dot_cols(grad16, head[...]).astype(bf16).astype(f32)
             value, gain, shift = norm_adjoint(i_last[step], tail[0:1], back_n)
@@ -1632,12 +1599,7 @@
 
         when_it(it < 3, prefetch)
 
-        def saved():
-            for save in saves(it):
-                save.wait()
-
-        when_it(it > 0, saved)
-        s_out[...] = flow[...].astype(bf16)
+        s_out[keep] = flow[...].astype(bf16)
         sum_norm[layer, 4:5] += jnp.sum(flow[...], axis=0, keepdims=True)
         for load in fetch(it):
             load.wait()
@@ -1656,17 +1618,22 @@
 
         def chunk(c, carry):
             part = pl.ds(pl.multiple_of(c * FCHUNK, FCHUNK), FCHUNK)
-            grad = dot_cols(s_out[...], w_out[layer, part, :]).astype(bf16).astype(f32)
+            grad = dot_cols(s_out[keep], w_out[layer, part, :]).astype(bf16).astype(f32)
             grad = grad * gelu_slope(i_before[slot, :, part].astype(f32))
             sum_c1[layer, 0:1, part] += jnp.sum(grad, axis=0, keepdims=True)
             grad16 = grad.astype(bf16)
-            s_pre[:, part] = grad16
+            s_pre[keep, :, part] = grad16
             g_norm[...] += dot_cols(grad16, w_in[layer, :, part])
             return carry
 
         lax.fori_loop(0, FF // FCHUNK, chunk, 0)
-        for save in saves(it):
-            save.start()
+
+        def section_ready():
+            for load in section_loads(0):
+                load.wait()
+
+        when_it(it >= 2, section_ready)
+        when_it(it == 2, late_load.wait)
         value, gain, shift = norm_adjoint(
             i_mixed[slot], norms[layer, 2:3], g_norm[...].astype(bf16).astype(f32)
         )
@@ -1676,7 +1643,7 @@
         split_units(flow[...], units)
         when_it(it == 0, lambda: pl.semaphore_wait(barrier, CHIPS))
         finish_one = spread_units(
-            me, core, sibling, units, mine, others, sems[:5], lambda: None
+            me, core, sibling, units, mine, others, sems[:5], lambda: meanwhile_in(it)
         )
         groups = to_spectrum(mine, others, column, rows, waves)
         for g in range(4):
@@ -1692,7 +1659,8 @@
             from_spectrum(g, dot_cols(grad_before16, w1[layer]).astype(bf16), rows, back)
         finish_two = gather_units(
             row, me, core, sibling, back, inverse,
-            (own_sum, to_sib, from_sib, ready, landed), sems[5:], finish_one, lambda: None,
+            (own_sum, to_sib, from_sib, ready, landed), sems[5:], finish_one,
+            lambda: meanwhile_out(it),
         )
         join_units(landed, joined)
         value, gain, shift = norm_adjoint(i_stream[slot], norms[layer, 0:1], joined[...])
@@ -1700,27 +1668,52 @@
         sum_norm[layer, 0:1] += gain
         sum_norm[layer, 1:2] += shift
         when_it(it == 1, loads[5].wait)
-        when_it(it == 3, lambda: embed_save(1).wait())
 
         def embed_adjoint():
-            s_embed[...] = flow[...].astype(bf16)
+            s_embed[step] = flow[...].astype(bf16)
             sum_tail[2:3] += jnp.sum(flow[...], axis=0, keepdims=True)
-            embed_save(step).start()
 
         when_it(layer == 0, embed_adjoint)
 
         def carry_back():
-            carried[...] = mask[...] * dot_cols(s_embed[...], embed[...]).astype(bf16).astype(f32)
+            carried[...] = mask[...] * dot_cols(s_embed[1], embed[...]).astype(bf16).astype(f32)
 
         when_it(it == 1, carry_back)
         finish_two()
         return carry
 
     lax.fori_loop(0, 4, body, 0)
-    for save in saves(3):
-        save.wait()
-    pred_save(0).wait()
-    embed_save(0).wait()
+    block = me % NBLK
+
+    def put_layer(at, idx):
+        put_rows(wide, at, sum_norm[idx, 0:1])
+        put_rows(wide, at + 6, sum_norm[idx, 1:2])
+        put_block_weight(wide, at + AT_W1, block, grad_w1[idx], square)
+        put_block_bias(wide, at + AT_B1, block, grad_b[idx, 0:1])
+        put_block_weight(wide, at + AT_W2, block, grad_w2[idx], square)
+        put_block_bias(wide, at + AT_B2, block, grad_b[idx, 1:2])
+        put_rows(wide, at + AT_NORM[2], sum_norm[idx, 2:3])
+        put_rows(wide, at + AT_NORM[3], sum_norm[idx, 3:4])
+
+    def put_small(i, at):
+        if i == 0:
+            put_rows(wide, at, sum_tail[2:3])
+            put_layer(at + 6, 0)
+        elif i == 2:
+            put_rows(wide, at, sum_norm[0, 4:5])
+            put_layer(at + 6, 1)
+        elif i == 4:
+            put_rows(wide, at, sum_norm[1, 4:5])
+            put_rows(wide, at + 6, sum_tail[0:1])
+            put_rows(wide, at + 12, sum_tail[1:2])
+        elif i == 5:
+            put_rows(wide, at, sum_head[0:1])
+        else:
+            put_rows(wide, at, sum_c1[i // 2, 0:1])
+
+    write_section(0, (inputs, x1), (s_embed.at[0], s_embed.at[1]), bufs)
+    for i in range(6):
+        write_small(i, put_small, bufs)
 
 
 def backward_pass(*args):
@@ -1729,22 +1722,17 @@
     shape = jax.ShapeDtypeStruct
     return pl.pallas_call(
         backward_kernel,
-        out_shape=[
-            shape((2, CELLS, PIN), bf16),
-            shape((4, CELLS, D), bf16),
-            shape((4, CELLS, FF), bf16),
-            shape((2, CELLS, D), bf16),
-            shape((2, 8, D), f32),
-            shape((2, 8, FF), f32),
-            shape((8, D), f32),
-            shape((8, PIN), f32),
-            shape((2, 256, 256), f32),
-            shape((2, 256, 256), f32),
-            shape((2, 8, 256), f32),
-        ],
-        in_specs=[whole] * 10 + [anywhere] * 12,
-        out_specs=[anywhere] * 4 + [whole] * 7,
+        out_shape=shape((GROWS, LANES), bf16),
+        in_specs=[whole] * 10 + [anywhere] * 12 + [whole] * 2 + [anywhere] * 3,
+        out_specs=anywhere,
         scratch_shapes=[
+            vm((2, 8, D), f32),
+            vm((2, 8, FF), f32),
+            vm((8, D), f32),
+            vm((8, PIN), f32),
+            vm((2, 256, 256), f32),
+            vm((2, 256, 256), f32),
+            vm((2, 8, 256), f32),
             vm((PIN, D), bf16),
             vm((2, D, FF), bf16),
             vm((2, FF, D), bf16),
@@ -1757,20 +1745,29 @@
             vm((2, CELLS, FF), bf16),
             vm((2, CELLS, D), f32),
             vm((2, CELLS, PIN), f32),
-            vm((CELLS, PIN), bf16),
-            vm((CELLS, D), bf16),
-            vm((CELLS, FF), bf16),
-            vm((CELLS, D), bf16),
+            vm((2, CELLS, PIN), bf16),
+            vm((3, CELLS, D), bf16),
+            vm((3, CELLS, FF), bf16),
+            vm((2, CELLS, D), bf16),
             vm((CELLS, D), f32),
+            vm((2, CELLS, D), bf16),
+            vm((2, CELLS, FF), bf16),
+            vm((2, CELLS, D), bf16),
+            vm((FF, 256), bf16),
+            vm((256, FF), bf16),
+            vm((7712, LANES), f32),
+            vm((7712, LANES), bf16),
+            vm((12, 16, LANES), f32),
+            vm((2, PADC, PADC), f32),
             dma((6,)),
             dma((4, 2)),
-            dma((2,)),
-            dma((2,)),
-            dma((2,)),
+            dma((3,)),
+            dma((2, 2)),
+            dma,
         ]
         + filter_scratch(),
         compiler_params=pltpu.CompilerParams(
-            collective_id=3, has_side_effects=True, vmem_limit_bytes=56 << 20
+            collective_id=3, has_side_effects=True, vmem_limit_bytes=60 << 20
         ),
         name="backward_pass",
     )(*args)
@@ -1806,15 +1803,9 @@
         inputs, goals, flat_mask, flat_weight, *tables, flat
     )
     mats, (x1, loss, norms, tail, w1, b1, w2) = rest[:6], rest[6:]
-    (g_pred, g_out, g_pre, g_embed, sum_norm, sum_c1, sum_tail, sum_head, grad_w1, grad_w2, grad_b) = (
-        backward_pass(
-            flat_weight * (2.0 / total_weight), flat_mask, norms, tail, *tables, w1, b1, w2, *mats,
-            streams, waves, mixeds, befores, lasts, errors,
-        )
-    )
-    flat_grad = pack_flat(
-        inputs, x1, normeds, hiddens, tails, g_embed, g_pre, g_out, g_pred,
-        sum_norm, sum_c1, sum_tail, sum_head, grad_w1, grad_w2, grad_b,
+    flat_grad = backward_pass(
+        flat_weight * (2.0 / total_weight), flat_mask, norms, tail, *tables, w1, b1, w2, *mats,
+        streams, waves, mixeds, befores, lasts, errors, inputs, x1, normeds, hiddens, tails,
     )
     loss_tile = jnp.concatenate([loss.reshape(1, LANES), jnp.zeros((7, LANES), f32)])
     summed, stats = rs(flat_grad, loss_tile)

time: 487 us -> 460 us (0.945)
  Pallas kernels: 455 us -> 434 us
  local copies, waits for them, and re-layouts: 9.29 us -> 4.31 us
    pallas_call x2 -> x1, Pallas kernels: 146 us -> 124 us  [backward_pass(): pl.pallas_call(backward_kernel, out_shape=shape((GROWS, LANES), bf16), in...]
    unnamed x30 -> x12, local copies, waits for them, and re-layouts: 4.99 us -> 0.03 us
where the time goes in v4:
time: 460 us; the launch traced here: 459 us
  Pallas kernels  434 us (94%)
  other arithmetic  15.2 us (3%)
    pallas_call x1, Pallas kernels, backward_pass(): pl.pallas_call(backward_kernel, out_shape=shape((GROWS, LANES), bf16), in...  124 us
    pallas_call x1, Pallas kernels, forward_pass(): pl.pallas_call(forward_kernel, out_shape=[shape((4, CELLS, D), f32), shap...  107 us
    pallas_call x1, Pallas kernels, rs(): pl.pallas_call(sum_kernel, out_shape=[shape((CHR, 128), f32), shape((16,...  107 us
    pallas_call x1, Pallas kernels, ag(): pl.pallas_call(gather_kernel, out_shape=jax.ShapeDtypeStruct((32 * CH, 12...  96.1 us
  transfers between devices with their start and end apart: 1, of which 0 were waited for; matrix products, arithmetic and copies ran while one was open for 2% of the time, Pallas kernels for 0%

profile of v4, /device:TPU:0, one launch (start us, length us, event | category | flops | bytes accessed | tf_op | source)
XLA Modules:
  0.0 458.9 jit_solution(10107939180460075770)
XLA Ops:
  0.6 0.0 copy-start
  0.6 0.0 copy-start.4
  0.7 1.6 convert_element_type.58
  2.2 1.3 collective-permute-start
  3.6 0.0 copy-done.4
  3.6 0.2 slice_reduce_fusion.4
  3.9 0.1 compare_and_fusion.1
  3.9 0.1 fusion.5
  4.0 0.1 and_convert_fusion
  4.1 0.1 reshape.390
  4.2 0.7 reshape.391.refs_2_.refs_1_
  4.9 0.0 copy-done
  4.9 0.0 copy-start.3
  4.9 0.1 convert_bitcast_fusion
  5.0 0.1 compare_and_fusion
  5.1 0.1 fusion.7
  5.2 0.1 and_select_fusion
  5.3 0.1 mul.121.refs_3_
  5.4 0.0 copy-start.2
  5.4 0.0 copy-start.5
  5.4 1.2 fusion.11
  6.6 0.7 select_reduce_fusion
  8.0 0.0 copy-done.3
  8.0 0.8 fusion.3.refs_0_.refs_22_
  8.8 0.9 pad_maximum_fusion.refs_1_
  9.7 0.0 copy-done.2
  9.7 0.6 broadcast_multiply_fusion.refs_0_
  10.4 0.0 copy-done.5
  10.4 1.4 dynamic-slice_bitcast_fusion
  11.7 0.0 collective-permute-done
  11.7 2.7 fusion.2.shard
  14.4 96.1 %gather_weights.1.refs_7_ = bf16[94208,128]{1,0:T(8,128)(2,1)} custom-call(bf16[2944,128]{1,0:T(8,128)(2,1)} %fusion.2.shard), custom_call_target="tpu_custom_call" | custom-call | tf_op jit(solution)/shard_map/gather_weights/pallas_call | solution.py:737
  110.5 106.8 %forward_pass.1 = (f32[4,128,768]{2,1,0:T(8,128)}, bf16[4,4,256,256]{3,2,1,0:T(8,128)(2,1)}, f32[4,128,768]{2,1,0:T(8,128)}, bf16[4,128,768]{2,1,0:T(8,128)(2,1)...) custom-call(bf16[128,1280]{1,0:T(8,128)(2,1)} %fusion.3.refs_0_.refs, ...), custom_call_target="tpu_custom_call" | custom-call | tf_op jit(solution)/shard_map/forward_pass/pallas_call | solution.py:1424
  217.3 0.9 reduce.4
  218.2 0.6 concatenate.7.loss
  218.9 124.0 %backward_pass.1.grad = bf16[93904,128]{1,0:T(8,128)(2,1)} custom-call(f32[128,1]{1,0:T(8,128)} %broadcast_multiply_fusion.refs_0_, f32[128,1]{1,0:T(8,128)} %reshape.391.refs_2_.refs_1_, f32[2,4,768]{2,1,0:T(4,128)} %get-tuple-element.31.refs_2_, f32[2,768]{1,0:T(2,128)} %get-tuple-element.32.refs_3_, bf16[128,128]{1,0:T(8,128)(2,1)} %get-tuple-element.68.refs_4_, ...), custom_call_target="tpu_custom_call" | custom-call | tf_op jit(solution)/shard_map/backward_pass/pallas_call | solution.py:1723
  342.9 0.0 copy-start.1
  342.9 106.6 %sum_gradients.1 = (f32[2960,128]{1,0:T(8,128)}, f32[16,128]{1,0:T(8,128)}) custom-call(bf16[93904,128]{1,0:T(8,128)(2,1)} %backward_pass.1.grad, f32[8,128]{1,0:T(8,128)} %concatenate.7.loss), custom_call_target="tpu_custom_call" | custom-call | tf_op jit(solution)/shard_map/sum_gradients/pallas_call | solution.py:975
  449.5 1.3 slice_reduce_fusion
  451.6 0.0 copy-done.1
  451.6 5.0 %fusion.8 = (bf16[375552]{0:T(1024)(128)(2,1)}, f32[375552]{0:T(1024)}, f32[375552]{0:T(1024)}, f32[375552]{0:T(1024)}) fusion(f32[375552]{0:T(1024)S(1)} %copy-done, f32[]{:T(128)S(6)} %div.36, f32[2960,128]{1,0:T(8,128)} %get-tuple-element.53, s32[]{:T(128)S(6)} %select_n.50, f32[375552]{0:T(1024)S(1)} %copy-done.1, f32[375552]{0:T(1024)} %param.14), kind=kLoop, calls=%fused_computation.42 | loop fusion | flops 6384384 | bytes 11266568 | tf_op jit(solution)/shard_map/convert_element_type | solution.py:1832
  (6 shorter events, 0.1 us)
Async XLA Ops:
  0.6 4.3 copy-start
  0.6 3.0 copy-start.4
  2.2 9.5 %collective-permute-start = (bf16[320,128]{1,0:T(8,128)(2,1)S(1)}, bf16[320,128]{1,0:T(8,128)(2,1)S(1)}, u32[]{:S(2)}, u32[]{:S(2)}) collective-permute-start(bf16[320,128]{1,0:T(8,128)(2,1)S(1)} %slice_bitcast_fusion), channel_id=1, source_target_pairs={{1,0},{2,1},{3,2},{4,3},{5,4},{6,5},{7,6},{8,7},{9,8},{10,9},{11,1... | collective-permute-start | bytes 245768 | tf_op jit(solution)/shard_map/ppermute | solution.py:1781
  4.9 3.1 copy-start.3
  5.4 4.3 copy-start.2
  5.4 5.0 %copy-start.5 = (bf16[2,128,128]{2,1,0:T(8,128)(2,1)S(1)}, bf16[2,128,128]{2,1,0:T(8,128)(2,1)}, u32[]{:S(2)}) copy-start(bf16[2,128,128]{2,1,0:T(8,128)(2,1)} %constant.121.clone) | copy-start | bytes 196612
  342.9 108.7 %copy-start.1 = (f32[375552]{0:T(1024)S(1)}, f32[375552]{0:T(1024)}, u32[]{:S(2)}) copy-start(f32[375552]{0:T(1024)} %param.13) | copy-start | bytes 4506628

commit v5 on v4

--- a/solution.py
+++ b/solution.py
@@ -332,7 +332,7 @@
         pl.semaphore_signal(
             barrier,
             inc=1,
-            device_id=chip_device(lax.rem(me + k, CHIPS), core),
+            device_id=chip_device(me ^ (CHIPS - k), core),
             device_id_type=MESH,
         )
         return carry
@@ -390,20 +390,20 @@
     send_a, recv_a, send_f, recv_f, local_sem = sems
 
     def out(k):
-        chip = lax.rem(me + k, CHIPS)
+        chip = me ^ k
         return remote(
             units.at[chip], mine.at[me], send_a.at[k], recv_a.at[k], chip_device(chip, core)
         )
 
     def handed(k):
-        chip = lax.rem(me + CHIPS - k, CHIPS)
+        chip = me ^ k
         return remote(mine.at[chip], others.at[chip], send_f.at[k], recv_f.at[k], sibling)
 
     own = pltpu.make_async_copy(units.at[me], mine.at[me], local_sem)
     own.start()
 
     def begin(k, carry):
-        out(k).start()
+        out(CHIPS - k).start()
         return carry
 
     lax.fori_loop(1, CHIPS, begin, 0)
@@ -412,8 +412,8 @@
     handed(0).start()
 
     def hand(k, carry):
-        out(k).wait_recv()
-        handed(k).start()
+        out(CHIPS - k).wait_recv()
+        handed(CHIPS - k).start()
         return carry
 
     lax.fori_loop(1, CHIPS, hand, 0)
@@ -486,7 +486,7 @@
         )
 
     def partial(j, carry):
-        pair = lax.rem(row + 1 + j, 8)
+        pair = row ^ (7 - j)
         for half in range(2):
             sums = dot(inverse_table[...], back[2 * pair + half])
             part = pl.ds(32 * half, 32)
@@ -507,13 +507,13 @@
     own = pltpu.make_async_copy(ready.at[me], landed.at[me], local_sem)
 
     def total(j, carry):
-        pair = lax.rem(row + 1 + j, 8)
+        pair = row ^ (7 - j)
         swap(pair).wait_recv()
         rows = pl.ds(2 * pair, 2)
         ready[rows] = (own_sum[rows] + from_sib[rows].astype(f32)).astype(bf16)
         for x in range(2):
             chip = 2 * pair + x
-            k = lax.rem(chip - me + CHIPS, CHIPS)
+            k = chip ^ me
 
             @pl.when(k != 0)
             def _():
@@ -526,7 +526,7 @@
     meanwhile()
 
     def landed_all(k, carry):
-        home(lax.rem(me + k, CHIPS), k).wait_recv()
+        home(me ^ k, k).wait_recv()
         return carry
 
     lax.fori_loop(1, CHIPS, landed_all, 0)
@@ -534,7 +534,7 @@
 
     def finish():
         def sent(k, carry):
-            home(lax.rem(me + k, CHIPS), k).wait_send()
+            home(me ^ k, k).wait_send()
             return carry
 
         lax.fori_loop(1, CHIPS, sent, 0)
@@ -1142,7 +1142,7 @@
 
 
 CELLS = 2 * UNIT
-FCHUNK = 768
+FCHUNK = 1024
 FILTER_SEMS = 10
 
 
@@ -1381,7 +1381,7 @@
         flow[...] = mixed + c2[layer]
 
         def chunk(c, carry):
-            part = pl.ds(pl.multiple_of(c * FCHUNK, FCHUNK), FCHUNK)
+            part = pl.ds(c * FCHUNK, FCHUNK)
             before = dot(s_norm[...], w_in[layer, :, part]) + c1[layer, :, part]
             s_before[:, part] = before.astype(bf16)
             hidden = gelu_of(before).astype(bf16)
@@ -1389,7 +1389,8 @@
             flow[...] += dot(hidden, w_out[layer, part, :])
             return carry
 
-        lax.fori_loop(0, FF // FCHUNK, chunk, 0)
+        for c in range(FF // FCHUNK):
+            chunk(c, 0)
         for save in saves(it):
             save.start()
         finish_two()
@@ -1617,7 +1618,7 @@
         g_norm[...] = jnp.zeros_like(g_norm)
 
         def chunk(c, carry):
-            part = pl.ds(pl.multiple_of(c * FCHUNK, FCHUNK), FCHUNK)
+            part = pl.ds(c * FCHUNK, FCHUNK)
             grad = dot_cols(s_out[keep], w_out[layer, part, :]).astype(bf16).astype(f32)
             grad = grad * gelu_slope(i_before[slot, :, part].astype(f32))
             sum_c1[layer, 0:1, part] += jnp.sum(grad, axis=0, keepdims=True)
@@ -1626,7 +1627,8 @@
             g_norm[...] += dot_cols(grad16, w_in[layer, :, part])
             return carry
 
-        lax.fori_loop(0, FF // FCHUNK, chunk, 0)
+        for c in range(FF // FCHUNK):
+            chunk(c, 0)
 
         def section_ready():
             for load in section_loads(0):

time: 460 us -> 454 us (0.987)
  Pallas kernels: 434 us -> 423 us
where the time goes in v5:
time: 454 us; the launch traced here: 449 us
  Pallas kernels  423 us (93%)
  other arithmetic  15.2 us (3%)
  between operations  4.98 us (1%)
    pallas_call x1, Pallas kernels, backward_pass(): pl.pallas_call(backward_kernel, out_shape=shape((GROWS, LANES), bf16), in...  119 us
    pallas_call x1, Pallas kernels, rs(): pl.pallas_call(sum_kernel, out_shape=[shape((CHR, 128), f32), shape((16,...  104 us
    pallas_call x1, Pallas kernels, forward_pass(): pl.pallas_call(forward_kernel, out_shape=[shape((4, CELLS, D), f32), shap...  104 us
    pallas_call x1, Pallas kernels, ag(): pl.pallas_call(gather_kernel, out_shape=jax.ShapeDtypeStruct((32 * CH, 12...  96.1 us
  transfers between devices with their start and end apart: 1, of which 0 were waited for; matrix products, arithmetic and copies ran while one was open for 2% of the time, Pallas kernels for 0%

profile of v5, /device:TPU:0, one launch (start us, length us, event | category | flops | bytes accessed | tf_op | source)
XLA Modules:
  0.0 449.1 jit_solution(6264115887674029443)
XLA Ops:
  0.6 0.0 copy-start
  0.6 0.0 copy-start.4
  0.7 1.6 convert_element_type.58
  2.2 1.3 collective-permute-start
  3.6 0.0 copy-done.4
  3.6 0.2 slice_reduce_fusion.4
  3.9 0.1 compare_and_fusion.1
  3.9 0.1 fusion.5
  4.0 0.1 and_convert_fusion
  4.1 0.1 reshape.390
  4.2 0.7 reshape.391.refs_2_.refs_1_
  4.9 0.0 copy-done
  4.9 0.0 copy-start.3
  4.9 0.1 convert_bitcast_fusion
  5.0 0.1 compare_and_fusion
  5.1 0.1 fusion.7
  5.2 0.1 and_select_fusion
  5.3 0.1 mul.121.refs_3_
  5.4 0.0 copy-start.2
  5.4 0.0 copy-start.5
  5.4 1.2 fusion.11
  6.6 0.7 select_reduce_fusion
  8.0 0.0 copy-done.3
  8.0 0.8 fusion.3.refs_0_.refs_22_
  8.8 0.9 pad_maximum_fusion.refs_1_
  9.7 0.0 copy-done.2
  9.7 0.6 broadcast_multiply_fusion.refs_0_
  10.4 0.0 copy-done.5
  10.4 1.4 dynamic-slice_bitcast_fusion
  11.7 0.0 collective-permute-done
  11.7 2.7 fusion.2.shard
  14.4 96.1 %gather_weights.1.refs_7_ = bf16[94208,128]{1,0:T(8,128)(2,1)} custom-call(bf16[2944,128]{1,0:T(8,128)(2,1)} %fusion.2.shard), custom_call_target="tpu_custom_call" | custom-call | tf_op jit(solution)/shard_map/gather_weights/pallas_call | solution.py:737
  110.5 103.6 %forward_pass.1 = (f32[4,128,768]{2,1,0:T(8,128)}, bf16[4,4,256,256]{3,2,1,0:T(8,128)(2,1)}, f32[4,128,768]{2,1,0:T(8,128)}, bf16[4,128,768]{2,1,0:T(8,128)(2,1)...) custom-call(bf16[128,1280]{1,0:T(8,128)(2,1)} %fusion.3.refs_0_.refs, ...), custom_call_target="tpu_custom_call" | custom-call | tf_op jit(solution)/shard_map/forward_pass/pallas_call | solution.py:1425
  214.1 0.9 reduce.4
  215.1 0.6 concatenate.7.loss
  215.7 119.5 %backward_pass.1.grad = bf16[93904,128]{1,0:T(8,128)(2,1)} custom-call(f32[128,1]{1,0:T(8,128)} %broadcast_multiply_fusion.refs_0_, f32[128,1]{1,0:T(8,128)} %reshape.391.refs_2_.refs_1_, f32[2,4,768]{2,1,0:T(4,128)} %get-tuple-element.31.refs_2_, f32[2,768]{1,0:T(2,128)} %get-tuple-element.32.refs_3_, bf16[128,128]{1,0:T(8,128)(2,1)} %get-tuple-element.68.refs_4_, ...), custom_call_target="tpu_custom_call" | custom-call | tf_op jit(solution)/shard_map/backward_pass/pallas_call | solution.py:1725
  335.2 0.0 copy-start.1
  335.2 104.1 %sum_gradients.1 = (f32[2960,128]{1,0:T(8,128)}, f32[16,128]{1,0:T(8,128)}) custom-call(bf16[93904,128]{1,0:T(8,128)(2,1)} %backward_pass.1.grad, f32[8,128]{1,0:T(8,128)} %concatenate.7.loss), custom_call_target="tpu_custom_call" | custom-call | tf_op jit(solution)/shard_map/sum_gradients/pallas_call | solution.py:975
  439.3 1.3 slice_reduce_fusion
  441.3 0.0 copy-done.1
  441.3 5.0 %fusion.8 = (bf16[375552]{0:T(1024)(128)(2,1)}, f32[375552]{0:T(1024)}, f32[375552]{0:T(1024)}, f32[375552]{0:T(1024)}) fusion(f32[375552]{0:T(1024)S(1)} %copy-done, f32[]{:T(128)S(6)} %div.36, f32[2960,128]{1,0:T(8,128)} %get-tuple-element.53, s32[]{:T(128)S(6)} %select_n.50, f32[375552]{0:T(1024)S(1)} %copy-done.1, f32[375552]{0:T(1024)} %param.14), kind=kLoop, calls=%fused_computation.42 | loop fusion | flops 6384384 | bytes 11266568 | tf_op jit(solution)/shard_map/convert_element_type | solution.py:1834
  (6 shorter events, 0.1 us)
Async XLA Ops:
  0.6 4.3 copy-start
  0.6 3.0 copy-start.4
  2.2 9.5 %collective-permute-start = (bf16[320,128]{1,0:T(8,128)(2,1)S(1)}, bf16[320,128]{1,0:T(8,128)(2,1)S(1)}, u32[]{:S(2)}, u32[]{:S(2)}) collective-permute-start(bf16[320,128]{1,0:T(8,128)(2,1)S(1)} %slice_bitcast_fusion), channel_id=1, source_target_pairs={{1,0},{2,1},{3,2},{4,3},{5,4},{6,5},{7,6},{8,7},{9,8},{10,9},{11,1... | collective-permute-start | bytes 245768 | tf_op jit(solution)/shard_map/ppermute | solution.py:1783
  4.9 3.1 copy-start.3
  5.4 4.3 copy-start.2
  5.4 5.0 %copy-start.5 = (bf16[2,128,128]{2,1,0:T(8,128)(2,1)S(1)}, bf16[2,128,128]{2,1,0:T(8,128)(2,1)}, u32[]{:S(2)}) copy-start(bf16[2,128,128]{2,1,0:T(8,128)(2,1)} %constant.121.clone) | copy-start | bytes 196612
  335.2 106.1 %copy-start.1 = (f32[375552]{0:T(1024)S(1)}, f32[375552]{0:T(1024)}, u32[]{:S(2)}) copy-start(f32[375552]{0:T(1024)} %param.13) | copy-start | bytes 4506628

commit v6 on v5

--- a/solution.py
+++ b/solution.py
@@ -823,7 +823,7 @@
             ways[way],
         )
 
-    order = (1, 2, 3, 0)
+    order = (1, 3, 2, 0)
 
     def begin_own(turn, carry):
         for what in order:
@@ -857,7 +857,7 @@
         return xin[turn, pl.ds(SUM_CUTS[2 + way] - SUM_CUTS[2], sizes[2 + way])].astype(f32)
 
     send_across(0)
-    for what in (2, 3):
+    for what in (3, 2):
         for way in range(2):
             held(own, 0, way, what)[...] = both(0, way, what).astype(bf16)
             ring(0, way, what, True).start()
@@ -868,7 +868,7 @@
 
     def step(turn, carry):
         send_across(turn + 1)
-        for what in (2, 3, 0):
+        for what in (3, 2, 0):
             for way in range(2):
                 part = both(turn, way, what)
                 if what == 0:

time: 454 us -> 453 us (level)
  no operation moved by 1% of the time
where the time goes in v6:
time: 453 us; the launch traced here: 448 us
  Pallas kernels  422 us (93%)
  other arithmetic  15.2 us (3%)
  between operations  4.98 us (1%)
    pallas_call x1, Pallas kernels, backward_pass(): pl.pallas_call(backward_kernel, out_shape=shape((GROWS, LANES), bf16), in...  119 us
    pallas_call x1, Pallas kernels, forward_pass(): pl.pallas_call(forward_kernel, out_shape=[shape((4, CELLS, D), f32), shap...  104 us
    pallas_call x1, Pallas kernels, rs(): pl.pallas_call(sum_kernel, out_shape=[shape((CHR, 128), f32), shape((16,...  103 us
    pallas_call x1, Pallas kernels, ag(): pl.pallas_call(gather_kernel, out_shape=jax.ShapeDtypeStruct((32 * CH, 12...  96.1 us
  transfers between devices with their start and end apart: 1, of which 0 were waited for; matrix products, arithmetic and copies ran while one was open for 2% of the time, Pallas kernels for 0%

profile of v6, /device:TPU:0, one launch (start us, length us, event | category | flops | bytes accessed | tf_op | source)
XLA Modules:
  0.0 448.1 jit_solution(12349480833219128087)
XLA Ops:
  0.6 0.0 copy-start
  0.6 0.0 copy-start.4
  0.7 1.6 convert_element_type.58
  2.2 1.3 collective-permute-start
  3.6 0.0 copy-done.4
  3.6 0.2 slice_reduce_fusion.4
  3.9 0.1 compare_and_fusion.1
  3.9 0.1 fusion.5
  4.0 0.1 and_convert_fusion
  4.1 0.1 reshape.390
  4.2 0.7 reshape.391.refs_2_.refs_1_
  4.9 0.0 copy-done
  4.9 0.0 copy-start.3
  4.9 0.1 convert_bitcast_fusion
  5.0 0.1 compare_and_fusion
  5.1 0.1 fusion.7
  5.2 0.1 and_select_fusion
  5.3 0.1 mul.121.refs_3_
  5.4 0.0 copy-start.2
  5.4 0.0 copy-start.5
  5.4 1.2 fusion.11
  6.6 0.7 select_reduce_fusion
  8.0 0.0 copy-done.3
  8.0 0.8 fusion.3.refs_0_.refs_22_
  8.8 0.9 pad_maximum_fusion.refs_1_
  9.7 0.0 copy-done.2
  9.7 0.6 broadcast_multiply_fusion.refs_0_
  10.4 0.0 copy-done.5
  10.4 1.4 dynamic-slice_bitcast_fusion
  11.7 0.0 collective-permute-done
  11.7 2.7 fusion.2.shard
  14.4 96.1 %gather_weights.1.refs_7_ = bf16[94208,128]{1,0:T(8,128)(2,1)} custom-call(bf16[2944,128]{1,0:T(8,128)(2,1)} %fusion.2.shard), custom_call_target="tpu_custom_call" | custom-call | tf_op jit(solution)/shard_map/gather_weights/pallas_call | solution.py:737
  110.5 103.6 %forward_pass.1 = (f32[4,128,768]{2,1,0:T(8,128)}, bf16[4,4,256,256]{3,2,1,0:T(8,128)(2,1)}, f32[4,128,768]{2,1,0:T(8,128)}, bf16[4,128,768]{2,1,0:T(8,128)(2,1)...) custom-call(bf16[128,1280]{1,0:T(8,128)(2,1)} %fusion.3.refs_0_.refs, ...), custom_call_target="tpu_custom_call" | custom-call | tf_op jit(solution)/shard_map/forward_pass/pallas_call | solution.py:1425
  214.1 0.9 reduce.4
  215.1 0.6 concatenate.7.loss
  215.7 119.5 %backward_pass.1.grad = bf16[93904,128]{1,0:T(8,128)(2,1)} custom-call(f32[128,1]{1,0:T(8,128)} %broadcast_multiply_fusion.refs_0_, f32[128,1]{1,0:T(8,128)} %reshape.391.refs_2_.refs_1_, f32[2,4,768]{2,1,0:T(4,128)} %get-tuple-element.31.refs_2_, f32[2,768]{1,0:T(2,128)} %get-tuple-element.32.refs_3_, bf16[128,128]{1,0:T(8,128)(2,1)} %get-tuple-element.68.refs_4_, ...), custom_call_target="tpu_custom_call" | custom-call | tf_op jit(solution)/shard_map/backward_pass/pallas_call | solution.py:1725
  335.2 0.0 copy-start.1
  335.2 103.1 %sum_gradients.1 = (f32[2960,128]{1,0:T(8,128)}, f32[16,128]{1,0:T(8,128)}) custom-call(bf16[93904,128]{1,0:T(8,128)(2,1)} %backward_pass.1.grad, f32[8,128]{1,0:T(8,128)} %concatenate.7.loss), custom_call_target="tpu_custom_call" | custom-call | tf_op jit(solution)/shard_map/sum_gradients/pallas_call | solution.py:975
  438.3 1.3 slice_reduce_fusion
  440.3 0.0 copy-done.1
  440.3 5.0 %fusion.8 = (bf16[375552]{0:T(1024)(128)(2,1)}, f32[375552]{0:T(1024)}, f32[375552]{0:T(1024)}, f32[375552]{0:T(1024)}) fusion(f32[375552]{0:T(1024)S(1)} %copy-done, f32[]{:T(128)S(6)} %div.36, f32[2960,128]{1,0:T(8,128)} %get-tuple-element.53, s32[]{:T(128)S(6)} %select_n.50, f32[375552]{0:T(1024)S(1)} %copy-done.1, f32[375552]{0:T(1024)} %param.14), kind=kLoop, calls=%fused_computation.42 | loop fusion | flops 6384384 | bytes 11266568 | tf_op jit(solution)/shard_map/convert_element_type | solution.py:1834
  (6 shorter events, 0.1 us)
Async XLA Ops:
  0.6 4.3 copy-start
  0.6 3.0 copy-start.4
  2.2 9.5 %collective-permute-start = (bf16[320,128]{1,0:T(8,128)(2,1)S(1)}, bf16[320,128]{1,0:T(8,128)(2,1)S(1)}, u32[]{:S(2)}, u32[]{:S(2)}) collective-permute-start(bf16[320,128]{1,0:T(8,128)(2,1)S(1)} %slice_bitcast_fusion), channel_id=1, source_target_pairs={{1,0},{2,1},{3,2},{4,3},{5,4},{6,5},{7,6},{8,7},{9,8},{10,9},{11,1... | collective-permute-start | bytes 245768 | tf_op jit(solution)/shard_map/ppermute | solution.py:1783
  4.9 3.1 copy-start.3
  5.4 4.3 copy-start.2
  5.4 5.0 %copy-start.5 = (bf16[2,128,128]{2,1,0:T(8,128)(2,1)S(1)}, bf16[2,128,128]{2,1,0:T(8,128)(2,1)}, u32[]{:S(2)}) copy-start(bf16[2,128,128]{2,1,0:T(8,128)(2,1)} %constant.121.clone) | copy-start | bytes 196612
  335.2 105.1 %copy-start.1 = (f32[375552]{0:T(1024)S(1)}, f32[375552]{0:T(1024)}, u32[]{:S(2)}) copy-start(f32[375552]{0:T(1024)} %param.13) | copy-start | bytes 4506628
